TPU v7x, 32 devices: a whole 2x2x4 slice. The times are simulated.
32 devices in a mesh: axial: 8 (over y, x, core), radial: 4 (over z).
Axes of the slice: x: 2, y: 2, z: 4, core: 2. Of those that a mesh axis runs over, the one named last changes fastest.
Arguments:
- species: float32 [5, 64, 32, 128], P(None, 'axial', 'radial')
- velocity: float32 [3, 64, 32, 128], P(None, 'axial', 'radial'), may hold values from -4 to 4
- diffusivity: float32 [64, 32, 128], P('axial', 'radial'), may hold values from 0.3 to 1
- parcels: float32 [8, 4, 16, 2048], P('axial', 'radial')
- counts: int32 [8, 4], P('axial', 'radial'), may hold values from 256 to 2048, as said below
- cells: int32 [8, 4, 2048], P('axial', 'radial'), may hold values from 0 to 8191, as said below
- leave_slots: int32 [8, 4, 4, 64], P('axial', 'radial'), may hold values from 0 to 2047, as said below
- leave_counts: int32 [8, 4, 4], P('axial', 'radial'), may hold values from 16 to 64, as said below
Outputs:
- species_out: float32 [5, 64, 32, 128], P(None, 'axial', 'radial')
- velocity_out: float32 [3, 64, 32, 128], P(None, 'axial', 'radial')
- staying: float32 [8, 4, 16, 2048], P('axial', 'radial')
- arrivals: float32 [8, 4, 4, 16, 64], P('axial', 'radial')
Inputs may be any that keep to these rules, and one draw needn't show every extreme that they name: `counts`: block 0 along the first dimension, 2 along the second is full; blocks near the injector hold several times the mean. `cells`: Non-decreasing along the slots of a block; slots that are not live hold 8191. `leave_slots`: entries below a face's count are live slots of that block, all distinct over the four faces; entries at or beyond the count are 0. `leave_counts`: some block sends 64 parcels through each of its faces.
All inputs are finite; a program needn't handle non-finite values.
Results may differ from a plain program's by a relative error of at most 0.0003.
Values sent between devices are 32-bit elements; how exact they have to be, the bound alone decides.
No kernel may reach another device: no remote copies, remote signals or barrier semaphores. Data moves between devices by JAX's collectives and lax.ppermute only.
A program may use at most 64 MiB of HBM per device.

v0:
```python
import jax
import jax.numpy as jnp
from jax import lax
from jax.sharding import PartitionSpec as P

time_step = 0.1


def extended_2(x, sides, width):
    for axis, dim in sides:
        size, length = (lax.axis_size(axis), x.shape[dim])
        up = [(i, (i + 1) % size) for i in range(size - 1)]
        down = [(j, i) for i, j in up]
        last = lax.slice_in_dim(x, length - width, length, axis=dim)
        first = lax.slice_in_dim(x, 0, width, axis=dim)
        before = lax.ppermute(last, axis, up)
        after = lax.ppermute(first, axis, down)
        x = jnp.concatenate([before, x, after], axis=dim)
    return x


def coefficient(vel_first, vel_second, vel_third, base_rate):
    kinetic = vel_first * vel_first + vel_second * vel_second + vel_third * vel_third
    return base_rate * (1.0 + 0.5 * jnp.tanh(0.5 * kinetic))


def operate(values, diffusion):
    widths = [(0, 0)] * (values.ndim - 1) + [(1, 1)]
    padded = jnp.pad(values, widths)
    diffusion_padded = jnp.pad(diffusion, ((0, 0), (0, 0), (1, 1)))
    weight_first = 0.5 * (diffusion[1:] + diffusion[:-1])
    flux_first = weight_first * (values[..., 1:, :, :] - values[..., :-1, :, :])
    change_first = flux_first[..., 1:, :, :] - flux_first[..., :-1, :, :]
    weight_second = 0.5 * (diffusion[:, 1:] + diffusion[:, :-1])
    flux_second = weight_second * (values[..., :, 1:, :] - values[..., :, :-1, :])
    change_second = flux_second[..., :, 1:, :] - flux_second[..., :, :-1, :]
    weight_third = 0.5 * (diffusion_padded[:, :, 1:] + diffusion_padded[:, :, :-1])
    flux_third = weight_third * (padded[..., 1:] - padded[..., :-1])
    change_third = flux_third[..., 1:] - flux_third[..., :-1]
    return (
        change_first[..., :, 1:-1, :]
        + change_second[..., 1:-1, :, :]
        + change_third[..., 1:-1, 1:-1, :]
    )


def advance_parcels(parcel_block, live_count, cell_index, slot_table, face_counts, gas_flat):
    slots_total = parcel_block.shape[-1]
    movers = slot_table.shape[-1]
    gas_here = jnp.take(gas_flat, cell_index, axis=1)
    old_velocity = parcel_block[0:3]
    old_mass = parcel_block[3]
    response = parcel_block[4]
    evaporation = parcel_block[5]
    drag_force = response * (gas_here - old_velocity)
    new_velocity = old_velocity + time_step * drag_force
    new_mass = old_mass * (1.0 - time_step * evaporation)
    new_position = parcel_block[6:9] + time_step * new_velocity
    pushed = jnp.concatenate(
        [new_velocity, new_mass[None], parcel_block[4:6], new_position, parcel_block[9:]], axis=0
    )
    slot_ids = jnp.arange(slots_total, dtype=jnp.int32)
    live_weight = (slot_ids < live_count).astype(jnp.float32)
    deposits = (
        jnp.stack(
            [
                old_mass * evaporation,
                -old_mass * drag_force[0],
                -old_mass * drag_force[1],
                -old_mass * drag_force[2],
            ],
            axis=0,
        )
        * live_weight[None, :]
    )
    source = jnp.zeros((4, gas_flat.shape[1]), jnp.float32).at[:, cell_index].add(deposits)
    face_valid = (jnp.arange(movers, dtype=jnp.int32)[None, :] < face_counts[:, None]).astype(
        jnp.float32
    )
    leaving = (
        jnp.zeros((slots_total,), jnp.float32)
        .at[slot_table.reshape(-1)]
        .max(face_valid.reshape(-1))
    )
    staying = pushed * (live_weight * (1.0 - leaving))[None, :]
    outgoing = (
        jnp.transpose(jnp.take(pushed, slot_table, axis=1), (1, 0, 2)) * face_valid[:, None, :]
    )
    return (staying, outgoing, source)


def body(species, velocity, diffusivity, parcels, counts, cells, leave_slots, leave_counts):
    width_x = species.shape[1]
    width_y = species.shape[2]
    width_z = species.shape[3]
    gas_flat = velocity.reshape(3, width_x * width_y * width_z)
    staying, outgoing, source = advance_parcels(
        parcels[0, 0], counts[0, 0], cells[0, 0], leave_slots[0, 0], leave_counts[0, 0], gas_flat
    )
    source_grid = source.reshape(4, width_x, width_y, width_z)
    fields = jnp.concatenate([species, velocity, diffusivity[None]], axis=0)
    extended = extended_2(fields, (("axial", 1), ("radial", 2)), 2)
    base_cycle = extended[8, 1:-1, 1:-1]
    flow = extended[:8]
    start = coefficient(flow[5], flow[6], flow[7], extended[8])
    first = flow[:, 1:-1, 1:-1] + time_step * operate(flow, start)
    row_global = lax.axis_index("axial") * width_x - 1 + jnp.arange(width_x + 2, dtype=jnp.int32)
    column_global = (
        lax.axis_index("radial") * width_y - 1 + jnp.arange(width_y + 2, dtype=jnp.int32)
    )
    row_inside = (row_global >= 0) & (row_global < width_x * lax.axis_size("axial"))
    column_inside = (column_global >= 0) & (column_global < width_y * lax.axis_size("radial"))
    inside = row_inside[:, None] & column_inside[None, :]
    first = jnp.where(inside[None, :, :, None], first, 0.0)
    later = coefficient(first[5], first[6], first[7], base_cycle)
    second = 0.5 * (fields[:8] + first[:, 1:-1, 1:-1] + time_step * operate(first, later))
    zero_grid = jnp.zeros_like(source_grid[0])
    added = jnp.stack(
        [
            source_grid[0],
            zero_grid,
            zero_grid,
            zero_grid,
            zero_grid,
            source_grid[1],
            source_grid[2],
            source_grid[3],
        ],
        axis=0,
    )
    result = second + time_step * added
    axial_pair = jnp.stack([outgoing[1], outgoing[0]], axis=0)
    radial_pair = jnp.stack([outgoing[3], outgoing[2]], axis=0)
    axial_got = extended_2(axial_pair, (("axial", 0),), 1)
    radial_got = extended_2(radial_pair, (("radial", 0),), 1)
    arrivals = jnp.stack([axial_got[0], axial_got[3], radial_got[0], radial_got[3]], axis=0)
    return (result[:5], result[5:], staying[None, None], arrivals[None, None])


def solution(mesh):
    return jax.shard_map(
        body,
        mesh=mesh,
        in_specs=(
            P(None, "axial", "radial", None),
            P(None, "axial", "radial", None),
            P("axial", "radial", None),
            P("axial", "radial", None, None),
            P("axial", "radial"),
            P("axial", "radial", None),
            P("axial", "radial", None, None),
            P("axial", "radial", None),
        ),
        out_specs=(
            P(None, "axial", "radial", None),
            P(None, "axial", "radial", None),
            P("axial", "radial", None, None),
            P("axial", "radial", None, None, None),
        ),
        check_vma=False,
    )
```

profile of v0, /device:TPU:12, one launch (start us, length us, event | category | flops | bytes accessed | tf_op | source)
XLA Modules:
  0.0 102.6 jit_solution(10981169428210601931)
XLA Ops:
  0.6 1.5 %pad_maximum_fusion.8 = (f32[9,2,8,128]{3,2,1,0:T(8,128)}, f32[9,2,8,128]{3,2,1,0:T(8,128)}) fusion(f32[1,8,8,128]{3,2,1,0:T(8,128)} %bitcast.92, f32[3,8,8,128]{3,2,1,0:T(8,128)} %param.9, f32[5,8,8,128]{3,2,1,0:T(8,128)} %param.8), kind=kLoop, calls=%fused_computation.90 | loop fusion | flops 73728 | bytes 442368 | tf_op jit(solution)/shard_map/slice | solution.py:14
  2.2 1.9 %collective-permute-start = (f32[9,2,8,128]{3,2,1,0:T(8,128)}, f32[9,2,8,128]{3,2,1,0:T(8,128)S(1)}, u32[]{:S(2)}, u32[]{:S(2)}) collective-permute-start(f32[9,2,8,128]{3,2,1,0:T(8,128)} %get-tuple-element.35), channel_id=1, source_target_pairs={{0,4},{4,8},{8,12},{12,16},{16,20},{20,24},{24,28},{1,5},{5,9},{9,... | collective-permute-start | bytes 221192 | tf_op jit(solution)/shard_map/ppermute | solution.py:16
  4.1 0.0 copy-start.2
  4.1 0.0 copy-start.4
  4.1 4.7 %collective-permute-start.1 = (f32[9,2,8,128]{3,2,1,0:T(8,128)}, f32[9,2,8,128]{3,2,1,0:T(8,128)S(1)}, u32[]{:S(2)}, u32[]{:S(2)}) collective-permute-start(f32[9,2,8,128]{3,2,1,0:T(8,128)} %get-tuple-element.36), channel_id=1, source_target_pairs={{4,0},{8,4},{12,8},{16,12},{20,16},{24,20},{28,24},{5,1},{9,5},{13... | collective-permute-start | bytes 221192 | tf_op jit(solution)/shard_map/ppermute | solution.py:17
  8.8 3.4 %copy.76 = f32[3,8,8,128]{0,3,2,1:T(8,128)} copy(f32[3,8,8,128]{3,2,1,0:T(8,128)} %param.9) | data formatting | bytes 196608 | tf_op args[1]
  12.3 0.0 copy-start.5
  12.3 0.6 copy-done.5
  12.9 7.6 %gather_fusion = f32[2048,3]{1,0:T(8,128)S(1)} fusion(f32[3,8192]{0,1:T(8,128)} %bitcast.87, s32[2048]{0:T(1024)S(1)} %broadcast_clamp_fusion), kind=kCustom, calls=%fused_computation | custom fusion | bytes 57344 | tf_op jit(solution)/shard_map/jit(_take)/gather | solution.py:50
  20.5 0.3 copy.77
  20.9 0.7 bitcast_add_fusion
  21.5 0.7 fusion.52
  22.2 0.4 copy.85
  22.6 0.4 copy.84
  22.9 1.1 %copy.86 = f32[3,2048]{0,1:T(8,128)S(1)} copy(f32[3,2048]{1,0:T(4,128)} %get-tuple-element.16) | data formatting | bytes 49152 | tf_op jit(solution)/shard_map/add | solution.py:58
  24.1 1.4 %copy.89 = f32[1,1,7,2048]{2,3,1,0:T(8,128)} copy(f32[1,1,7,2048]{3,2,1,0:T(8,128)S(1)} %slice.345) | data formatting | bytes 114688
  25.4 1.3 %copy.88 = f32[1,1,2,2048]{2,3,1,0:T(8,128)} copy(f32[1,1,2,2048]{3,2,1,0:T(2,128)S(1)} %slice.343) | data formatting | bytes 32768
  26.8 1.3 %compare_select_fusion.3 = s32[4,64,1]{1,0,2:T(4,128)} fusion(s32[1,1,4,64]{3,2,1,0:T(4,128)} %param.14), kind=kLoop, calls=%fused_computation.128 | loop fusion | flops 768 | bytes 2048 | tf_op jit(solution)/shard_map/jit(_take)/jit(_where)/select_n | solution.py:87
  28.1 1.3 %reshape.414 = s32[256]{0:T(256)} reshape(s32[4,64,1]{1,0,2:T(4,128)} %compare_select_fusion.3) | data formatting | bytes 2048 | tf_op jit(solution)/shard_map/jit(_take)/jit(_where)/select_n | solution.py:87
  29.4 1.2 %pad_clamp_fusion = s32[1024]{0:T(1024)} fusion(s32[256]{0:T(256)} %reshape.414), kind=kLoop, calls=%fused_computation.130 | loop fusion | flops 1024 | bytes 5120 | tf_op jit(solution)/shard_map/jit(_take)/gather | solution.py:87
  30.6 4.3 %concatenate.29 = f32[16,2048]{0,1:T(8,128)} concatenate(f32[3,2048]{0,1:T(8,128)S(1)} %copy.84, f32[1,2048]{0,1:T(8,128)S(1)} %copy.85, f32[2,2048]{0,1:T(8,128)} %bitcast.89, f32[3,2048]{0,1:T(8,128)S(1)} %copy.86, f32[7,2048]{0,1:T(8,128)} %bitcast.88), dimensions={0} | concatenate | bytes 262144 | tf_op jit(solution)/shard_map/concatenate | solution.py:59
  34.8 2.1 %gather_fusion.1 = f32[256,16]{1,0:T(8,128)S(1)} fusion(f32[16,2048]{0,1:T(8,128)} %concatenate.29, s32[1024]{0:T(1024)} %pad_clamp_fusion), kind=kCustom, calls=%fused_computation.1 | custom fusion | bytes 33792 | tf_op jit(solution)/shard_map/jit(_take)/gather | solution.py:87
  36.9 0.1 copy.87
  37.0 0.8 fusion.56
  37.8 1.9 %collective-permute-start.4 = (f32[1,16,64]{2,1,0:T(8,128)S(1)}, f32[1,16,64]{2,1,0:T(8,128)S(1)}, u32[]{:S(2)}, u32[]{:S(2)}) collective-permute-start(f32[1,16,64]{2,1,0:T(8,128)S(1)} %get-tuple-element.47), channel_id=1, source_target_pairs={{0,4},{4,8},{8,12},{12,16},{16,20},{20,24},{24,28},{1,5},{5,9},{9,... | collective-permute-start | bytes 12296 | tf_op jit(solution)/shard_map/ppermute | solution.py:16
  39.7 4.5 %collective-permute-start.5 = (f32[1,16,64]{2,1,0:T(8,128)S(1)}, f32[1,16,64]{2,1,0:T(8,128)S(1)}, u32[]{:S(2)}, u32[]{:S(2)}) collective-permute-start(f32[1,16,64]{2,1,0:T(8,128)S(1)} %get-tuple-element.50), channel_id=1, source_target_pairs={{4,0},{8,4},{12,8},{16,12},{20,16},{24,20},{28,24},{5,1},{9,5},{13... | collective-permute-start | bytes 12296 | tf_op jit(solution)/shard_map/ppermute | solution.py:17
  44.3 3.5 %collective-permute-start.6 = (f32[1,16,64]{2,1,0:T(8,128)S(1)}, f32[1,16,64]{2,1,0:T(8,128)S(1)}, u32[]{:S(2)}, u32[]{:S(2)}) collective-permute-start(f32[1,16,64]{2,1,0:T(8,128)S(1)} %get-tuple-element.49), channel_id=1, source_target_pairs={{0,1},{1,2},{2,3},{4,5},{5,6},{6,7},{8,9},{9,10},{10,11},{12,13},{... | collective-permute-start | bytes 12296 | tf_op jit(solution)/shard_map/ppermute | solution.py:16
  47.8 0.7 multiply_add_fusion
  48.5 0.1 reshape.432
  48.6 0.8 reshape_squeeze.3
  50.0 0.8 fusion.45
  50.8 0.4 copy.78
  51.2 16.6 %scatter_custom_fusion = f32[4,8192]{0,1:T(8,128)} fusion(s32[2048]{0:T(1024)} %bitcast.100, f32[2048,4]{1,0:T(8,128)S(1)} %copy.78, f32[]{:T(128)} %constant.29.clone.1), kind=kCustom, calls=%fused_computation.8 | custom fusion | flops 8192 | bytes 131584 | tf_op jit(solution)/shard_map/scatter-add | solution.py:76
  67.8 13.9 %slice_reduce_fusion = (f32[8192]{0:T(1024)S(1)}, f32[8192]{0:T(1024)S(1)}, f32[8192]{0:T(1024)S(1)}, f32[8192]{0:T(1024)S(1)}) fusion(f32[4,8192]{0,1:T(8,128)} %scatter_custom_fusion), kind=kLoop, calls=%fused_computation.4 | loop fusion | bytes 262144 | tf_op jit(solution)/shard_map/slice | solution.py:127
  81.8 2.3 %scatter_custom_fusion.1 = f32[2048]{0:T(1024)S(1)} fusion(s32[256]{0:T(256)S(1)} %bitcast.101, f32[256]{0:T(256)S(1)} %reshape.432, f32[]{:T(128)} %constant.29.clone.1), kind=kCustom, calls=%fused_computation.132 | custom fusion | flops 256 | bytes 8196 | tf_op jit(solution)/shard_map/scatter-max | solution.py:83
  84.1 0.2 concatenate.28
  84.3 0.7 broadcast_multiply_fusion
  85.0 0.1 broadcast_and_fusion
  85.1 2.1 %collective-permute-start.7 = (f32[1,16,64]{2,1,0:T(8,128)S(1)}, f32[1,16,64]{2,1,0:T(8,128)S(1)}, u32[]{:S(2)}, u32[]{:S(2)}) collective-permute-start(f32[1,16,64]{2,1,0:T(8,128)S(1)} %get-tuple-element.48), channel_id=1, source_target_pairs={{1,0},{2,1},{3,2},{5,4},{6,5},{7,6},{9,8},{10,9},{11,10},{13,12},{... | collective-permute-start | bytes 12296 | tf_op jit(solution)/shard_map/ppermute | solution.py:17
  87.2 0.0 collective-permute-done.1
  87.3 0.1 pad_maximum_fusion.5
  87.3 3.7 %collective-permute-start.2 = (f32[9,12,2,128]{3,2,1,0:T(2,128)S(1)}, f32[9,12,2,128]{3,2,1,0:T(2,128)S(1)}, u32[]{:S(2)}, u32[]{:S(2)}) collective-permute-start(f32[9,12,2,128]{3,2,1,0:T(2,128)S(1)} %get-tuple-element.33), channel_id=1, source_target_pairs={{0,1},{1,2},{2,3},{4,5},{5,6},{6,7},{8,9},{9,10},{10,11},{12,13},{... | collective-permute-start | bytes 331784 | tf_op jit(solution)/shard_map/ppermute | solution.py:16
  91.0 2.3 %collective-permute-start.3 = (f32[9,12,2,128]{3,2,1,0:T(2,128)S(1)}, f32[9,12,2,128]{3,2,1,0:T(2,128)S(1)}, u32[]{:S(2)}, u32[]{:S(2)}) collective-permute-start(f32[9,12,2,128]{3,2,1,0:T(2,128)S(1)} %get-tuple-element.34), channel_id=1, source_target_pairs={{1,0},{2,1},{3,2},{5,4},{6,5},{7,6},{9,8},{10,9},{11,10},{13,12},{... | collective-permute-start | bytes 331784 | tf_op jit(solution)/shard_map/ppermute | solution.py:17
  93.4 0.6 maximum_bitcast_fusion
  94.0 3.6 %collective-permute-done.3 = f32[9,12,2,128]{3,2,1,0:T(2,128)S(1)} collective-permute-done((f32[9,12,2,128]{3,2,1,0:T(2,128)S(1)}, f32[9,12,2,128]{3,2,1,0:T(2,128)S(1)}, u32[]{:S(2)}, u32[]{:S(2)}) %collective-permute-start.3) | collective-permute-done | bytes 110624 | tf_op jit(solution)/shard_map/ppermute | solution.py:17
  97.7 0.2 pad_maximum_fusion
  97.9 0.1 slice.382
  98.0 0.1 fusion.22
  98.2 0.5 fusion.3
  98.6 0.3 fusion.59
  98.9 0.1 fusion.6
  99.1 0.1 fusion.61
  99.2 0.1 fusion.7
  99.3 0.1 fusion.62
  99.4 0.4 fusion.12
  99.9 0.1 fusion.24
  100.0 0.1 fusion.14
  100.1 0.1 fusion.64
  100.2 0.1 fusion.8
  100.3 0.4 fusion.5
  100.8 0.2 fusion.60
  101.0 0.3 fusion.19
  101.2 0.7 slice.419
  101.9 0.6 slice.420
  (41 shorter events, 0.4 us)
Async XLA Ops:
  2.2 82.9 %collective-permute-start = (f32[9,2,8,128]{3,2,1,0:T(8,128)}, f32[9,2,8,128]{3,2,1,0:T(8,128)S(1)}, u32[]{:S(2)}, u32[]{:S(2)}) collective-permute-start(f32[9,2,8,128]{3,2,1,0:T(8,128)} %get-tuple-element.35), channel_id=1, source_target_pairs={{0,4},{4,8},{8,12},{12,16},{16,20},{20,24},{24,28},{1,5},{5,9},{9,... | collective-permute-start | bytes 221192 | tf_op jit(solution)/shard_map/ppermute | solution.py:16
  4.1 8.1 %copy-start.2 = (f32[1,1,16,2048]{3,2,1,0:T(8,128)S(1)}, f32[1,1,16,2048]{3,2,1,0:T(8,128)}, u32[]{:S(2)}) copy-start(f32[1,1,16,2048]{3,2,1,0:T(8,128)} %param.11) | copy-start | bytes 393220
  4.1 8.2 %copy-start.4 = (s32[1,1,2048]{2,1,0:T(1,128)S(1)}, s32[1,1,2048]{2,1,0:T(1,128)}, u32[]{:S(2)}) copy-start(s32[1,1,2048]{2,1,0:T(1,128)} %param.13) | copy-start | bytes 24580
  4.1 83.1 %collective-permute-start.1 = (f32[9,2,8,128]{3,2,1,0:T(8,128)}, f32[9,2,8,128]{3,2,1,0:T(8,128)S(1)}, u32[]{:S(2)}, u32[]{:S(2)}) collective-permute-start(f32[9,2,8,128]{3,2,1,0:T(8,128)} %get-tuple-element.36), channel_id=1, source_target_pairs={{4,0},{8,4},{12,8},{16,12},{20,16},{24,20},{28,24},{5,1},{9,5},{13... | collective-permute-start | bytes 221192 | tf_op jit(solution)/shard_map/ppermute | solution.py:17
  12.3 0.6 copy-start.5
  20.9 0.7 copy-start.6
  37.8 53.2 %collective-permute-start.4 = (f32[1,16,64]{2,1,0:T(8,128)S(1)}, f32[1,16,64]{2,1,0:T(8,128)S(1)}, u32[]{:S(2)}, u32[]{:S(2)}) collective-permute-start(f32[1,16,64]{2,1,0:T(8,128)S(1)} %get-tuple-element.47), channel_id=1, source_target_pairs={{0,4},{4,8},{8,12},{12,16},{16,20},{20,24},{24,28},{1,5},{5,9},{9,... | collective-permute-start | bytes 12296 | tf_op jit(solution)/shard_map/ppermute | solution.py:16
  39.7 53.7 %collective-permute-start.5 = (f32[1,16,64]{2,1,0:T(8,128)S(1)}, f32[1,16,64]{2,1,0:T(8,128)S(1)}, u32[]{:S(2)}, u32[]{:S(2)}) collective-permute-start(f32[1,16,64]{2,1,0:T(8,128)S(1)} %get-tuple-element.50), channel_id=1, source_target_pairs={{4,0},{8,4},{12,8},{16,12},{20,16},{24,20},{28,24},{5,1},{9,5},{13... | collective-permute-start | bytes 12296 | tf_op jit(solution)/shard_map/ppermute | solution.py:17
  44.3 49.1 %collective-permute-start.6 = (f32[1,16,64]{2,1,0:T(8,128)S(1)}, f32[1,16,64]{2,1,0:T(8,128)S(1)}, u32[]{:S(2)}, u32[]{:S(2)}) collective-permute-start(f32[1,16,64]{2,1,0:T(8,128)S(1)} %get-tuple-element.49), channel_id=1, source_target_pairs={{0,1},{1,2},{2,3},{4,5},{5,6},{6,7},{8,9},{9,10},{10,11},{12,13},{... | collective-permute-start | bytes 12296 | tf_op jit(solution)/shard_map/ppermute | solution.py:16
  67.7 19.5 %copy-start = (f32[5,8,8,128]{3,2,1,0:T(8,128)S(1)}, f32[5,8,8,128]{3,2,1,0:T(8,128)}, u32[]{:S(2)}) copy-start(f32[5,8,8,128]{3,2,1,0:T(8,128)} %param.8) | copy-start | bytes 491524
  67.8 19.5 %copy-start.1 = (f32[3,8,8,128]{3,2,1,0:T(8,128)S(1)}, f32[3,8,8,128]{3,2,1,0:T(8,128)}, u32[]{:S(2)}) copy-start(f32[3,8,8,128]{3,2,1,0:T(8,128)} %param.9) | copy-start | bytes 294916
  67.8 19.5 %copy-start.3 = (f32[8,8,128]{2,1,0:T(8,128)S(1)}, f32[8,8,128]{2,1,0:T(8,128)}, u32[]{:S(2)}) copy-start(f32[8,8,128]{2,1,0:T(8,128)} %param.10) | copy-start | bytes 98308
  85.1 8.3 %collective-permute-start.7 = (f32[1,16,64]{2,1,0:T(8,128)S(1)}, f32[1,16,64]{2,1,0:T(8,128)S(1)}, u32[]{:S(2)}, u32[]{:S(2)}) collective-permute-start(f32[1,16,64]{2,1,0:T(8,128)S(1)} %get-tuple-element.48), channel_id=1, source_target_pairs={{1,0},{2,1},{3,2},{5,4},{6,5},{7,6},{9,8},{10,9},{11,10},{13,12},{... | collective-permute-start | bytes 12296 | tf_op jit(solution)/shard_map/ppermute | solution.py:17
  87.3 6.7 %collective-permute-start.2 = (f32[9,12,2,128]{3,2,1,0:T(2,128)S(1)}, f32[9,12,2,128]{3,2,1,0:T(2,128)S(1)}, u32[]{:S(2)}, u32[]{:S(2)}) collective-permute-start(f32[9,12,2,128]{3,2,1,0:T(2,128)S(1)} %get-tuple-element.33), channel_id=1, source_target_pairs={{0,1},{1,2},{2,3},{4,5},{5,6},{6,7},{8,9},{9,10},{10,11},{12,13},{... | collective-permute-start | bytes 331784 | tf_op jit(solution)/shard_map/ppermute | solution.py:16
  91.0 6.6 %collective-permute-start.3 = (f32[9,12,2,128]{3,2,1,0:T(2,128)S(1)}, f32[9,12,2,128]{3,2,1,0:T(2,128)S(1)}, u32[]{:S(2)}, u32[]{:S(2)}) collective-permute-start(f32[9,12,2,128]{3,2,1,0:T(2,128)S(1)} %get-tuple-element.34), channel_id=1, source_target_pairs={{1,0},{2,1},{3,2},{5,4},{6,5},{7,6},{9,8},{10,9},{11,10},{13,12},{... | collective-permute-start | bytes 331784 | tf_op jit(solution)/shard_map/ppermute | solution.py:17
where the time goes:
time: 103 us
  local copies, waits for them, and re-layouts  41.9 us (41%)
  other arithmetic  30.5 us (30%)
  starting transfers between devices  24.7 us (24%)
  waiting for transfers between devices  3.66 us (4%)
  between operations  1.83 us (2%)
    scatter-add x1, other arithmetic, advance_parcels(): jnp.zeros((4, gas_flat.shape[1]), jnp.float32).at[:, cell_index]  16.6 us
    slice x1, local copies, waits for them, and re-layouts, body(): source_grid[3]  13.9 us
    ppermute x4, starting transfers between devices, extended_2(): after = lax.ppermute(first, axis, down)  13.7 us
    ppermute x4, starting transfers between devices, extended_2(): before = lax.ppermute(last, axis, up)  11 us
    gather x2, local copies, waits for them, and re-layouts, advance_parcels(): gas_here = jnp.take(gas_flat, cell_index, axis=1)  7.97 us
    unnamed x21, local copies, waits for them, and re-layouts  6.76 us
    concatenate x2, local copies, waits for them, and re-layouts, advance_parcels(): jnp.concatenate([new_velocity, new_mass[None], parcel_block[4:6], new_pos...  4.46 us
    ppermute x4, waiting for transfers between devices, extended_2(): after = lax.ppermute(first, axis, down)  3.65 us
  transfers between devices with their start and end apart: 8, of which 1 were waited for; matrix products, arithmetic and copies ran while one was open for 64% of the time, Pallas kernels for 0%

commit v1 on v0

v1 whole, which is shorter than its diff:
```python
import functools

import jax
import jax.numpy as jnp
import numpy as np
from jax import lax
from jax.experimental import pallas as pl
from jax.experimental.pallas import tpu as pltpu
from jax.sharding import PartitionSpec as P

time_step = 0.1
AXES = ("axial", "radial")
LARGEST = float(jnp.finfo(jnp.bfloat16).max)
F32, BF16, I32 = jnp.float32, jnp.bfloat16, jnp.int32
SPECIES, VECTORS = 5, 3
FLOW = SPECIES + VECTORS
FIELDS = FLOW + 1
ROWS = 16
LANES = 128
VMEM_LIMIT = 16 * 1024 * 1024


def pairing(sizes, axis, odd):
    size, other = sizes[axis], sizes[1 - axis]

    def partner(here):
        at = list(here)
        step = 1 if (here[axis] % 2 == 1) == odd else -1
        if 0 <= at[axis] + step < size:
            at[axis] += step
        elif (at[1 - axis] ^ 1) < other:
            at[1 - axis] ^= 1
        return tuple(at)

    flat = lambda at: at[0] * sizes[1] + at[1]
    blocks = [(i, j) for i in range(sizes[0]) for j in range(sizes[1])]
    pairs = [(flat(at), flat(partner(at))) for at in blocks]
    assert sorted(t for _, t in pairs) == list(range(len(blocks)))
    return pairs


def split(x):
    high = jnp.clip(x, -LARGEST, LARGEST).astype(BF16)
    return high, (x - high.astype(F32)).astype(BF16)


def one_hot(index, depth):
    rows = lax.broadcasted_iota(I32, (depth, index.shape[1]), 0)
    return (rows == index).astype(F32).astype(BF16)


def pick(table, index):
    rows = lax.broadcasted_iota(I32, table.shape, 0)
    return jnp.sum(jnp.where(rows == index, table, 0.0), axis=0, keepdims=True)


def dot(a, b):
    return jnp.dot(a, b, preferred_element_type=F32)


def dot_t(a, b):
    return lax.dot_general(a, b, (((1,), (1,)), ((), ())), preferred_element_type=F32)


def pack_kernel(
    width_x, width_y, species, velocity, diffusivity, parcels, cells, slots, face_counts,
    axial_even, axial_odd, radial_even, radial_odd, leaving,
):
    cells_of = width_x * width_y
    even_x = lax.rem(lax.axis_index("axial"), 2) == 0
    even_y = lax.rem(lax.axis_index("radial"), 2) == 0
    tile = width_y
    for f in range(FIELDS):
        ref, base = (
            (species, f) if f < SPECIES else (velocity, f - SPECIES) if f < FLOW else (diffusivity, 0)
        )
        for layer in range(2):
            at = pl.ds((2 * f + layer) * tile, tile)
            low = ref[pl.ds(base * cells_of + layer * width_y, width_y), :]
            high = ref[pl.ds(base * cells_of + (width_x - 2 + layer) * width_y, width_y), :]
            axial_even[at, :] = jnp.where(even_x, high, low)
            axial_odd[at, :] = jnp.where(even_x, low, high)
            low = ref[pl.ds(base * cells_of + layer, width_x, stride=width_y), :]
            high = ref[pl.ds(base * cells_of + width_y - 2 + layer, width_x, stride=width_y), :]
            radial_even[at, :] = jnp.where(even_y, high, low)
            radial_odd[at, :] = jnp.where(even_y, low, high)

    movers = slots.shape[1]
    lane = lax.broadcasted_iota(I32, (1, 2 * movers), 1)
    pairs = [jnp.concatenate([slots[i : i + 1, :], slots[i + 1 : i + 2, :]], axis=1) for i in (0, 2)]
    valid = [
        lane < jnp.where(lane < movers, face_counts[0, 0, i], movers + face_counts[0, 0, i + 1]) for i in (0, 2)
    ]
    slot = jnp.concatenate(pairs, axis=1)
    valid = jnp.concatenate([v.astype(F32) for v in valid], axis=1)
    chunk, place = lax.shift_right_logical(slot, 7), lax.bitwise_and(slot, LANES - 1)
    chunks = parcels.shape[1] // LANES
    hot_place = one_hot(place, LANES)
    hot_chunk = lax.broadcasted_iota(I32, (chunks, slot.shape[1]), 0) == chunk
    count = dot_t(jnp.where(hot_chunk, valid, 0.0).astype(BF16), hot_place)
    leaving[...] = count
    stacked = jnp.concatenate([parcels[:, h * LANES : (h + 1) * LANES] for h in range(chunks)], axis=0)
    cell = cells[...]
    cell_high = lax.shift_right_logical(cell, 7).astype(F32)
    cell_low = lax.bitwise_and(cell, LANES - 1).astype(F32)
    first, second = split(stacked)
    left = jnp.concatenate([first, cell_high.astype(BF16), cell_low.astype(BF16)], axis=0)
    right = jnp.concatenate([second, jnp.zeros((2 * chunks, LANES), BF16)], axis=0)
    table = dot(jnp.concatenate([left, right], axis=1), jnp.concatenate([hot_place, hot_place], axis=0))
    rows = jnp.zeros((ROWS, slot.shape[1]), F32)
    for h in range(chunks):
        rows = rows + jnp.where(chunk == h, table[h * ROWS : (h + 1) * ROWS], 0.0)
    row_of = jnp.sum(
        jnp.where(hot_chunk, table[chunks * ROWS : chunks * ROWS + chunks], 0.0), axis=0, keepdims=True
    ).astype(I32)
    lane_of = jnp.sum(
        jnp.where(hot_chunk, table[chunks * ROWS + chunks :], 0.0), axis=0, keepdims=True
    ).astype(I32)
    gas = gas_at(velocity[...], row_of, one_hot(lane_of, LANES), cells_of)
    response, evaporation = rows[4:5], rows[5:6]
    pushed = [rows[i : i + 1] + time_step * (response * (gas[i] - rows[i : i + 1])) for i in range(3)]
    pushed.append(rows[3:4] * (1.0 - time_step * evaporation))
    pushed.extend([response, evaporation])
    pushed.extend(rows[6 + i : 7 + i] + time_step * pushed[i] for i in range(3))
    base = 2 * FIELDS * tile
    for packets, lo in (((axial_even, axial_odd), 0), ((radial_even, radial_odd), 2 * movers)):
        skip = 0 if lo == 0 else 3 * tile
        for ref in packets:
            part = slice(lo, lo + 2 * movers)
            for i, row in enumerate(pushed):
                ref[base + skip + i : base + skip + i + 1, :] = row[:, part] * valid[:, part]
            ref[base + skip + 9 : base + skip + ROWS, :] = rows[9:ROWS, part] * valid[:, part]
    for ref in (radial_even, radial_odd):
        ref[base : base + 3 * tile, :] = jnp.zeros((3 * tile, LANES), F32)


def gas_at(velocity, row_of, hot_lane, rows):
    high, low = split(velocity)
    table = dot(
        jnp.concatenate([high, low], axis=1), jnp.concatenate([hot_lane, hot_lane], axis=0)
    )
    return [pick(table[i * rows : (i + 1) * rows], row_of) for i in range(VECTORS)]


def parcel_kernel(width_x, width_y, velocity, parcels, cells, counts, leaving, staying, source):
    rows = width_x * width_y
    slots = parcels.shape[1]
    cell = cells[0]
    row_of, lane_of = lax.shift_right_logical(cell, 7), lax.bitwise_and(cell, LANES - 1)
    hot_lane = one_hot(lane_of, LANES)
    gas = gas_at(velocity[...], row_of, hot_lane, rows)
    live = counts[0, 0]
    slot = lax.broadcasted_iota(I32, (1, slots), 1)
    live_weight = (slot < live).astype(F32)
    chunks = slots // LANES
    stay = jnp.where(leaving[...] > 0.5, 0.0, 1.0)
    keep = jnp.concatenate([stay[h : h + 1] for h in range(chunks)], axis=1) * live_weight
    mass, response, evaporation = parcels[3:4], parcels[4:5], parcels[5:6]
    drag = [response * (gas[i] - parcels[i : i + 1]) for i in range(3)]
    deposits = [mass * evaporation] + [-mass * d for d in drag]
    for i in range(3):
        moved = parcels[i : i + 1] + time_step * drag[i]
        staying[i : i + 1, :] = moved * keep
        staying[6 + i : 7 + i, :] = (parcels[6 + i : 7 + i] + time_step * moved) * keep
    staying[3:4, :] = mass * (1.0 - time_step * evaporation) * keep
    staying[4:6, :] = parcels[4:6] * keep
    staying[9:ROWS, :] = parcels[9:ROWS] * keep
    hot_row = one_hot(row_of, rows)
    halves = [split(d * live_weight) for d in deposits]
    left = jnp.concatenate([hot_row * half[i] for i in range(2) for half in halves], axis=0)
    total = dot_t(left, hot_lane)
    source[...] = total[: 4 * rows] + total[4 * rows :]


def corner_kernel(
    width_x, width_y, from_even, from_odd, even_in, odd_in, radial_even, radial_odd
):
    tile = width_y
    base = 2 * FIELDS * tile
    even_x = lax.rem(lax.axis_index("axial"), 2) == 0
    even_y = lax.rem(lax.axis_index("radial"), 2) == 0
    at_x, size_x = lax.axis_index("axial"), lax.axis_size("axial")
    has = [at_x > 0, at_x < size_x - 1]
    radial_even[...] = even_in[...]
    radial_odd[...] = odd_in[...]
    for side in range(2):
        layer = 1 - side
        for y, part in ((0, "low"), (width_y - 1, "high")):
            flow = [
                ref[pl.ds(layer * tile + y, FLOW, stride=2 * tile), :] for ref in (from_even, from_odd)
            ]
            base_rate = [
                ref[pl.ds((2 * FLOW + layer) * tile + y, 1), :] for ref in (from_even, from_odd)
            ]
            lower_is_odd = even_x if side == 0 else jnp.logical_not(even_x)
            choose = lambda v: jnp.where(has[side], jnp.where(lower_is_odd, v[1], v[0]), 0.0)
            flow, base_rate = choose(flow), choose(base_rate)
            for ref, is_high in ((radial_even, even_y), (radial_odd, jnp.logical_not(even_y))):
                @pl.when(is_high if part == "high" else jnp.logical_not(is_high))
                def _(ref=ref, flow=flow, base_rate=base_rate, side=side):
                    ref[base + side * tile : base + side * tile + FLOW, :] = flow
                    ref[base + 2 * tile + side : base + 2 * tile + side + 1, :] = base_rate


def coefficient(vel_first, vel_second, vel_third, base_rate):
    kinetic = vel_first * vel_first + vel_second * vel_second + vel_third * vel_third
    return base_rate * (1.0 + 0.5 * jnp.tanh(0.5 * kinetic))


def shifted_z(x):
    lane = lax.broadcasted_iota(I32, x.shape, x.ndim - 1)
    below = jnp.where(lane == 0, 0.0, pltpu.roll(x, 1, x.ndim - 1))
    above = jnp.where(lane == x.shape[-1] - 1, 0.0, pltpu.roll(x, x.shape[-1] - 1, x.ndim - 1))
    return below, above


def shifted_row(x, before, after):
    axis = x.ndim - 2
    row = lax.broadcasted_iota(I32, x.shape, axis)
    below = jnp.where(row == 0, before, pltpu.roll(x, 1, axis))
    above = jnp.where(row == x.shape[axis] - 1, after, pltpu.roll(x, x.shape[axis] - 1, axis))
    return below, above


def change(x, d, others_x, others_d):
    half = 0.5 * time_step
    total = None
    for (low, high), (d_low, d_high) in zip(others_x, others_d):
        part = (d_high + d) * (high - x) - (d + d_low) * (x - low)
        total = part if total is None else total + part
    return half * total


def stencil_kernel(
    width_x, width_y, species, velocity, diffusivity, from_even, from_odd, beside_even, beside_odd, source,
    species_out, velocity_out, arrivals,
):
    tile = width_y
    rows = width_x * width_y
    depth = LANES
    at_x, size_x = lax.axis_index("axial"), lax.axis_size("axial")
    at_y, size_y = lax.axis_index("radial"), lax.axis_size("radial")
    even_x, even_y = lax.rem(at_x, 2) == 0, lax.rem(at_y, 2) == 0
    has_low_x, has_high_x = at_x > 0, at_x < size_x - 1
    has_low_y, has_high_y = at_y > 0, at_y < size_y - 1

    def axial_halo(lo, n):
        a, b = from_even[lo : lo + n, :], from_odd[lo : lo + n, :]
        return (
            jnp.where(has_low_x, jnp.where(even_x, b, a), 0.0),
            jnp.where(has_high_x, jnp.where(even_x, a, b), 0.0),
        )

    def radial_halo(lo, n):
        a, b = beside_even[lo : lo + n, :], beside_odd[lo : lo + n, :]
        return (
            jnp.where(has_low_y, jnp.where(even_y, b, a), 0.0),
            jnp.where(has_high_y, jnp.where(even_y, a, b), 0.0),
        )

    base = 2 * FIELDS * tile
    corners = radial_halo(base, 3 * tile)

    def corner(side_y, side_x, f):
        at = side_x * tile + f if f < FLOW else 2 * tile + side_x
        return corners[side_y][at : at + 1]

    def own(f):
        ref, at = (species, f) if f < SPECIES else (velocity, f - SPECIES) if f < FLOW else (diffusivity, 0)
        main = ref[at * rows : (at + 1) * rows, :].reshape(width_x, width_y, depth)
        edges = [ref[pl.ds(at * rows + y, width_x, stride=width_y), :] for y in (0, width_y - 1)]
        return main, edges

    def assemble(f):
        main, edges = own(f)
        low_x, high_x = axial_halo(2 * f * tile, 2 * tile)
        long = jnp.concatenate(
            [low_x.reshape(2, tile, depth), main, high_x.reshape(2, tile, depth)], axis=0
        )
        low_y, high_y = radial_halo(2 * f * tile, 2 * tile)
        near = [low_y[tile:], high_y[:tile]]
        far = [low_y[:tile], high_y[tile:]]
        before, after = (
            jnp.concatenate(
                [corner(s, 0, f).reshape(1, 1, depth)]
                + [near[s][i : i + 1].reshape(1, 1, depth) for i in range(width_x)]
                + [corner(s, 1, f).reshape(1, 1, depth)],
                axis=0,
            )
            for s in range(2)
        )
        inner = long[1:-1]
        y_pair = shifted_row(inner, before, after)
        main_pairs = [(long[:-2], long[2:]), y_pair, shifted_z(inner)]
        side = []
        for s in range(2):
            x_pair = shifted_row(near[s], corner(s, 0, f), corner(s, 1, f))
            y_side = (far[s], edges[s]) if s == 0 else (edges[s], far[s])
            side.append((near[s], [x_pair, y_side, shifted_z(near[s])]))
        return long, inner, main_pairs, side, far, edges, main

    held = [assemble(f) for f in range(FIELDS)]

    def start_of(get):
        return coefficient(get(held[5]), get(held[6]), get(held[7]), get(held[8]))

    start_inner = start_of(lambda h: h[1])
    start_main = [
        tuple(start_of(lambda h, i=i, j=j: h[2][i][j]) for j in range(2)) for i in range(3)
    ]
    start_side = []
    for s in range(2):
        start_side.append(
            (
                start_of(lambda h: h[3][s][0]),
                [
                    tuple(start_of(lambda h, i=i, j=j: h[3][s][1][i][j]) for j in range(2))
                    for i in range(3)
                ],
            )
        )

    x_of = lax.broadcasted_iota(I32, (width_x + 2, 1, 1), 0)
    first, first_side = [], []
    for f in range(FLOW):
        _, inner, pairs, side, _, _, _ = held[f]
        value = inner + change(inner, start_inner, pairs, start_main)
        low = jnp.where(has_low_x, value[:1], 0.0)
        high = jnp.where(has_high_x, value[-1:], 0.0)
        first.append(jnp.concatenate([low, value[1:-1], high], axis=0))
        sides = []
        for s, has in ((0, has_low_y), (1, has_high_y)):
            x, others = side[s]
            moved = x + change(x, start_side[s][0], others, start_side[s][1])
            sides.append(jnp.where(has, moved, 0.0))
        first_side.append(sides)

    base_inner = held[8][1]
    base_side = [held[8][3][s][0] for s in range(2)]
    later = coefficient(first[5], first[6], first[7], base_inner)
    later_side = [
        coefficient(first_side[5][s], first_side[6][s], first_side[7][s], base_side[s]) for s in range(2)
    ]

    def second_pairs(long, sides):
        main = long[1:-1]
        before, after = (
            jnp.concatenate([sides[s][i : i + 1].reshape(1, 1, depth) for i in range(width_x)], axis=0)
            for s in range(2)
        )
        return main, [(long[:-2], long[2:]), shifted_row(main, before, after), shifted_z(main)]

    later_main, later_pairs = second_pairs(later, later_side)
    for f in range(FLOW):
        main, pairs = second_pairs(first[f], first_side[f])
        value = 0.5 * (held[f][6] + main + change(main, later_main, pairs, later_pairs))
        value = value.reshape(rows, depth)
        part = 0 if f == 0 else f - SPECIES + 1 if f >= SPECIES else None
        if part is not None:
            value = value + time_step * source[part * rows : (part + 1) * rows, :]
        ref, at = (species_out, f) if f < SPECIES else (velocity_out, f - SPECIES)
        ref[at * rows : (at + 1) * rows, :] = value

    movers = arrivals.shape[-1]
    low, high = axial_halo(base, ROWS)
    arrivals[0] = low[:, :movers]
    arrivals[1] = high[:, movers : 2 * movers]
    low, high = radial_halo(base + 3 * tile, ROWS)
    arrivals[2] = low[:, :movers]
    arrivals[3] = high[:, movers : 2 * movers]


def call(kernel, outs, ins, flops, name, smem=(), aliases=None):
    vmem = pl.BlockSpec(memory_space=pltpu.VMEM)
    scalar = pl.BlockSpec(memory_space=pltpu.SMEM)
    moved = sum(int(np.prod(x.shape)) * 4 for x in list(ins) + list(outs))
    return pl.pallas_call(
        kernel,
        out_shape=[jax.ShapeDtypeStruct(s.shape, s.dtype) for s in outs],
        in_specs=[scalar if i in smem else vmem for i in range(len(ins))],
        out_specs=[vmem] * len(outs),
        compiler_params=pltpu.CompilerParams(vmem_limit_bytes=VMEM_LIMIT),
        cost_estimate=pl.CostEstimate(flops=flops, bytes_accessed=moved, transcendentals=0),
        input_output_aliases=aliases or {},
        name=name,
    )(*ins)


def f32(*shape):
    return jax.ShapeDtypeStruct(shape, F32)


def body(sizes, species, velocity, diffusivity, parcels, counts, cells, leave_slots, leave_counts):
    _, width_x, width_y, depth = species.shape
    rows = width_x * width_y
    slots, movers = parcels.shape[-1], leave_slots.shape[-1]
    assert depth == LANES == 2 * movers and width_x == width_y == 8
    permute = lambda x, axis, odd: lax.ppermute(x, AXES, pairing(sizes, axis, odd))
    species2 = species.reshape(SPECIES * rows, depth)
    velocity2 = velocity.reshape(VECTORS * rows, depth)
    diffusivity2 = diffusivity.reshape(rows, depth)
    parcels2 = parcels.reshape(ROWS, slots)
    axial_rows = 2 * FIELDS * width_y + ROWS
    radial_rows = axial_rows + 3 * width_y

    axial_even, axial_odd, radial_even, radial_odd, leaving = call(
        functools.partial(pack_kernel, width_x, width_y),
        [f32(axial_rows, depth)] * 2 + [f32(radial_rows, depth)] * 2 + [f32(slots // LANES, LANES)],
        [
            species2, velocity2, diffusivity2, parcels2, cells.reshape(slots // LANES, LANES),
            leave_slots.reshape(4, movers), leave_counts,
        ],
        10**8, "pack_faces", smem=(6,),
    )
    from_even = permute(axial_even, 0, False)
    from_odd = permute(axial_odd, 0, True)
    staying, source = call(
        functools.partial(parcel_kernel, width_x, width_y),
        [f32(ROWS, slots), f32(4 * rows, depth)],
        [velocity2, parcels2, cells.reshape(1, 1, slots), counts, leaving],
        10**9, "push_parcels", smem=(3,),
    )
    radial_even, radial_odd = call(
        functools.partial(corner_kernel, width_x, width_y),
        [f32(radial_rows, depth)] * 2,
        [from_even, from_odd, radial_even, radial_odd],
        10**6, "put_corners",
    )
    beside_even = permute(radial_even, 1, False)
    beside_odd = permute(radial_odd, 1, True)
    species_out, velocity_out, arrivals = call(
        functools.partial(stencil_kernel, width_x, width_y),
        [f32(SPECIES * rows, depth), f32(VECTORS * rows, depth), f32(4, ROWS, movers)],
        [species2, velocity2, diffusivity2, from_even, from_odd, beside_even, beside_odd, source],
        10**7, "stencils",
    )
    return (
        species_out.reshape(species.shape),
        velocity_out.reshape(velocity.shape),
        staying[None, None],
        arrivals[None, None],
    )


def solution(mesh):
    sizes = tuple(mesh.shape[axis] for axis in AXES)
    return jax.shard_map(
        functools.partial(body, sizes),
        mesh=mesh,
        in_specs=(
            P(None, "axial", "radial", None),
            P(None, "axial", "radial", None),
            P("axial", "radial", None),
            P("axial", "radial", None, None),
            P("axial", "radial"),
            P("axial", "radial", None),
            P("axial", "radial", None, None),
            P("axial", "radial", None),
        ),
        out_specs=(
            P(None, "axial", "radial", None),
            P(None, "axial", "radial", None),
            P("axial", "radial", None, None),
            P("axial", "radial", None, None, None),
        ),
        check_vma=False,
    )
```

time: 103 us -> 19.5 us (0.19)
  the two profiles are of different devices: /device:TPU:12 before, /device:TPU:20 now
where the time goes in v1:
time: 19.5 us; the launch traced here: 19.2 us
  waiting for transfers between devices  6.45 us (33%)
  local copies, waits for them, and re-layouts  4.16 us (21%)
  Pallas kernels  3.99 us (20%)
  starting transfers between devices  3.25 us (17%)
  between operations  1.37 us (7%)
    ppermute x4, waiting for transfers between devices, body(): lax.ppermute(x, AXES, pairing(sizes, axis, odd))  6.45 us
    unnamed x20, local copies, waits for them, and re-layouts  4.16 us
    pallas_call x4, Pallas kernels, call(): pl.pallas_call(kernel, out_shape=[jax.ShapeDtypeStruct(s.shape, s.dtype)...  3.99 us
    ppermute x4, starting transfers between devices, body(): lax.ppermute(x, AXES, pairing(sizes, axis, odd))  3.25 us
  transfers between devices with their start and end apart: 4, of which 3 were waited for; matrix products, arithmetic and copies ran while one was open for 0% of the time, Pallas kernels for 7%

profile of v1, /device:TPU:20, one launch (start us, length us, event | category | flops | bytes accessed | tf_op | source)
XLA Modules:
  0.0 19.2 jit_solution(7142611888899763494)
XLA Ops:
  0.6 0.0 copy-start.7
  0.6 0.0 copy-start.8
  0.7 0.0 copy-start.9
  0.7 0.7 %copy-done.7 = s32[1,1,2048]{2,1,0:T(1,128)S(1)} copy-done((s32[1,1,2048]{2,1,0:T(1,128)S(1)}, s32[1,1,2048]{2,1,0:T(1,128)}, u32[]{:S(2)}) %copy-start.7) | copy-done | bytes 8216
  1.3 0.0 copy-done.8
  1.3 0.0 copy-done.9
  1.3 0.0 copy-start
  1.3 0.9 %copy-done = f32[5,8,8,128]{3,2,1,0:T(8,128)S(1)} copy-done((f32[5,8,8,128]{3,2,1,0:T(8,128)S(1)}, f32[5,8,8,128]{3,2,1,0:T(8,128)}, u32[]{:S(2)}) %copy-start) | copy-done | bytes 163864
  2.3 0.0 copy-start.2
  2.3 0.9 %copy-done.2 = f32[3,8,8,128]{3,2,1,0:T(8,128)S(1)} copy-done((f32[3,8,8,128]{3,2,1,0:T(8,128)S(1)}, f32[3,8,8,128]{3,2,1,0:T(8,128)}, u32[]{:S(2)}) %copy-start.2) | copy-done | bytes 98328
  3.1 0.0 copy-start.4
  3.1 0.9 %copy-done.4 = f32[1,1,16,2048]{3,2,1,0:T(8,128)S(1)} copy-done((f32[1,1,16,2048]{3,2,1,0:T(8,128)S(1)}, f32[1,1,16,2048]{3,2,1,0:T(8,128)}, u32[]{:S(2)}) %copy-start.4) | copy-done | bytes 131096
  4.1 0.0 copy-start.6
  4.1 0.8 %copy-done.6 = f32[8,8,128]{2,1,0:T(8,128)S(1)} copy-done((f32[8,8,128]{2,1,0:T(8,128)S(1)}, f32[8,8,128]{2,1,0:T(8,128)}, u32[]{:S(2)}) %copy-start.6) | copy-done | bytes 32792
  4.8 1.1 %pack_faces.1 = (f32[160,128]{1,0:T(8,128)S(1)}, f32[160,128]{1,0:T(8,128)S(1)}, f32[184,128]{1,0:T(8,128)S(1)}, f32[184,128]{1,0:T(8,128)S(1)}, f32[16,128]{1,0:T(8,128)S(1)}) custom-call(f32[320,128]{1,0:T(8,128)S(1)} %bitcast.10, f32[192,128]{1,0:T(8,128)S(1)} %bitcast.12, f32[64,128]{1,0:T(8,128)S(1)} %bitcast.17, f32[16,2048]{1,0:T(8,128)S(1)} %bitcast.15, ...), custom_call_target="tpu_custom_call" | custom-call | flops 100000000 | bytes 795664 | tf_op jit(solution)/shard_map/pack_faces/pallas_call | solution.py:377
  5.9 0.1 collective-permute-start
  6.0 1.5 %collective-permute-start.1 = (f32[160,128]{1,0:T(8,128)S(1)}, f32[160,128]{1,0:T(8,128)S(1)}, u32[]{:S(2)}, u32[]{:S(2)}) collective-permute-start(f32[160,128]{1,0:T(8,128)S(1)} %get-tuple-element.17), channel_id=1, source_target_pairs={{0,1},{1,0},{2,3},{3,2},{4,8},{5,9},{6,10},{7,11},{8,4},{9,5},{10,... | collective-permute-start | bytes 245768 | tf_op jit(solution)/shard_map/ppermute | solution.py:398
  7.5 0.0 collective-permute-done.from_even
  7.5 3.8 %collective-permute-done.1.from_odd = f32[160,128]{1,0:T(8,128)S(1)} collective-permute-done((f32[160,128]{1,0:T(8,128)S(1)}, f32[160,128]{1,0:T(8,128)S(1)}, u32[]{:S(2)}, u32[]{:S(2)}) %collective-permute-start.1) | collective-permute-done | bytes 81952 | tf_op jit(solution)/shard_map/ppermute | solution.py:398
  11.3 0.0 copy-start.3
  11.3 0.0 copy-start.5
  11.3 0.1 put_corners.1
  11.4 1.6 %collective-permute-start.2 = (f32[184,128]{1,0:T(8,128)S(1)}, f32[184,128]{1,0:T(8,128)S(1)}, u32[]{:S(2)}, u32[]{:S(2)}) collective-permute-start(f32[184,128]{1,0:T(8,128)S(1)} %get-tuple-element.20), channel_id=1, source_target_pairs={{0,1},{1,0},{2,3},{3,2},{4,5},{5,4},{6,7},{7,6},{8,9},{9,8},{10,11... | collective-permute-start | bytes 282632 | tf_op jit(solution)/shard_map/ppermute | solution.py:398
  13.0 0.0 collective-permute-start.3
  13.7 0.0 copy-done.3
  13.7 0.0 copy-done.5
  13.7 0.0 copy-start.1
  13.7 1.3 %push_parcels.1 = (f32[16,2048]{1,0:T(8,128)}, f32[256,128]{1,0:T(8,128)S(1)}) custom-call(f32[192,128]{1,0:T(8,128)S(1)} %bitcast.13, f32[16,2048]{1,0:T(8,128)S(1)} %bitcast.16, s32[1,1,2048]{2,1,0:T(1,128)S(1)} %copy-done.7, s32[1,1]{1,0:T(1,128)S(6)} %copy.12.counts, f32[16,128]{1,0:T(8,128)S(1)} %get-tuple-element.22.leaving), custom_call_target="tpu_custom_call" | custom-call | flops 1000000000 | bytes 507908 | tf_op jit(solution)/shard_map/push_parcels/pallas_call | solution.py:377
  15.0 1.0 %collective-permute-done.2.beside_even = f32[184,128]{1,0:T(8,128)S(1)} collective-permute-done((f32[184,128]{1,0:T(8,128)S(1)}, f32[184,128]{1,0:T(8,128)S(1)}, u32[]{:S(2)}, u32[]{:S(2)}) %collective-permute-start.2) | collective-permute-done | bytes 94240 | tf_op jit(solution)/shard_map/ppermute | solution.py:398
  16.0 1.6 %collective-permute-done.3.beside_odd = f32[184,128]{1,0:T(8,128)S(1)} collective-permute-done((f32[184,128]{1,0:T(8,128)S(1)}, f32[184,128]{1,0:T(8,128)S(1)}, u32[]{:S(2)}, u32[]{:S(2)}) %collective-permute-start.3) | collective-permute-done | bytes 94240 | tf_op jit(solution)/shard_map/ppermute | solution.py:398
  17.6 0.0 copy-done.1
  17.6 1.6 %stencils.1 = (f32[320,128]{1,0:T(8,128)}, f32[192,128]{1,0:T(8,128)}, f32[4,16,64]{2,1,0:T(8,128)}) custom-call(f32[320,128]{1,0:T(8,128)S(1)} %bitcast.11, f32[192,128]{1,0:T(8,128)S(1)} %bitcast.14, f32[64,128]{1,0:T(8,128)S(1)} %bitcast.18, f32[160,128]{1,0:T(8,128)S(1)} %collective-permute-done.from_even, ...), custom_call_target="tpu_custom_call" | custom-call | flops 10000000 | bytes 1056768 | tf_op jit(solution)/shard_map/stencils/pallas_call | solution.py:377
Async XLA Ops:
  0.6 0.7 %copy-start.7 = (s32[1,1,2048]{2,1,0:T(1,128)S(1)}, s32[1,1,2048]{2,1,0:T(1,128)}, u32[]{:S(2)}) copy-start(s32[1,1,2048]{2,1,0:T(1,128)} %cells.1) | copy-start | bytes 24580
  0.6 0.7 %copy-start.8 = (s32[1,1,4,64]{3,2,1,0:T(4,128)S(1)}, s32[1,1,4,64]{3,2,1,0:T(4,128)}, u32[]{:S(2)}) copy-start(s32[1,1,4,64]{3,2,1,0:T(4,128)} %param.14) | copy-start | bytes 3076
  0.7 0.7 %copy-start.9 = (s32[1,1,4]{2,1,0:T(1,128)S(1)}, s32[1,1,4]{2,1,0:T(1,128)}, u32[]{:S(2)}) copy-start(s32[1,1,4]{2,1,0:T(1,128)} %face_counts.1) | copy-start | bytes 52
  1.3 0.9 %copy-start = (f32[5,8,8,128]{3,2,1,0:T(8,128)S(1)}, f32[5,8,8,128]{3,2,1,0:T(8,128)}, u32[]{:S(2)}) copy-start(f32[5,8,8,128]{3,2,1,0:T(8,128)} %param.8) | copy-start | bytes 491524
  2.3 0.9 %copy-start.2 = (f32[3,8,8,128]{3,2,1,0:T(8,128)S(1)}, f32[3,8,8,128]{3,2,1,0:T(8,128)}, u32[]{:S(2)}) copy-start(f32[3,8,8,128]{3,2,1,0:T(8,128)} %param.9) | copy-start | bytes 294916
  3.1 0.9 %copy-start.4 = (f32[1,1,16,2048]{3,2,1,0:T(8,128)S(1)}, f32[1,1,16,2048]{3,2,1,0:T(8,128)}, u32[]{:S(2)}) copy-start(f32[1,1,16,2048]{3,2,1,0:T(8,128)} %param.11) | copy-start | bytes 393220
  4.1 0.8 %copy-start.6 = (f32[8,8,128]{2,1,0:T(8,128)S(1)}, f32[8,8,128]{2,1,0:T(8,128)}, u32[]{:S(2)}) copy-start(f32[8,8,128]{2,1,0:T(8,128)} %param.10) | copy-start | bytes 98308
  5.9 1.6 %collective-permute-start = (f32[160,128]{1,0:T(8,128)S(1)}, f32[160,128]{1,0:T(8,128)S(1)}, u32[]{:S(2)}, u32[]{:S(2)}) collective-permute-start(f32[160,128]{1,0:T(8,128)S(1)} %get-tuple-element.16), channel_id=1, source_target_pairs={{0,4},{1,5},{2,6},{3,7},{4,0},{5,1},{6,2},{7,3},{8,12},{9,13},{10,... | collective-permute-start | bytes 245768 | tf_op jit(solution)/shard_map/ppermute | solution.py:398
  6.0 5.4 %collective-permute-start.1 = (f32[160,128]{1,0:T(8,128)S(1)}, f32[160,128]{1,0:T(8,128)S(1)}, u32[]{:S(2)}, u32[]{:S(2)}) collective-permute-start(f32[160,128]{1,0:T(8,128)S(1)} %get-tuple-element.17), channel_id=1, source_target_pairs={{0,1},{1,0},{2,3},{3,2},{4,8},{5,9},{6,10},{7,11},{8,4},{9,5},{10,... | collective-permute-start | bytes 245768 | tf_op jit(solution)/shard_map/ppermute | solution.py:398
  11.3 2.4 %copy-start.3 = (f32[3,8,8,128]{3,2,1,0:T(8,128)S(1)}, f32[3,8,8,128]{3,2,1,0:T(8,128)}, u32[]{:S(2)}) copy-start(f32[3,8,8,128]{3,2,1,0:T(8,128)} %param.9) | copy-start | bytes 294916
  11.3 2.4 %copy-start.5 = (f32[1,1,16,2048]{3,2,1,0:T(8,128)S(1)}, f32[1,1,16,2048]{3,2,1,0:T(8,128)}, u32[]{:S(2)}) copy-start(f32[1,1,16,2048]{3,2,1,0:T(8,128)} %param.11) | copy-start | bytes 393220
  11.4 4.6 %collective-permute-start.2 = (f32[184,128]{1,0:T(8,128)S(1)}, f32[184,128]{1,0:T(8,128)S(1)}, u32[]{:S(2)}, u32[]{:S(2)}) collective-permute-start(f32[184,128]{1,0:T(8,128)S(1)} %get-tuple-element.20), channel_id=1, source_target_pairs={{0,1},{1,0},{2,3},{3,2},{4,5},{5,4},{6,7},{7,6},{8,9},{9,8},{10,11... | collective-permute-start | bytes 282632 | tf_op jit(solution)/shard_map/ppermute | solution.py:398
  13.0 4.6 %collective-permute-start.3 = (f32[184,128]{1,0:T(8,128)S(1)}, f32[184,128]{1,0:T(8,128)S(1)}, u32[]{:S(2)}, u32[]{:S(2)}) collective-permute-start(f32[184,128]{1,0:T(8,128)S(1)} %get-tuple-element.21), channel_id=1, source_target_pairs={{0,4},{1,2},{2,1},{3,7},{4,0},{5,6},{6,5},{7,3},{8,12},{9,10},{10,... | collective-permute-start | bytes 282632 | tf_op jit(solution)/shard_map/ppermute | solution.py:398
  13.7 3.9 %copy-start.1 = (f32[5,8,8,128]{3,2,1,0:T(8,128)S(1)}, f32[5,8,8,128]{3,2,1,0:T(8,128)}, u32[]{:S(2)}) copy-start(f32[5,8,8,128]{3,2,1,0:T(8,128)} %param.8) | copy-start | bytes 491524

commit v2 on v1

--- a/solution.py
+++ b/solution.py
@@ -63,9 +63,24 @@
 
 
 def pack_kernel(
-    width_x, width_y, species, velocity, diffusivity, parcels, cells, slots, face_counts,
-    axial_even, axial_odd, radial_even, radial_odd, leaving,
+    width_x, width_y, species_in, velocity_in, diffusivity_in, parcels_in, cells_in, slots_in, face_counts_in,
+    axial_even, axial_odd, radial_even, radial_odd, kept,
+    species, velocity, diffusivity, parcels, cells, slots, face_counts, arrived,
 ):
+    copies = [
+        pltpu.make_async_copy(src, dst, arrived.at[i])
+        for i, (src, dst) in enumerate(
+            (
+                (slots_in, slots), (face_counts_in, face_counts), (cells_in, cells),
+                (parcels_in, parcels), (velocity_in, velocity), (species_in, species),
+                (diffusivity_in, diffusivity),
+            )
+        )
+    ]
+    for copy in copies:
+        copy.start()
+    for copy in copies:
+        copy.wait()
     cells_of = width_x * width_y
     even_x = lax.rem(lax.axis_index("axial"), 2) == 0
     even_y = lax.rem(lax.axis_index("radial"), 2) == 0
@@ -97,8 +112,8 @@
     chunks = parcels.shape[1] // LANES
     hot_place = one_hot(place, LANES)
     hot_chunk = lax.broadcasted_iota(I32, (chunks, slot.shape[1]), 0) == chunk
-    count = dot_t(jnp.where(hot_chunk, valid, 0.0).astype(BF16), hot_place)
-    leaving[...] = count
+    leaving = dot_t(jnp.where(hot_chunk, valid, 0.0).astype(BF16), hot_place)
+    kept[...] = jnp.where(leaving > 0.5, 0.0, 1.0)
     stacked = jnp.concatenate([parcels[:, h * LANES : (h + 1) * LANES] for h in range(chunks)], axis=0)
     cell = cells[...]
     cell_high = lax.shift_right_logical(cell, 7).astype(F32)
@@ -124,14 +139,11 @@
     pushed.extend(rows[6 + i : 7 + i] + time_step * pushed[i] for i in range(3))
     base = 2 * FIELDS * tile
     for packets, lo in (((axial_even, axial_odd), 0), ((radial_even, radial_odd), 2 * movers)):
-        skip = 0 if lo == 0 else 3 * tile
         for ref in packets:
             part = slice(lo, lo + 2 * movers)
             for i, row in enumerate(pushed):
-                ref[base + skip + i : base + skip + i + 1, :] = row[:, part] * valid[:, part]
-            ref[base + skip + 9 : base + skip + ROWS, :] = rows[9:ROWS, part] * valid[:, part]
-    for ref in (radial_even, radial_odd):
-        ref[base : base + 3 * tile, :] = jnp.zeros((3 * tile, LANES), F32)
+                ref[base + i : base + i + 1, :] = row[:, part] * valid[:, part]
+            ref[base + 9 : base + ROWS, :] = rows[9:ROWS, part] * valid[:, part]
 
 
 def gas_at(velocity, row_of, hot_lane, rows):
@@ -142,22 +154,18 @@
     return [pick(table[i * rows : (i + 1) * rows], row_of) for i in range(VECTORS)]
 
 
-def parcel_kernel(width_x, width_y, velocity, parcels, cells, counts, leaving, staying, source):
+def parcel_kernel(width_x, width_y, velocity, parcels, cells, kept, counts, staying_out, source, staying, sent):
     rows = width_x * width_y
     slots = parcels.shape[1]
     cell = cells[0]
     row_of, lane_of = lax.shift_right_logical(cell, 7), lax.bitwise_and(cell, LANES - 1)
     hot_lane = one_hot(lane_of, LANES)
     gas = gas_at(velocity[...], row_of, hot_lane, rows)
-    live = counts[0, 0]
-    slot = lax.broadcasted_iota(I32, (1, slots), 1)
-    live_weight = (slot < live).astype(F32)
     chunks = slots // LANES
-    stay = jnp.where(leaving[...] > 0.5, 0.0, 1.0)
-    keep = jnp.concatenate([stay[h : h + 1] for h in range(chunks)], axis=1) * live_weight
+    live = (lax.broadcasted_iota(I32, (1, slots), 1) < counts[0, 0]).astype(F32)
+    keep = jnp.concatenate([kept[h : h + 1, :] for h in range(chunks)], axis=1) * live
     mass, response, evaporation = parcels[3:4], parcels[4:5], parcels[5:6]
     drag = [response * (gas[i] - parcels[i : i + 1]) for i in range(3)]
-    deposits = [mass * evaporation] + [-mass * d for d in drag]
     for i in range(3):
         moved = parcels[i : i + 1] + time_step * drag[i]
         staying[i : i + 1, :] = moved * keep
@@ -165,41 +173,40 @@
     staying[3:4, :] = mass * (1.0 - time_step * evaporation) * keep
     staying[4:6, :] = parcels[4:6] * keep
     staying[9:ROWS, :] = parcels[9:ROWS] * keep
+    copy = pltpu.make_async_copy(staying, staying_out, sent)
+    copy.start()
+    deposits = [mass * evaporation] + [-mass * d for d in drag]
     hot_row = one_hot(row_of, rows)
-    halves = [split(d * live_weight) for d in deposits]
+    halves = [split(d * live) for d in deposits]
     left = jnp.concatenate([hot_row * half[i] for i in range(2) for half in halves], axis=0)
     total = dot_t(left, hot_lane)
     source[...] = total[: 4 * rows] + total[4 * rows :]
-
-
-def corner_kernel(
-    width_x, width_y, from_even, from_odd, even_in, odd_in, radial_even, radial_odd
-):
+    copy.wait()
+
+
+def corner_kernel(width_x, width_y, from_even, from_odd, radial_even, radial_odd):
     tile = width_y
-    base = 2 * FIELDS * tile
     even_x = lax.rem(lax.axis_index("axial"), 2) == 0
     even_y = lax.rem(lax.axis_index("radial"), 2) == 0
     at_x, size_x = lax.axis_index("axial"), lax.axis_size("axial")
     has = [at_x > 0, at_x < size_x - 1]
-    radial_even[...] = even_in[...]
-    radial_odd[...] = odd_in[...]
+    for ref in (radial_even, radial_odd):
+        ref[2 * tile : 3 * tile, :] = jnp.zeros((tile, LANES), F32)
     for side in range(2):
         layer = 1 - side
-        for y, part in ((0, "low"), (width_y - 1, "high")):
-            flow = [
-                ref[pl.ds(layer * tile + y, FLOW, stride=2 * tile), :] for ref in (from_even, from_odd)
-            ]
-            base_rate = [
-                ref[pl.ds((2 * FLOW + layer) * tile + y, 1), :] for ref in (from_even, from_odd)
-            ]
-            lower_is_odd = even_x if side == 0 else jnp.logical_not(even_x)
-            choose = lambda v: jnp.where(has[side], jnp.where(lower_is_odd, v[1], v[0]), 0.0)
-            flow, base_rate = choose(flow), choose(base_rate)
-            for ref, is_high in ((radial_even, even_y), (radial_odd, jnp.logical_not(even_y))):
-                @pl.when(is_high if part == "high" else jnp.logical_not(is_high))
-                def _(ref=ref, flow=flow, base_rate=base_rate, side=side):
-                    ref[base + side * tile : base + side * tile + FLOW, :] = flow
-                    ref[base + 2 * tile + side : base + 2 * tile + side + 1, :] = base_rate
+        lower_is_odd = even_x if side == 0 else jnp.logical_not(even_x)
+        choose = lambda v: jnp.where(has[side], jnp.where(lower_is_odd, v[1], v[0]), 0.0)
+        flow, base_rate = [], []
+        for y in (0, width_y - 1):
+            flow.append(
+                choose([r[pl.ds(layer * tile + y, FLOW, stride=2 * tile), :] for r in (from_even, from_odd)])
+            )
+            base_rate.append(
+                choose([r[pl.ds((2 * FLOW + layer) * tile + y, 1), :] for r in (from_even, from_odd)])
+            )
+        for ref, high in ((radial_even, even_y), (radial_odd, jnp.logical_not(even_y))):
+            ref[side * tile : side * tile + FLOW, :] = jnp.where(high, flow[1], flow[0])
+            ref[2 * tile + side : 2 * tile + side + 1, :] = jnp.where(high, base_rate[1], base_rate[0])
 
 
 def coefficient(vel_first, vel_second, vel_third, base_rate):
@@ -232,8 +239,8 @@
 
 
 def stencil_kernel(
-    width_x, width_y, species, velocity, diffusivity, from_even, from_odd, beside_even, beside_odd, source,
-    species_out, velocity_out, arrivals,
+    width_x, width_y, species, velocity, diffusivity, from_even, from_odd, beside_even, beside_odd, corner_even, corner_odd, source,
+    species_out, velocity_out, arrivals_out, result, arrivals, sent,
 ):
     tile = width_y
     rows = width_x * width_y
@@ -251,15 +258,15 @@
             jnp.where(has_high_x, jnp.where(even_x, a, b), 0.0),
         )
 
-    def radial_halo(lo, n):
-        a, b = beside_even[lo : lo + n, :], beside_odd[lo : lo + n, :]
+    def radial_halo(lo, n, refs=(beside_even, beside_odd)):
+        a, b = (ref[lo : lo + n, :] for ref in refs)
         return (
             jnp.where(has_low_y, jnp.where(even_y, b, a), 0.0),
             jnp.where(has_high_y, jnp.where(even_y, a, b), 0.0),
         )
 
     base = 2 * FIELDS * tile
-    corners = radial_halo(base, 3 * tile)
+    corners = radial_halo(0, 3 * tile, (corner_even, corner_odd))
 
     def corner(side_y, side_x, f):
         at = side_x * tile + f if f < FLOW else 2 * tile + side_x
@@ -350,6 +357,16 @@
         )
         return main, [(long[:-2], long[2:]), shifted_row(main, before, after), shifted_z(main)]
 
+    movers = arrivals.shape[-1]
+    low, high = axial_halo(base, ROWS)
+    arrivals[0] = low[:, :movers]
+    arrivals[1] = high[:, movers : 2 * movers]
+    low, high = radial_halo(base, ROWS)
+    arrivals[2] = low[:, :movers]
+    arrivals[3] = high[:, movers : 2 * movers]
+    copies = [pltpu.make_async_copy(arrivals, arrivals_out, sent.at[FLOW])]
+    copies[0].start()
+
     later_main, later_pairs = second_pairs(later, later_side)
     for f in range(FLOW):
         main, pairs = second_pairs(first[f], first_side[f])
@@ -358,30 +375,26 @@
         part = 0 if f == 0 else f - SPECIES + 1 if f >= SPECIES else None
         if part is not None:
             value = value + time_step * source[part * rows : (part + 1) * rows, :]
+        result[f] = value
         ref, at = (species_out, f) if f < SPECIES else (velocity_out, f - SPECIES)
-        ref[at * rows : (at + 1) * rows, :] = value
-
-    movers = arrivals.shape[-1]
-    low, high = axial_halo(base, ROWS)
-    arrivals[0] = low[:, :movers]
-    arrivals[1] = high[:, movers : 2 * movers]
-    low, high = radial_halo(base + 3 * tile, ROWS)
-    arrivals[2] = low[:, :movers]
-    arrivals[3] = high[:, movers : 2 * movers]
-
-
-def call(kernel, outs, ins, flops, name, smem=(), aliases=None):
-    vmem = pl.BlockSpec(memory_space=pltpu.VMEM)
-    scalar = pl.BlockSpec(memory_space=pltpu.SMEM)
+        copies.append(pltpu.make_async_copy(result.at[f], ref.at[pl.ds(at * rows, rows), :], sent.at[f]))
+        copies[-1].start()
+    for copy in copies:
+        copy.wait()
+
+
+def call(kernel, outs, ins, flops, name, scratch=(), smem=(), far_ins=(), far_outs=()):
+    vmem, scalar, far = (pl.BlockSpec(memory_space=m) for m in (pltpu.VMEM, pltpu.SMEM, pltpu.HBM))
     moved = sum(int(np.prod(x.shape)) * 4 for x in list(ins) + list(outs))
+    ins = [pltpu.with_memory_space_constraint(x, pltpu.HBM) if i in far_ins else x for i, x in enumerate(ins)]
     return pl.pallas_call(
         kernel,
         out_shape=[jax.ShapeDtypeStruct(s.shape, s.dtype) for s in outs],
-        in_specs=[scalar if i in smem else vmem for i in range(len(ins))],
-        out_specs=[vmem] * len(outs),
+        in_specs=[far if i in far_ins else scalar if i in smem else vmem for i in range(len(ins))],
+        out_specs=[far if i in far_outs else vmem for i in range(len(outs))],
+        scratch_shapes=list(scratch),
         compiler_params=pltpu.CompilerParams(vmem_limit_bytes=VMEM_LIMIT),
         cost_estimate=pl.CostEstimate(flops=flops, bytes_accessed=moved, transcendentals=0),
-        input_output_aliases=aliases or {},
         name=name,
     )(*ins)
 
@@ -400,39 +413,47 @@
     velocity2 = velocity.reshape(VECTORS * rows, depth)
     diffusivity2 = diffusivity.reshape(rows, depth)
     parcels2 = parcels.reshape(ROWS, slots)
-    axial_rows = 2 * FIELDS * width_y + ROWS
-    radial_rows = axial_rows + 3 * width_y
-
-    axial_even, axial_odd, radial_even, radial_odd, leaving = call(
+    packet_rows = 2 * FIELDS * width_y + ROWS
+    chunks = slots // LANES
+
+    def near(x):
+        return pltpu.VMEM(x.shape, x.dtype)
+
+    fields = [species2, velocity2, diffusivity2]
+    cells2 = cells.reshape(chunks, LANES)
+    slots2 = leave_slots.reshape(4, movers)
+    axial_even, axial_odd, radial_even, radial_odd, kept = call(
         functools.partial(pack_kernel, width_x, width_y),
-        [f32(axial_rows, depth)] * 2 + [f32(radial_rows, depth)] * 2 + [f32(slots // LANES, LANES)],
-        [
-            species2, velocity2, diffusivity2, parcels2, cells.reshape(slots // LANES, LANES),
-            leave_slots.reshape(4, movers), leave_counts,
-        ],
-        10**8, "pack_faces", smem=(6,),
+        [f32(packet_rows, depth)] * 4 + [f32(chunks, LANES)],
+        fields + [parcels2, cells2, slots2, leave_counts],
+        10**8, "pack_faces", far_ins=range(7),
+        scratch=[near(x) for x in fields + [parcels2, cells2, slots2]]
+        + [pltpu.SMEM(leave_counts.shape, I32), pltpu.SemaphoreType.DMA((7,))],
     )
     from_even = permute(axial_even, 0, False)
     from_odd = permute(axial_odd, 0, True)
+    beside_even = permute(radial_even, 1, False)
+    beside_odd = permute(radial_odd, 1, True)
+    counts, kept = lax.optimization_barrier((counts, kept))
     staying, source = call(
         functools.partial(parcel_kernel, width_x, width_y),
         [f32(ROWS, slots), f32(4 * rows, depth)],
-        [velocity2, parcels2, cells.reshape(1, 1, slots), counts, leaving],
-        10**9, "push_parcels", smem=(3,),
-    )
-    radial_even, radial_odd = call(
+        [velocity2, parcels2, cells.reshape(1, 1, slots), kept, counts],
+        10**9, "push_parcels", smem=(4,), far_outs=(0,),
+        scratch=[near(f32(ROWS, slots)), pltpu.SemaphoreType.DMA],
+    )
+    corner_even, corner_odd = call(
         functools.partial(corner_kernel, width_x, width_y),
-        [f32(radial_rows, depth)] * 2,
-        [from_even, from_odd, radial_even, radial_odd],
-        10**6, "put_corners",
-    )
-    beside_even = permute(radial_even, 1, False)
-    beside_odd = permute(radial_odd, 1, True)
+        [f32(3 * width_y, depth)] * 2, [from_even, from_odd], 10**6, "take_corners",
+    )
+    corner_even = permute(corner_even, 1, False)
+    corner_odd = permute(corner_odd, 1, True)
     species_out, velocity_out, arrivals = call(
         functools.partial(stencil_kernel, width_x, width_y),
         [f32(SPECIES * rows, depth), f32(VECTORS * rows, depth), f32(4, ROWS, movers)],
-        [species2, velocity2, diffusivity2, from_even, from_odd, beside_even, beside_odd, source],
-        10**7, "stencils",
+        fields + [from_even, from_odd, beside_even, beside_odd, corner_even, corner_odd, source],
+        10**7, "stencils", far_outs=(0, 1, 2),
+        scratch=[near(f32(FLOW, rows, depth)), near(f32(4, ROWS, movers)), pltpu.SemaphoreType.DMA((FLOW + 1,))],
     )
     return (
         species_out.reshape(species.shape),

time: 19.5 us -> 15 us (0.77)
  local copies, waits for them, and re-layouts: 4.16 us -> 0.02 us
  waiting for transfers between devices: 6.45 us -> 3.96 us
  starting transfers between devices: 3.25 us -> 4.83 us
  Pallas kernels: 3.99 us -> 4.66 us
    unnamed x20 -> x10, local copies, waits for them, and re-layouts: 4.16 us -> 0.02 us
    ppermute x4 -> x6, waiting for transfers between devices: 6.45 us -> 3.96 us  [body(): lax.ppermute(x, AXES, pairing(sizes, axis, odd))]
    ppermute x4 -> x6, starting transfers between devices: 3.25 us -> 4.83 us  [body(): lax.ppermute(x, AXES, pairing(sizes, axis, odd))]
    pallas_call x4, Pallas kernels: 3.99 us -> 4.66 us  [call(): pl.pallas_call(kernel, out_shape=[jax.ShapeDtypeStruct(s.shape, s.dtype)...]
  transfers between devices with their start and end apart: 4 -> 6, of which waited for: 3 -> 3; matrix products, arithmetic and copies ran while one was open for 0% -> 0% of each run, Pallas kernels for 7% -> 9%
where the time goes in v2:
time: 15 us; the launch traced here: 14.9 us
  starting transfers between devices  4.83 us (32%)
  Pallas kernels  4.66 us (31%)
  waiting for transfers between devices  3.96 us (26%)
  between operations  1.38 us (9%)
    ppermute x6, starting transfers between devices, body(): lax.ppermute(x, AXES, pairing(sizes, axis, odd))  4.83 us
    pallas_call x4, Pallas kernels, call(): pl.pallas_call(kernel, out_shape=[jax.ShapeDtypeStruct(s.shape, s.dtype)...  4.66 us
    ppermute x6, waiting for transfers between devices, body(): lax.ppermute(x, AXES, pairing(sizes, axis, odd))  3.96 us
  transfers between devices with their start and end apart: 6, of which 3 were waited for; matrix products, arithmetic and copies ran while one was open for 0% of the time, Pallas kernels for 9%

profile of v2, /device:TPU:20, one launch (start us, length us, event | category | flops | bytes accessed | tf_op | source)
XLA Modules:
  0.0 14.9 jit_solution(4402011085090823933)
XLA Ops:
  0.6 0.0 copy-start.2
  0.6 1.7 %pack_faces.1 = (f32[160,128]{1,0:T(8,128)S(1)}, f32[160,128]{1,0:T(8,128)S(1)}, f32[160,128]{1,0:T(8,128)S(1)}, f32[160,128]{1,0:T(8,128)S(1)}, f32[16,128]{1,0:T(8,128)S(1)}) custom-call(f32[320,128]{1,0:T(8,128)} %bitcast.10, f32[192,128]{1,0:T(8,128)} %bitcast.12, f32[64,128]{1,0:T(8,128)} %bitcast.17, f32[16,2048]{1,0:T(8,128)} %bitcast.15, ...), custom_call_target="tpu_custom_call" | custom-call | flops 100000000 | bytes 771088 | tf_op jit(solution)/shard_map/pack_faces/pallas_call | solution.py:390
  2.4 0.0 copy-start.1
  2.4 0.1 collective-permute-start
  2.5 1.5 %collective-permute-start.1 = (f32[160,128]{1,0:T(8,128)S(1)}, f32[160,128]{1,0:T(8,128)S(1)}, u32[]{:S(2)}, u32[]{:S(2)}) collective-permute-start(f32[160,128]{1,0:T(8,128)S(1)} %get-tuple-element.19), channel_id=1, source_target_pairs={{0,1},{1,0},{2,3},{3,2},{4,8},{5,9},{6,10},{7,11},{8,4},{9,5},{10,... | collective-permute-start | bytes 245768 | tf_op jit(solution)/shard_map/ppermute | solution.py:411
  4.0 1.6 %collective-permute-start.2 = (f32[160,128]{1,0:T(8,128)S(1)}, f32[160,128]{1,0:T(8,128)S(1)}, u32[]{:S(2)}, u32[]{:S(2)}) collective-permute-start(f32[160,128]{1,0:T(8,128)S(1)} %get-tuple-element.20), channel_id=1, source_target_pairs={{0,1},{1,0},{2,3},{3,2},{4,5},{5,4},{6,7},{7,6},{8,9},{9,8},{10,11... | collective-permute-start | bytes 245768 | tf_op jit(solution)/shard_map/ppermute | solution.py:411
  5.6 0.0 collective-permute-start.3
  6.2 0.0 copy-start.4
  6.2 0.0 collective-permute-done.from_even
  6.3 1.6 %collective-permute-done.1.from_odd = f32[160,128]{1,0:T(8,128)S(1)} collective-permute-done((f32[160,128]{1,0:T(8,128)S(1)}, f32[160,128]{1,0:T(8,128)S(1)}, u32[]{:S(2)}, u32[]{:S(2)}) %collective-permute-start.1) | collective-permute-done | bytes 81952 | tf_op jit(solution)/shard_map/ppermute | solution.py:411
  7.8 1.6 %collective-permute-start.4 = (f32[24,128]{1,0:T(8,128)S(1)}, f32[24,128]{1,0:T(8,128)S(1)}, u32[]{:S(2)}, u32[]{:S(2)}) collective-permute-start(f32[24,128]{1,0:T(8,128)S(1)} %get-tuple-element.22), channel_id=1, source_target_pairs={{0,1},{1,0},{2,3},{3,2},{4,5},{5,4},{6,7},{7,6},{8,9},{9,8},{10,11... | collective-permute-start | bytes 36872 | tf_op jit(solution)/shard_map/ppermute | solution.py:411
  9.5 0.0 copy-start
  9.5 0.0 copy-start.3
  9.5 0.0 collective-permute-start.5
  9.5 0.0 copy-done.2
  9.5 0.0 copy-done.1
  9.5 0.0 copy-done.4
  9.5 1.3 %push_parcels.1 = (f32[16,2048]{1,0:T(8,128)}, f32[256,128]{1,0:T(8,128)S(1)}) custom-call(f32[192,128]{1,0:T(8,128)S(1)} %bitcast.13, f32[16,2048]{1,0:T(8,128)S(1)} %bitcast.16, s32[1,1,2048]{2,1,0:T(1,128)S(1)} %copy-done.4, f32[16,128]{1,0:T(8,128)S(1)} %get-tuple-element.25.kept, s32[1,1]{1,0:T(1,128)S(6)} %copy.12.counts), custom_call_target="tpu_custom_call" | custom-call | flops 1000000000 | bytes 507908 | tf_op jit(solution)/shard_map/push_parcels/pallas_call | solution.py:390
  10.8 0.0 collective-permute-done.2.beside_even
  10.8 0.0 collective-permute-done.3.beside_odd
  10.8 0.8 %collective-permute-done.4.corner_even = f32[24,128]{1,0:T(8,128)S(1)} collective-permute-done((f32[24,128]{1,0:T(8,128)S(1)}, f32[24,128]{1,0:T(8,128)S(1)}, u32[]{:S(2)}, u32[]{:S(2)}) %collective-permute-start.4) | collective-permute-done | bytes 12320 | tf_op jit(solution)/shard_map/ppermute | solution.py:411
  11.6 1.6 %collective-permute-done.5.corner_odd = f32[24,128]{1,0:T(8,128)S(1)} collective-permute-done((f32[24,128]{1,0:T(8,128)S(1)}, f32[24,128]{1,0:T(8,128)S(1)}, u32[]{:S(2)}, u32[]{:S(2)}) %collective-permute-start.5) | collective-permute-done | bytes 12320 | tf_op jit(solution)/shard_map/ppermute | solution.py:411
  13.2 0.0 copy-done
  13.2 0.0 copy-done.3
  13.2 1.7 %stencils.1 = (f32[320,128]{1,0:T(8,128)}, f32[192,128]{1,0:T(8,128)}, f32[4,16,64]{2,1,0:T(8,128)}) custom-call(f32[320,128]{1,0:T(8,128)S(1)} %bitcast.11, f32[192,128]{1,0:T(8,128)S(1)} %bitcast.14, f32[64,128]{1,0:T(8,128)S(1)} %bitcast.18, f32[160,128]{1,0:T(8,128)S(1)} %collective-permute-done.from_even, ...), custom_call_target="tpu_custom_call" | custom-call | flops 10000000 | bytes 1056768 | tf_op jit(solution)/shard_map/stencils/pallas_call | solution.py:390
  (1 shorter events, 0.0 us)
Async XLA Ops:
  0.6 8.9 %copy-start.2 = (f32[1,1,16,2048]{3,2,1,0:T(8,128)S(1)}, f32[1,1,16,2048]{3,2,1,0:T(8,128)}, u32[]{:S(2)}) copy-start(f32[1,1,16,2048]{3,2,1,0:T(8,128)} %param.11) | copy-start | bytes 393220
  2.4 7.1 %copy-start.1 = (f32[3,8,8,128]{3,2,1,0:T(8,128)S(1)}, f32[3,8,8,128]{3,2,1,0:T(8,128)}, u32[]{:S(2)}) copy-start(f32[3,8,8,128]{3,2,1,0:T(8,128)} %param.9) | copy-start | bytes 294916
  2.4 3.9 %collective-permute-start = (f32[160,128]{1,0:T(8,128)S(1)}, f32[160,128]{1,0:T(8,128)S(1)}, u32[]{:S(2)}, u32[]{:S(2)}) collective-permute-start(f32[160,128]{1,0:T(8,128)S(1)} %get-tuple-element.18), channel_id=1, source_target_pairs={{0,4},{1,5},{2,6},{3,7},{4,0},{5,1},{6,2},{7,3},{8,12},{9,13},{10,... | collective-permute-start | bytes 245768 | tf_op jit(solution)/shard_map/ppermute | solution.py:411
  2.5 5.4 %collective-permute-start.1 = (f32[160,128]{1,0:T(8,128)S(1)}, f32[160,128]{1,0:T(8,128)S(1)}, u32[]{:S(2)}, u32[]{:S(2)}) collective-permute-start(f32[160,128]{1,0:T(8,128)S(1)} %get-tuple-element.19), channel_id=1, source_target_pairs={{0,1},{1,0},{2,3},{3,2},{4,8},{5,9},{6,10},{7,11},{8,4},{9,5},{10,... | collective-permute-start | bytes 245768 | tf_op jit(solution)/shard_map/ppermute | solution.py:411
  4.0 6.8 %collective-permute-start.2 = (f32[160,128]{1,0:T(8,128)S(1)}, f32[160,128]{1,0:T(8,128)S(1)}, u32[]{:S(2)}, u32[]{:S(2)}) collective-permute-start(f32[160,128]{1,0:T(8,128)S(1)} %get-tuple-element.20), channel_id=1, source_target_pairs={{0,1},{1,0},{2,3},{3,2},{4,5},{5,4},{6,7},{7,6},{8,9},{9,8},{10,11... | collective-permute-start | bytes 245768 | tf_op jit(solution)/shard_map/ppermute | solution.py:411
  5.6 5.2 %collective-permute-start.3 = (f32[160,128]{1,0:T(8,128)S(1)}, f32[160,128]{1,0:T(8,128)S(1)}, u32[]{:S(2)}, u32[]{:S(2)}) collective-permute-start(f32[160,128]{1,0:T(8,128)S(1)} %get-tuple-element.21), channel_id=1, source_target_pairs={{0,4},{1,2},{2,1},{3,7},{4,0},{5,6},{6,5},{7,3},{8,12},{9,10},{10,... | collective-permute-start | bytes 245768 | tf_op jit(solution)/shard_map/ppermute | solution.py:411
  6.2 3.3 %copy-start.4 = (s32[1,1,2048]{2,1,0:T(1,128)S(1)}, s32[1,1,2048]{2,1,0:T(1,128)}, u32[]{:S(2)}) copy-start(s32[1,1,2048]{2,1,0:T(1,128)} %cells.1) | copy-start | bytes 24580
  7.8 3.8 %collective-permute-start.4 = (f32[24,128]{1,0:T(8,128)S(1)}, f32[24,128]{1,0:T(8,128)S(1)}, u32[]{:S(2)}, u32[]{:S(2)}) collective-permute-start(f32[24,128]{1,0:T(8,128)S(1)} %get-tuple-element.22), channel_id=1, source_target_pairs={{0,1},{1,0},{2,3},{3,2},{4,5},{5,4},{6,7},{7,6},{8,9},{9,8},{10,11... | collective-permute-start | bytes 36872 | tf_op jit(solution)/shard_map/ppermute | solution.py:411
  9.5 3.7 %copy-start = (f32[5,8,8,128]{3,2,1,0:T(8,128)S(1)}, f32[5,8,8,128]{3,2,1,0:T(8,128)}, u32[]{:S(2)}) copy-start(f32[5,8,8,128]{3,2,1,0:T(8,128)} %param.8) | copy-start | bytes 491524
  9.5 3.7 %copy-start.3 = (f32[8,8,128]{2,1,0:T(8,128)S(1)}, f32[8,8,128]{2,1,0:T(8,128)}, u32[]{:S(2)}) copy-start(f32[8,8,128]{2,1,0:T(8,128)} %param.10) | copy-start | bytes 98308
  9.5 3.7 %collective-permute-start.5 = (f32[24,128]{1,0:T(8,128)S(1)}, f32[24,128]{1,0:T(8,128)S(1)}, u32[]{:S(2)}, u32[]{:S(2)}) collective-permute-start(f32[24,128]{1,0:T(8,128)S(1)} %get-tuple-element.23), channel_id=1, source_target_pairs={{0,4},{1,2},{2,1},{3,7},{4,0},{5,6},{6,5},{7,3},{8,12},{9,10},{10,... | collective-permute-start | bytes 36872 | tf_op jit(solution)/shard_map/ppermute | solution.py:411

commit v3 on v2

--- a/solution.py
+++ b/solution.py
@@ -20,23 +20,28 @@
 VMEM_LIMIT = 16 * 1024 * 1024
 
 
-def pairing(sizes, axis, odd):
-    size, other = sizes[axis], sizes[1 - axis]
-
-    def partner(here):
-        at = list(here)
-        step = 1 if (here[axis] % 2 == 1) == odd else -1
-        if 0 <= at[axis] + step < size:
-            at[axis] += step
-        elif (at[1 - axis] ^ 1) < other:
-            at[1 - axis] ^= 1
-        return tuple(at)
-
+def complete(sizes, target):
     flat = lambda at: at[0] * sizes[1] + at[1]
     blocks = [(i, j) for i in range(sizes[0]) for j in range(sizes[1])]
-    pairs = [(flat(at), flat(partner(at))) for at in blocks]
-    assert sorted(t for _, t in pairs) == list(range(len(blocks)))
+    pairs = [(flat(at), flat(target(*at))) for at in blocks]
+    assert sorted(t for _, t in pairs) == list(range(len(blocks))) and all(s != t for s, t in pairs)
     return pairs
+
+
+def axial_swap(sizes, odd):
+    def target(a, r):
+        other = a + 1 if (a % 2 == 1) == odd else a - 1
+        return (other, r) if 0 <= other < sizes[0] else (a, r ^ 1)
+
+    return complete(sizes, target)
+
+
+def radial_shift(sizes, even_up):
+    def target(a, r):
+        other = r + 1 if (a % 2 == 0) == even_up else r - 1
+        return (a, other) if 0 <= other < sizes[1] else (a ^ 1, r)
+
+    return complete(sizes, target)
 
 
 def split(x):
@@ -64,7 +69,7 @@
 
 def pack_kernel(
     width_x, width_y, species_in, velocity_in, diffusivity_in, parcels_in, cells_in, slots_in, face_counts_in,
-    axial_even, axial_odd, radial_even, radial_odd, kept,
+    axial_even, axial_odd, radial_one, radial_two, kept,
     species, velocity, diffusivity, parcels, cells, slots, face_counts, arrived,
 ):
     copies = [
@@ -83,7 +88,6 @@
         copy.wait()
     cells_of = width_x * width_y
     even_x = lax.rem(lax.axis_index("axial"), 2) == 0
-    even_y = lax.rem(lax.axis_index("radial"), 2) == 0
     tile = width_y
     for f in range(FIELDS):
         ref, base = (
@@ -97,8 +101,8 @@
             axial_odd[at, :] = jnp.where(even_x, low, high)
             low = ref[pl.ds(base * cells_of + layer, width_x, stride=width_y), :]
             high = ref[pl.ds(base * cells_of + width_y - 2 + layer, width_x, stride=width_y), :]
-            radial_even[at, :] = jnp.where(even_y, high, low)
-            radial_odd[at, :] = jnp.where(even_y, low, high)
+            radial_one[at, :] = jnp.where(even_x, high, low)
+            radial_two[at, :] = jnp.where(even_x, low, high)
 
     movers = slots.shape[1]
     lane = lax.broadcasted_iota(I32, (1, 2 * movers), 1)
@@ -138,7 +142,7 @@
     pushed.extend([response, evaporation])
     pushed.extend(rows[6 + i : 7 + i] + time_step * pushed[i] for i in range(3))
     base = 2 * FIELDS * tile
-    for packets, lo in (((axial_even, axial_odd), 0), ((radial_even, radial_odd), 2 * movers)):
+    for packets, lo in (((axial_even, axial_odd), 0), ((radial_one, radial_two), 2 * movers)):
         for ref in packets:
             part = slice(lo, lo + 2 * movers)
             for i, row in enumerate(pushed):
@@ -184,13 +188,12 @@
     copy.wait()
 
 
-def corner_kernel(width_x, width_y, from_even, from_odd, radial_even, radial_odd):
+def corner_kernel(width_x, width_y, from_odd, from_even, radial_one, radial_two):
     tile = width_y
     even_x = lax.rem(lax.axis_index("axial"), 2) == 0
-    even_y = lax.rem(lax.axis_index("radial"), 2) == 0
     at_x, size_x = lax.axis_index("axial"), lax.axis_size("axial")
     has = [at_x > 0, at_x < size_x - 1]
-    for ref in (radial_even, radial_odd):
+    for ref in (radial_one, radial_two):
         ref[2 * tile : 3 * tile, :] = jnp.zeros((tile, LANES), F32)
     for side in range(2):
         layer = 1 - side
@@ -204,7 +207,7 @@
             base_rate.append(
                 choose([r[pl.ds((2 * FLOW + layer) * tile + y, 1), :] for r in (from_even, from_odd)])
             )
-        for ref, high in ((radial_even, even_y), (radial_odd, jnp.logical_not(even_y))):
+        for ref, high in ((radial_one, even_x), (radial_two, jnp.logical_not(even_x))):
             ref[side * tile : side * tile + FLOW, :] = jnp.where(high, flow[1], flow[0])
             ref[2 * tile + side : 2 * tile + side + 1, :] = jnp.where(high, base_rate[1], base_rate[0])
 
@@ -239,7 +242,7 @@
 
 
 def stencil_kernel(
-    width_x, width_y, species, velocity, diffusivity, from_even, from_odd, beside_even, beside_odd, corner_even, corner_odd, source,
+    width_x, width_y, species, velocity, diffusivity, from_odd, from_even, beside_one, beside_two, corner_two, corner_one, source,
     species_out, velocity_out, arrivals_out, result, arrivals, sent,
 ):
     tile = width_y
@@ -247,7 +250,7 @@
     depth = LANES
     at_x, size_x = lax.axis_index("axial"), lax.axis_size("axial")
     at_y, size_y = lax.axis_index("radial"), lax.axis_size("radial")
-    even_x, even_y = lax.rem(at_x, 2) == 0, lax.rem(at_y, 2) == 0
+    even_x = lax.rem(at_x, 2) == 0
     has_low_x, has_high_x = at_x > 0, at_x < size_x - 1
     has_low_y, has_high_y = at_y > 0, at_y < size_y - 1
 
@@ -258,15 +261,15 @@
             jnp.where(has_high_x, jnp.where(even_x, a, b), 0.0),
         )
 
-    def radial_halo(lo, n, refs=(beside_even, beside_odd)):
+    def radial_halo(lo, n, refs=(beside_one, beside_two)):
         a, b = (ref[lo : lo + n, :] for ref in refs)
         return (
-            jnp.where(has_low_y, jnp.where(even_y, b, a), 0.0),
-            jnp.where(has_high_y, jnp.where(even_y, a, b), 0.0),
+            jnp.where(has_low_y, jnp.where(even_x, a, b), 0.0),
+            jnp.where(has_high_y, jnp.where(even_x, b, a), 0.0),
         )
 
     base = 2 * FIELDS * tile
-    corners = radial_halo(0, 3 * tile, (corner_even, corner_odd))
+    corners = radial_halo(0, 3 * tile, (corner_one, corner_two))
 
     def corner(side_y, side_x, f):
         at = side_x * tile + f if f < FLOW else 2 * tile + side_x
@@ -408,7 +411,7 @@
     rows = width_x * width_y
     slots, movers = parcels.shape[-1], leave_slots.shape[-1]
     assert depth == LANES == 2 * movers and width_x == width_y == 8
-    permute = lambda x, axis, odd: lax.ppermute(x, AXES, pairing(sizes, axis, odd))
+    permute = lambda x, pairs: lax.ppermute(x, AXES, pairs)
     species2 = species.reshape(SPECIES * rows, depth)
     velocity2 = velocity.reshape(VECTORS * rows, depth)
     diffusivity2 = diffusivity.reshape(rows, depth)
@@ -422,7 +425,7 @@
     fields = [species2, velocity2, diffusivity2]
     cells2 = cells.reshape(chunks, LANES)
     slots2 = leave_slots.reshape(4, movers)
-    axial_even, axial_odd, radial_even, radial_odd, kept = call(
+    axial_even, axial_odd, radial_one, radial_two, kept = call(
         functools.partial(pack_kernel, width_x, width_y),
         [f32(packet_rows, depth)] * 4 + [f32(chunks, LANES)],
         fields + [parcels2, cells2, slots2, leave_counts],
@@ -430,10 +433,10 @@
         scratch=[near(x) for x in fields + [parcels2, cells2, slots2]]
         + [pltpu.SMEM(leave_counts.shape, I32), pltpu.SemaphoreType.DMA((7,))],
     )
-    from_even = permute(axial_even, 0, False)
-    from_odd = permute(axial_odd, 0, True)
-    beside_even = permute(radial_even, 1, False)
-    beside_odd = permute(radial_odd, 1, True)
+    from_odd = permute(axial_odd, axial_swap(sizes, True))
+    from_even = permute(axial_even, axial_swap(sizes, False))
+    beside_one = permute(radial_one, radial_shift(sizes, True))
+    beside_two = permute(radial_two, radial_shift(sizes, False))
     counts, kept = lax.optimization_barrier((counts, kept))
     staying, source = call(
         functools.partial(parcel_kernel, width_x, width_y),
@@ -442,16 +445,16 @@
         10**9, "push_parcels", smem=(4,), far_outs=(0,),
         scratch=[near(f32(ROWS, slots)), pltpu.SemaphoreType.DMA],
     )
-    corner_even, corner_odd = call(
+    corner_one, corner_two = call(
         functools.partial(corner_kernel, width_x, width_y),
-        [f32(3 * width_y, depth)] * 2, [from_even, from_odd], 10**6, "take_corners",
-    )
-    corner_even = permute(corner_even, 1, False)
-    corner_odd = permute(corner_odd, 1, True)
+        [f32(3 * width_y, depth)] * 2, [from_odd, from_even], 10**6, "take_corners",
+    )
+    corner_two = permute(corner_two, radial_shift(sizes, False))
+    corner_one = permute(corner_one, radial_shift(sizes, True))
     species_out, velocity_out, arrivals = call(
         functools.partial(stencil_kernel, width_x, width_y),
         [f32(SPECIES * rows, depth), f32(VECTORS * rows, depth), f32(4, ROWS, movers)],
-        fields + [from_even, from_odd, beside_even, beside_odd, corner_even, corner_odd, source],
+        fields + [from_odd, from_even, beside_one, beside_two, corner_two, corner_one, source],
         10**7, "stencils", far_outs=(0, 1, 2),
         scratch=[near(f32(FLOW, rows, depth)), near(f32(4, ROWS, movers)), pltpu.SemaphoreType.DMA((FLOW + 1,))],
     )

time: 15 us -> 13.8 us (0.920)
  the two profiles are of different devices: /device:TPU:20 before, /device:TPU:3 now
where the time goes in v3:
time: 13.8 us; the launch traced here: 13.6 us
  Pallas kernels  4.65 us (34%)
  starting transfers between devices  4.63 us (34%)
  waiting for transfers between devices  2.92 us (21%)
  between operations  1.38 us (10%)
    pallas_call x4, Pallas kernels, call(): pl.pallas_call(kernel, out_shape=[jax.ShapeDtypeStruct(s.shape, s.dtype)...  4.65 us
    ppermute x6, starting transfers between devices, body(): permute = lambda x, pairs: lax.ppermute(x, AXES, pairs)  4.63 us
    ppermute x6, waiting for transfers between devices, body(): permute = lambda x, pairs: lax.ppermute(x, AXES, pairs)  2.92 us
  transfers between devices with their start and end apart: 6, of which 2 were waited for; matrix products, arithmetic and copies ran while one was open for 0% of the time, Pallas kernels for 9%

profile of v3, /device:TPU:3, one launch (start us, length us, event | category | flops | bytes accessed | tf_op | source)
XLA Modules:
  0.0 13.6 jit_solution(52230159542928631)
XLA Ops:
  0.6 0.0 copy-start.2
  0.6 1.7 %pack_faces.1 = (f32[160,128]{1,0:T(8,128)S(1)}, f32[160,128]{1,0:T(8,128)S(1)}, f32[160,128]{1,0:T(8,128)S(1)}, f32[160,128]{1,0:T(8,128)S(1)}, f32[16,128]{1,0:T(8,128)S(1)}) custom-call(f32[320,128]{1,0:T(8,128)} %bitcast.10, f32[192,128]{1,0:T(8,128)} %bitcast.12, f32[64,128]{1,0:T(8,128)} %bitcast.17, f32[16,2048]{1,0:T(8,128)} %bitcast.15, ...), custom_call_target="tpu_custom_call" | custom-call | flops 100000000 | bytes 771088 | tf_op jit(solution)/shard_map/pack_faces/pallas_call | solution.py:393
  2.4 0.0 copy-start.1
  2.4 1.8 %collective-permute-start = (f32[160,128]{1,0:T(8,128)S(1)}, f32[160,128]{1,0:T(8,128)S(1)}, u32[]{:S(2)}, u32[]{:S(2)}) collective-permute-start(f32[160,128]{1,0:T(8,128)S(1)} %get-tuple-element.18), channel_id=1, source_target_pairs={{0,1},{1,0},{2,3},{3,2},{4,8},{5,9},{6,10},{7,11},{8,4},{9,5},{10,... | collective-permute-start | bytes 245768 | tf_op jit(solution)/shard_map/ppermute | solution.py:414
  4.2 0.0 collective-permute-start.1
  4.2 0.5 %collective-permute-start.2 = (f32[160,128]{1,0:T(8,128)S(1)}, f32[160,128]{1,0:T(8,128)S(1)}, u32[]{:S(2)}, u32[]{:S(2)}) collective-permute-start(f32[160,128]{1,0:T(8,128)S(1)} %get-tuple-element.20), channel_id=1, source_target_pairs={{0,1},{1,2},{2,3},{3,7},{4,0},{5,4},{6,5},{7,6},{8,9},{9,10},{10,1... | collective-permute-start | bytes 245768 | tf_op jit(solution)/shard_map/ppermute | solution.py:414
  4.7 1.0 %collective-permute-start.3 = (f32[160,128]{1,0:T(8,128)S(1)}, f32[160,128]{1,0:T(8,128)S(1)}, u32[]{:S(2)}, u32[]{:S(2)}) collective-permute-start(f32[160,128]{1,0:T(8,128)S(1)} %get-tuple-element.21), channel_id=1, source_target_pairs={{0,4},{1,0},{2,1},{3,2},{4,5},{5,6},{6,7},{7,3},{8,12},{9,8},{10,9... | collective-permute-start | bytes 245768 | tf_op jit(solution)/shard_map/ppermute | solution.py:414
  6.3 0.0 copy-start.4
  6.4 1.7 %collective-permute-done.from_odd = f32[160,128]{1,0:T(8,128)S(1)} collective-permute-done((f32[160,128]{1,0:T(8,128)S(1)}, f32[160,128]{1,0:T(8,128)S(1)}, u32[]{:S(2)}, u32[]{:S(2)}) %collective-permute-start) | collective-permute-done | bytes 81952 | tf_op jit(solution)/shard_map/ppermute | solution.py:414
  8.0 0.0 collective-permute-done.1.from_even
  8.1 1.3 %collective-permute-start.4 = (f32[24,128]{1,0:T(8,128)S(1)}, f32[24,128]{1,0:T(8,128)S(1)}, u32[]{:S(2)}, u32[]{:S(2)}) collective-permute-start(f32[24,128]{1,0:T(8,128)S(1)} %get-tuple-element.22), channel_id=1, source_target_pairs={{0,4},{1,0},{2,1},{3,2},{4,5},{5,6},{6,7},{7,3},{8,12},{9,8},{10,9... | collective-permute-start | bytes 36872 | tf_op jit(solution)/shard_map/ppermute | solution.py:414
  9.4 0.0 copy-start
  9.4 0.0 copy-start.3
  9.4 0.0 collective-permute-start.5
  9.4 0.0 copy-done.2
  9.4 0.0 copy-done.1
  9.4 0.0 copy-done.4
  9.4 1.3 %push_parcels.1 = (f32[16,2048]{1,0:T(8,128)}, f32[256,128]{1,0:T(8,128)S(1)}) custom-call(f32[192,128]{1,0:T(8,128)S(1)} %bitcast.13, f32[16,2048]{1,0:T(8,128)S(1)} %bitcast.16, s32[1,1,2048]{2,1,0:T(1,128)S(1)} %copy-done.4, f32[16,128]{1,0:T(8,128)S(1)} %get-tuple-element.25.kept, s32[1,1]{1,0:T(1,128)S(6)} %copy.12.counts), custom_call_target="tpu_custom_call" | custom-call | flops 1000000000 | bytes 507908 | tf_op jit(solution)/shard_map/push_parcels/pallas_call | solution.py:393
  10.7 0.0 collective-permute-done.2.beside_one
  10.7 0.0 collective-permute-done.3.beside_two
  10.7 0.0 collective-permute-done.4.corner_two
  10.7 1.2 %collective-permute-done.5.corner_one = f32[24,128]{1,0:T(8,128)S(1)} collective-permute-done((f32[24,128]{1,0:T(8,128)S(1)}, f32[24,128]{1,0:T(8,128)S(1)}, u32[]{:S(2)}, u32[]{:S(2)}) %collective-permute-start.5) | collective-permute-done | bytes 12320 | tf_op jit(solution)/shard_map/ppermute | solution.py:414
  11.9 0.0 copy-done
  11.9 0.0 copy-done.3
  11.9 1.6 %stencils.1 = (f32[320,128]{1,0:T(8,128)}, f32[192,128]{1,0:T(8,128)}, f32[4,16,64]{2,1,0:T(8,128)}) custom-call(f32[320,128]{1,0:T(8,128)S(1)} %bitcast.11, f32[192,128]{1,0:T(8,128)S(1)} %bitcast.14, f32[64,128]{1,0:T(8,128)S(1)} %bitcast.18, f32[160,128]{1,0:T(8,128)S(1)} %collective-permute-done.from_odd, ...), custom_call_target="tpu_custom_call" | custom-call | flops 10000000 | bytes 1056768 | tf_op jit(solution)/shard_map/stencils/pallas_call | solution.py:393
  (1 shorter events, 0.0 us)
Async XLA Ops:
  0.6 8.8 %copy-start.2 = (f32[1,1,16,2048]{3,2,1,0:T(8,128)S(1)}, f32[1,1,16,2048]{3,2,1,0:T(8,128)}, u32[]{:S(2)}) copy-start(f32[1,1,16,2048]{3,2,1,0:T(8,128)} %param.11) | copy-start | bytes 393220
  2.4 7.0 %copy-start.1 = (f32[3,8,8,128]{3,2,1,0:T(8,128)S(1)}, f32[3,8,8,128]{3,2,1,0:T(8,128)}, u32[]{:S(2)}) copy-start(f32[3,8,8,128]{3,2,1,0:T(8,128)} %param.9) | copy-start | bytes 294916
  2.4 5.7 %collective-permute-start = (f32[160,128]{1,0:T(8,128)S(1)}, f32[160,128]{1,0:T(8,128)S(1)}, u32[]{:S(2)}, u32[]{:S(2)}) collective-permute-start(f32[160,128]{1,0:T(8,128)S(1)} %get-tuple-element.18), channel_id=1, source_target_pairs={{0,1},{1,0},{2,3},{3,2},{4,8},{5,9},{6,10},{7,11},{8,4},{9,5},{10,... | collective-permute-start | bytes 245768 | tf_op jit(solution)/shard_map/ppermute | solution.py:414
  4.2 3.8 %collective-permute-start.1 = (f32[160,128]{1,0:T(8,128)S(1)}, f32[160,128]{1,0:T(8,128)S(1)}, u32[]{:S(2)}, u32[]{:S(2)}) collective-permute-start(f32[160,128]{1,0:T(8,128)S(1)} %get-tuple-element.19), channel_id=1, source_target_pairs={{0,4},{1,5},{2,6},{3,7},{4,0},{5,1},{6,2},{7,3},{8,12},{9,13},{10,... | collective-permute-start | bytes 245768 | tf_op jit(solution)/shard_map/ppermute | solution.py:414
  4.2 6.5 %collective-permute-start.2 = (f32[160,128]{1,0:T(8,128)S(1)}, f32[160,128]{1,0:T(8,128)S(1)}, u32[]{:S(2)}, u32[]{:S(2)}) collective-permute-start(f32[160,128]{1,0:T(8,128)S(1)} %get-tuple-element.20), channel_id=1, source_target_pairs={{0,1},{1,2},{2,3},{3,7},{4,0},{5,4},{6,5},{7,6},{8,9},{9,10},{10,1... | collective-permute-start | bytes 245768 | tf_op jit(solution)/shard_map/ppermute | solution.py:414
  4.7 6.0 %collective-permute-start.3 = (f32[160,128]{1,0:T(8,128)S(1)}, f32[160,128]{1,0:T(8,128)S(1)}, u32[]{:S(2)}, u32[]{:S(2)}) collective-permute-start(f32[160,128]{1,0:T(8,128)S(1)} %get-tuple-element.21), channel_id=1, source_target_pairs={{0,4},{1,0},{2,1},{3,2},{4,5},{5,6},{6,7},{7,3},{8,12},{9,8},{10,9... | collective-permute-start | bytes 245768 | tf_op jit(solution)/shard_map/ppermute | solution.py:414
  6.3 3.1 %copy-start.4 = (s32[1,1,2048]{2,1,0:T(1,128)S(1)}, s32[1,1,2048]{2,1,0:T(1,128)}, u32[]{:S(2)}) copy-start(s32[1,1,2048]{2,1,0:T(1,128)} %cells.1) | copy-start | bytes 24580
  8.1 2.6 %collective-permute-start.4 = (f32[24,128]{1,0:T(8,128)S(1)}, f32[24,128]{1,0:T(8,128)S(1)}, u32[]{:S(2)}, u32[]{:S(2)}) collective-permute-start(f32[24,128]{1,0:T(8,128)S(1)} %get-tuple-element.22), channel_id=1, source_target_pairs={{0,4},{1,0},{2,1},{3,2},{4,5},{5,6},{6,7},{7,3},{8,12},{9,8},{10,9... | collective-permute-start | bytes 36872 | tf_op jit(solution)/shard_map/ppermute | solution.py:414
  9.4 2.6 %copy-start = (f32[5,8,8,128]{3,2,1,0:T(8,128)S(1)}, f32[5,8,8,128]{3,2,1,0:T(8,128)}, u32[]{:S(2)}) copy-start(f32[5,8,8,128]{3,2,1,0:T(8,128)} %param.8) | copy-start | bytes 491524
  9.4 2.6 %copy-start.3 = (f32[8,8,128]{2,1,0:T(8,128)S(1)}, f32[8,8,128]{2,1,0:T(8,128)}, u32[]{:S(2)}) copy-start(f32[8,8,128]{2,1,0:T(8,128)} %param.10) | copy-start | bytes 98308
  9.4 2.5 %collective-permute-start.5 = (f32[24,128]{1,0:T(8,128)S(1)}, f32[24,128]{1,0:T(8,128)S(1)}, u32[]{:S(2)}, u32[]{:S(2)}) collective-permute-start(f32[24,128]{1,0:T(8,128)S(1)} %get-tuple-element.23), channel_id=1, source_target_pairs={{0,1},{1,2},{2,3},{3,7},{4,0},{5,4},{6,5},{7,6},{8,9},{9,10},{10,1... | collective-permute-start | bytes 36872 | tf_op jit(solution)/shard_map/ppermute | solution.py:414

commit v4 on v3

v4 whole, which is shorter than its diff:
```python
import functools

import jax
import jax.numpy as jnp
import numpy as np
from jax import lax
from jax.experimental import pallas as pl
from jax.experimental.pallas import tpu as pltpu
from jax.sharding import PartitionSpec as P

time_step = 0.1
AXES = ("axial", "radial")
LARGEST = float(jnp.finfo(jnp.bfloat16).max)
F32, BF16, I32 = jnp.float32, jnp.bfloat16, jnp.int32
SPECIES, VECTORS = 5, 3
FLOW = SPECIES + VECTORS
FIELDS = FLOW + 1
ROWS = 16
LANES = 128
VMEM_LIMIT = 16 * 1024 * 1024


def complete(sizes, target):
    flat = lambda at: at[0] * sizes[1] + at[1]
    blocks = [(i, j) for i in range(sizes[0]) for j in range(sizes[1])]
    pairs = [(flat(at), flat(target(*at))) for at in blocks]
    assert sorted(t for _, t in pairs) == list(range(len(blocks))) and all(s != t for s, t in pairs)
    return pairs


def axial_swap(sizes, odd):
    def target(a, r):
        other = a + 1 if (a % 2 == 1) == odd else a - 1
        return (other, r) if 0 <= other < sizes[0] else (a, r ^ 1)

    return complete(sizes, target)


def radial_shift(sizes, even_up):
    def target(a, r):
        other = r + 1 if (a % 2 == 0) == even_up else r - 1
        return (a, other) if 0 <= other < sizes[1] else (a ^ 1, r)

    return complete(sizes, target)


def split(x):
    high = jnp.clip(x, -LARGEST, LARGEST).astype(BF16)
    return high, (x - high.astype(F32)).astype(BF16)


def one_hot(index, depth):
    rows = lax.broadcasted_iota(I32, (depth, index.shape[1]), 0)
    return (rows == index).astype(F32).astype(BF16)


def pick(table, index):
    rows = lax.broadcasted_iota(I32, table.shape, 0)
    return jnp.sum(jnp.where(rows == index, table, 0.0), axis=0, keepdims=True)


def dot(a, b):
    return jnp.dot(a, b, preferred_element_type=F32)


def dot_t(a, b):
    return lax.dot_general(a, b, (((1,), (1,)), ((), ())), preferred_element_type=F32)


def pack_kernel(
    width_x, width_y, species_in, velocity_in, diffusivity_in, parcels_in, cells_in, slots_in, face_counts_in,
    axial_even, axial_odd, radial_one, radial_two, kept,
    species, velocity, diffusivity, parcels, cells, slots, face_counts, arrived,
):
    copies = [
        pltpu.make_async_copy(src, dst, arrived.at[i])
        for i, (src, dst) in enumerate(
            (
                (slots_in, slots), (face_counts_in, face_counts), (cells_in, cells),
                (parcels_in, parcels), (velocity_in, velocity), (species_in, species),
                (diffusivity_in, diffusivity),
            )
        )
    ]
    for copy in copies:
        copy.start()
    for copy in copies[:4]:
        copy.wait()
    cells_of, tile = width_x * width_y, width_y
    movers = slots.shape[1]
    lane = lax.broadcasted_iota(I32, (1, 2 * movers), 1)
    pairs = [jnp.concatenate([slots[i : i + 1, :], slots[i + 1 : i + 2, :]], axis=1) for i in (0, 2)]
    valid = [
        lane < jnp.where(lane < movers, face_counts[0, 0, i], movers + face_counts[0, 0, i + 1]) for i in (0, 2)
    ]
    slot = jnp.concatenate(pairs, axis=1)
    valid = jnp.concatenate([v.astype(F32) for v in valid], axis=1)
    chunk, place = lax.shift_right_logical(slot, 7), lax.bitwise_and(slot, LANES - 1)
    chunks = parcels.shape[1] // LANES
    hot_place = one_hot(place, LANES)
    hot_chunk = lax.broadcasted_iota(I32, (chunks, slot.shape[1]), 0) == chunk
    leaving = dot_t(jnp.where(hot_chunk, valid, 0.0).astype(BF16), hot_place)
    kept[...] = jnp.where(leaving > 0.5, 0.0, 1.0)
    stacked = jnp.concatenate([parcels[:, h * LANES : (h + 1) * LANES] for h in range(chunks)], axis=0)
    cell = cells[...]
    cell_high = lax.shift_right_logical(cell, 7).astype(F32)
    cell_low = lax.bitwise_and(cell, LANES - 1).astype(F32)
    first, second = split(stacked)
    left = jnp.concatenate([first, cell_high.astype(BF16), cell_low.astype(BF16)], axis=0)
    right = jnp.concatenate([second, jnp.zeros((2 * chunks, LANES), BF16)], axis=0)
    table = dot(jnp.concatenate([left, right], axis=1), jnp.concatenate([hot_place, hot_place], axis=0))
    rows = jnp.zeros((ROWS, slot.shape[1]), F32)
    for h in range(chunks):
        rows = rows + jnp.where(chunk == h, table[h * ROWS : (h + 1) * ROWS], 0.0)
    row_of = jnp.sum(
        jnp.where(hot_chunk, table[chunks * ROWS : chunks * ROWS + chunks], 0.0), axis=0, keepdims=True
    ).astype(I32)
    lane_of = jnp.sum(
        jnp.where(hot_chunk, table[chunks * ROWS + chunks :], 0.0), axis=0, keepdims=True
    ).astype(I32)
    copies[4].wait()
    gas = gas_at(velocity[...], row_of, one_hot(lane_of, LANES), cells_of)
    response, evaporation = rows[4:5], rows[5:6]
    pushed = [rows[i : i + 1] + time_step * (response * (gas[i] - rows[i : i + 1])) for i in range(3)]
    pushed.append(rows[3:4] * (1.0 - time_step * evaporation))
    pushed.extend([response, evaporation])
    pushed.extend(rows[6 + i : 7 + i] + time_step * pushed[i] for i in range(3))
    base = 2 * FIELDS * tile
    for packets, lo in (((axial_even, axial_odd), 0), ((radial_one, radial_two), 2 * movers)):
        for ref in packets:
            part = slice(lo, lo + 2 * movers)
            for i, row in enumerate(pushed):
                ref[base + i : base + i + 1, :] = row[:, part] * valid[:, part]
            ref[base + 9 : base + ROWS, :] = rows[9:ROWS, part] * valid[:, part]

    for copy in copies[5:]:
        copy.wait()
    even_x = lax.rem(lax.axis_index("axial"), 2) == 0
    for f in range(FIELDS):
        ref, base = (
            (species, f) if f < SPECIES else (velocity, f - SPECIES) if f < FLOW else (diffusivity, 0)
        )
        for layer in range(2):
            at = pl.ds((2 * f + layer) * tile, tile)
            low = ref[pl.ds(base * cells_of + layer * width_y, width_y), :]
            high = ref[pl.ds(base * cells_of + (width_x - 2 + layer) * width_y, width_y), :]
            axial_even[at, :] = jnp.where(even_x, high, low)
            axial_odd[at, :] = jnp.where(even_x, low, high)
            low = ref[pl.ds(base * cells_of + layer, width_x, stride=width_y), :]
            high = ref[pl.ds(base * cells_of + width_y - 2 + layer, width_x, stride=width_y), :]
            radial_one[at, :] = jnp.where(even_x, high, low)
            radial_two[at, :] = jnp.where(even_x, low, high)


def gas_at(velocity, row_of, hot_lane, rows):
    high, low = split(velocity)
    table = dot(
        jnp.concatenate([high, low], axis=1), jnp.concatenate([hot_lane, hot_lane], axis=0)
    )
    return [pick(table[i * rows : (i + 1) * rows], row_of) for i in range(VECTORS)]


def parcel_kernel(width_x, width_y, velocity, parcels, cells, kept, counts, staying, source):
    rows = width_x * width_y
    half, wide = rows // 2, 2 * LANES
    slots = parcels.shape[1]
    cell = cells[0]
    row_of, lane_of = lax.shift_right_logical(cell, 8), lax.bitwise_and(cell, wide - 1)
    hot_lane = one_hot(lane_of, wide)
    pairs = jnp.concatenate([velocity[pl.ds(i, VECTORS * half, stride=2), :] for i in range(2)], axis=1)
    table = dot(jnp.concatenate(split(pairs), axis=0), hot_lane)
    table = table[: VECTORS * half] + table[VECTORS * half :]
    gas = [pick(table[i * half : (i + 1) * half], row_of) for i in range(VECTORS)]
    chunks = slots // LANES
    live = (lax.broadcasted_iota(I32, (1, slots), 1) < counts[...]).astype(F32)
    keep = jnp.concatenate([kept[h : h + 1, :] for h in range(chunks)], axis=1) * live
    mass, response, evaporation = parcels[3:4], parcels[4:5], parcels[5:6]
    drag = [response * (gas[i] - parcels[i : i + 1]) for i in range(3)]
    for i in range(3):
        moved = parcels[i : i + 1] + time_step * drag[i]
        staying[i : i + 1, :] = moved * keep
        staying[6 + i : 7 + i, :] = (parcels[6 + i : 7 + i] + time_step * moved) * keep
    staying[3:4, :] = mass * (1.0 - time_step * evaporation) * keep
    staying[4:6, :] = parcels[4:6] * keep
    staying[9:ROWS, :] = parcels[9:ROWS] * keep
    deposits = [mass * evaporation] + [-mass * d for d in drag]
    hot_row = one_hot(row_of, half)
    halves = [split(d * live) for d in deposits]
    left = jnp.concatenate([hot_row * part[i] for i in range(2) for part in halves], axis=0)
    total = dot_t(left, hot_lane)
    total = total[: 4 * half] + total[4 * half :]
    for i in range(2):
        source[pl.ds(i, 4 * half, stride=2), :] = total[:, i * LANES : (i + 1) * LANES]


def corner_kernel(width_x, width_y, from_odd, from_even, radial_one, radial_two):
    tile = width_y
    even_x = lax.rem(lax.axis_index("axial"), 2) == 0
    at_x, size_x = lax.axis_index("axial"), lax.axis_size("axial")
    has = [at_x > 0, at_x < size_x - 1]
    for ref in (radial_one, radial_two):
        ref[2 * tile : 3 * tile, :] = jnp.zeros((tile, LANES), F32)
    for side in range(2):
        layer = 1 - side
        lower_is_odd = even_x if side == 0 else jnp.logical_not(even_x)
        choose = lambda v: jnp.where(has[side], jnp.where(lower_is_odd, v[1], v[0]), 0.0)
        flow, base_rate = [], []
        for y in (0, width_y - 1):
            flow.append(
                choose([r[pl.ds(layer * tile + y, FLOW, stride=2 * tile), :] for r in (from_even, from_odd)])
            )
            base_rate.append(
                choose([r[pl.ds((2 * FLOW + layer) * tile + y, 1), :] for r in (from_even, from_odd)])
            )
        for ref, high in ((radial_one, even_x), (radial_two, jnp.logical_not(even_x))):
            ref[side * tile : side * tile + FLOW, :] = jnp.where(high, flow[1], flow[0])
            ref[2 * tile + side : 2 * tile + side + 1, :] = jnp.where(high, base_rate[1], base_rate[0])


def coefficient(vel_first, vel_second, vel_third, base_rate):
    kinetic = vel_first * vel_first + vel_second * vel_second + vel_third * vel_third
    return base_rate * (1.0 + 0.5 * jnp.tanh(0.5 * kinetic))


def stencil_kernel(
    width_x, width_y, species, velocity, diffusivity, from_odd, from_even, beside_two, beside_one, source, staying,
    staying_out, arrivals_out, state, result, arrivals, sent,
):
    copies = [pltpu.make_async_copy(staying, staying_out, sent.at[0])]
    copies[0].start()
    tile = width_y
    rows = width_x * width_y
    depth = LANES
    at_x, size_x = lax.axis_index("axial"), lax.axis_size("axial")
    at_y, size_y = lax.axis_index("radial"), lax.axis_size("radial")
    even_x = lax.rem(at_x, 2) == 0
    has_x, has_y = [at_x > 0, at_x < size_x - 1], [at_y > 0, at_y < size_y - 1]
    row = lax.broadcasted_iota(I32, (1, tile, depth), 1)
    lane = lax.broadcasted_iota(I32, (1, tile, depth), 2)
    ends_of = [row == 0, row == tile - 1]
    edge = [lane == 0, lane == depth - 1]

    def keep(part, index, value):
        state[part, index * tile : (index + 1) * tile, :] = value

    def lines(part, index):
        base = index * tile
        return [state[part, base + i : base + i + 1, :].reshape(1, 1, depth) for i in range(tile)]

    def axial_halo(lo, n):
        a, b = from_even[lo : lo + n, :], from_odd[lo : lo + n, :]
        return (
            jnp.where(has_x[0], jnp.where(even_x, b, a), 0.0),
            jnp.where(has_x[1], jnp.where(even_x, a, b), 0.0),
        )

    def radial_halo(lo, n):
        a, b = beside_one[lo : lo + n, :], beside_two[lo : lo + n, :]
        return (
            jnp.where(has_y[0], jnp.where(even_x, a, b), 0.0),
            jnp.where(has_y[1], jnp.where(even_x, b, a), 0.0),
        )

    movers = arrivals.shape[-1]
    base = 2 * FIELDS * tile
    for side, (low, high) in ((0, axial_halo(base, ROWS)), (2, radial_halo(base, ROWS))):
        arrivals[side] = low[:, :movers]
        arrivals[side + 1] = high[:, movers : 2 * movers]
    copies.append(pltpu.make_async_copy(arrivals, arrivals_out, sent.at[1]))
    copies[-1].start()

    def up_down(x, axis):
        size = x.shape[axis]
        return pltpu.roll(x, 1, axis), pltpu.roll(x, size - 1, axis)

    def with_rows(x, low, high):
        below, above = up_down(x, 1)
        return jnp.where(ends_of[0], low, below), jnp.where(ends_of[1], high, above)

    def z_weights(d, scale):
        below, above = up_down(d, 2)
        low = scale * (d + jnp.where(edge[0], 0.0, below))
        high = scale * (d + jnp.where(edge[1], 0.0, above))
        return low, high

    def weights_of(scale, along, second, third):
        total = along[0] + along[1] + second[0] + second[1] + third[0] + third[1]
        inside = jnp.where(edge[0], 0.0, third[0]), jnp.where(edge[1], 0.0, third[1])
        return [scale * (1.0 - total), *along, *second, *inside]

    def weigh(weights, x, along, second):
        below, above = up_down(x, 2)
        total = weights[0] * x
        for w, v in zip(weights[1:], (*along, *second, below, above)):
            total = total + w * v
        return total

    long, sides = [], []
    for f in range(FIELDS):
        ref, at = (species, f) if f < SPECIES else (velocity, f - SPECIES) if f < FLOW else (diffusivity, 0)
        low, high = (h.reshape(2, tile, depth) for h in axial_halo(2 * f * tile, 2 * tile))
        main = ref[at * rows : (at + 1) * rows, :].reshape(width_x, tile, depth)
        long.append(jnp.concatenate([low, main, high], axis=0))
        low, high = (h.reshape(2, tile, depth) for h in radial_halo(2 * f * tile, 2 * tile))
        edges = [ref[pl.ds(at * rows + y, width_x, stride=width_y), :][None] for y in (0, width_y - 1)]
        near = jnp.concatenate([low[1:], high[:1]], axis=0)
        below = jnp.concatenate([low[:1], edges[1]], axis=0)
        above = jnp.concatenate([edges[0], high[1:]], axis=0)
        sides.append((near, below, above))
        for s in range(2):
            if f < FLOW:
                keep(0, 2 * f + s, long[f][(1, -2)[s]])
                keep(1, 2 * f + s, near[s])

    def beyond(part, index):
        low, high = (lines(part, 2 * index + s) for s in range(2))
        return [jnp.concatenate(v[:1] + v + v[-1:], axis=0) for v in (low, high)]

    half = 0.5 * time_step
    d = coefficient(long[5], long[6], long[7], long[8])
    d_near, d_below, d_above = (coefficient(*(sides[i][j] for i in (5, 6, 7, 8))) for j in range(3))
    for s in range(2):
        end = (1, -2)[s]
        for i, value in enumerate((d[end], d_near[s], long[8][end], sides[8][0][s])):
            keep(i, 2 * FLOW + s, value)
    ones = jnp.ones((width_x, 1, 1), F32)
    border = lambda low, high: jnp.concatenate([low, ones, high], axis=0)
    flag = lambda c: jnp.where(c, jnp.ones((1, 1, 1), F32), 0.0)
    exists = border(flag(has_x[0]), flag(has_x[1]))
    not_beside = jnp.concatenate([jnp.zeros((1, 1, 1), F32), ones, jnp.zeros((1, 1, 1), F32)], axis=0)
    inner = d[1:-1]
    along = half * (d[1:] + d[:-1])
    low, high = with_rows(inner, *beyond(1, FLOW))
    beside = [jnp.where(e, not_beside, 1.0) for e in ends_of]
    second = half * (inner + low) * beside[0], half * (inner + high) * beside[1]
    main_weights = weights_of(1.0, (along[:-1], along[1:]), second, z_weights(inner, half))
    main_weights = [
        jnp.concatenate([w[:1] * exists[:1], w[1:-1], w[-1:] * exists[-1:]], axis=0) for w in main_weights
    ]
    below, above = up_down(d_near, 1)
    side_exists = jnp.concatenate([flag(has_y[0]), flag(has_y[1])], axis=0)
    side_weights = weights_of(
        1.0,
        (
            jnp.where(ends_of[0], 0.0, half * (d_near + below)),
            jnp.where(ends_of[1], 0.0, half * (d_near + above)),
        ),
        (half * (d_near + d_below), half * (d_near + d_above)),
        z_weights(d_near, half),
    )
    side_weights = [w * side_exists for w in side_weights]

    first = []
    for f in range(FLOW):
        x = long[f][1:-1]
        first.append(weigh(main_weights, x, (long[f][:-2], long[f][2:]), with_rows(x, *beyond(1, f))))
        near, below, above = sides[f]
        moved = weigh(side_weights, near, up_down(near, 1), (below, above))
        if f >= SPECIES:
            sides[f] = moved
        for s in range(2):
            keep(2, 2 * f + s, first[f][(0, -1)[s]])
            keep(3, 2 * f + s, moved[s])
            keep(4, 2 * f + s, first[f][(1, -2)[s]])

    later = coefficient(first[5], first[6], first[7], long[8][1:-1])
    later_side = coefficient(sides[5], sides[6], sides[7], sides[8][0])
    for s in range(2):
        keep(3, 2 * FLOW + s, sides[8][0][s])
        keep(4, 2 * FLOW + s, later[(1, -2)[s]])
    for s in range(2):
        keep(5, s, later_side[s])

    scale = 0.5
    half = 0.5 * half
    inner = later[1:-1]
    along = half * (later[1:] + later[:-1])
    free = jnp.where(ends_of[0] | ends_of[1], 0.0, 1.0)
    along_low = jnp.concatenate([along[:1] * free, along[1:-1]], axis=0)
    along_high = jnp.concatenate([along[1:-1], along[-1:] * free], axis=0)
    low, high = (jnp.concatenate(lines(5, s), axis=0) for s in range(2))
    low, high = with_rows(inner, low, high)
    inside = jnp.concatenate([jnp.zeros((1, 1, 1), F32), ones[2:], jnp.zeros((1, 1, 1), F32)], axis=0)
    beside = [jnp.where(e, inside, 1.0) for e in ends_of]
    second = half * (inner + low) * beside[0], half * (inner + high) * beside[1]
    third = z_weights(inner, half)
    total = along_low + along_high + second[0] + second[1] + third[0] + third[1]
    weights = [
        scale - total, along_low, along_high, *second,
        jnp.where(edge[0], 0.0, third[0]), jnp.where(edge[1], 0.0, third[1]),
    ]
    for f in range(FLOW):
        x = first[f][1:-1]
        low, high = (jnp.concatenate(lines(3, 2 * f + s), axis=0) for s in range(2))
        value = weigh(weights, x, (first[f][:-2], first[f][2:]), with_rows(x, low, high))
        value = (value + scale * long[f][2:-2]).reshape(rows, depth)
        part = 0 if f == 0 else f - SPECIES + 1 if f >= SPECIES else None
        if part is not None:
            value = value + time_step * source[part * rows : (part + 1) * rows, :]
        result[f] = value
    for copy in copies:
        copy.wait()


def end_kernel(width_x, width_y, corner_two, corner_one, state, result, species_out, velocity_out, ends, sent):
    tile = width_y
    rows = width_x * width_y
    at_x, size_x = lax.axis_index("axial"), lax.axis_size("axial")
    at_y, size_y = lax.axis_index("radial"), lax.axis_size("radial")
    even_x = lax.rem(at_x, 2) == 0
    has_x, has_y = [at_x > 0, at_x < size_x - 1], [at_y > 0, at_y < size_y - 1]
    middle = pl.ds(tile, rows - 2 * tile)
    last = rows - tile
    copies = [
        pltpu.make_async_copy(
            result.at[pl.ds(0, SPECIES), middle, :], species_out.at[:, middle, :], sent.at[0]
        ),
        pltpu.make_async_copy(
            result.at[pl.ds(SPECIES, VECTORS), middle, :], velocity_out.at[:, middle, :], sent.at[1]
        ),
    ]
    for copy in copies:
        copy.start()
    for f in range(FLOW):
        ends[0, f * tile : (f + 1) * tile, :] = result[f, :tile, :]
        ends[1, f * tile : (f + 1) * tile, :] = result[f, last:, :]

    def fields_at(part, side, place):
        return state[part, pl.ds(side * tile + place, FLOW, stride=2 * tile), :]

    def one_at(part, side, place):
        at = (2 * FLOW + side) * tile + place
        return state[part, at : at + 1, :]

    def of(values, base_rate):
        return coefficient(values[5:6], values[6:7], values[7:8], base_rate)

    for side_y, y in ((0, 0), (1, width_y - 1)):
        a, b = corner_one[...], corner_two[...]
        corners = jnp.where(has_y[side_y], jnp.where(even_x, *((a, b) if side_y == 0 else (b, a))), 0.0)
        for side_x, x in ((0, 0), (1, width_x - 1)):
            flow = corners[side_x * tile : side_x * tile + FLOW]
            rate = of(flow, corners[2 * tile + side_x : 2 * tile + side_x + 1])
            here, later = fields_at(4, side_x, y), one_at(4, side_x, y)
            total = None
            for part, side, place, has in ((0, side_x, y, has_x[side_x]), (1, side_y, x, has_y[side_y])):
                flux = (one_at(part, side, place) + rate) * (flow - fields_at(part, side, place))
                moved = jnp.where(has, fields_at(part + 2, side, place) + 0.5 * time_step * flux, 0.0)
                term = (later + of(moved, one_at(part + 2, side, place))) * (moved - here)
                total = term if total is None else total + term
            at = pl.ds(y, FLOW, stride=tile)
            ends[side_x, at, :] = ends[side_x, at, :] + 0.25 * time_step * total
    for f in range(FLOW):
        ref, at = (species_out, f) if f < SPECIES else (velocity_out, f - SPECIES)
        for side, x in ((0, 0), (1, last)):
            copies.append(
                pltpu.make_async_copy(
                    ends.at[side, pl.ds(f * tile, tile), :], ref.at[at, pl.ds(x, tile), :],
                    sent.at[2 + 2 * f + side],
                )
            )
            copies[-1].start()
    for copy in copies:
        copy.wait()


def call(kernel, outs, ins, flops, name, scratch=(), far_ins=(), far_outs=()):
    vmem, far = (pl.BlockSpec(memory_space=m) for m in (pltpu.VMEM, pltpu.HBM))
    moved = sum(int(np.prod(x.shape)) * 4 for x in list(ins) + list(outs))
    ins = [pltpu.with_memory_space_constraint(x, pltpu.HBM) if i in far_ins else x for i, x in enumerate(ins)]
    return pl.pallas_call(
        kernel,
        out_shape=[jax.ShapeDtypeStruct(s.shape, s.dtype) for s in outs],
        in_specs=[far if i in far_ins else vmem for i in range(len(ins))],
        out_specs=[far if i in far_outs else vmem for i in range(len(outs))],
        scratch_shapes=list(scratch),
        compiler_params=pltpu.CompilerParams(vmem_limit_bytes=VMEM_LIMIT),
        cost_estimate=pl.CostEstimate(flops=flops, bytes_accessed=moved, transcendentals=0),
        name=name,
    )(*ins)


def f32(*shape):
    return jax.ShapeDtypeStruct(shape, F32)


def body(sizes, species, velocity, diffusivity, parcels, counts, cells, leave_slots, leave_counts):
    _, width_x, width_y, depth = species.shape
    rows = width_x * width_y
    slots, movers = parcels.shape[-1], leave_slots.shape[-1]
    assert depth == LANES == 2 * movers and width_x == width_y == 8
    permute = lambda x, pairs: lax.ppermute(x, AXES, pairs)
    species2 = species.reshape(SPECIES * rows, depth)
    velocity2 = velocity.reshape(VECTORS * rows, depth)
    diffusivity2 = diffusivity.reshape(rows, depth)
    parcels2 = parcels.reshape(ROWS, slots)
    packet_rows = 2 * FIELDS * width_y + ROWS
    chunks = slots // LANES

    def near(x):
        return pltpu.VMEM(x.shape, x.dtype)

    fields = [species2, velocity2, diffusivity2]
    cells2 = cells.reshape(chunks, LANES)
    slots2 = leave_slots.reshape(4, movers)
    axial_even, axial_odd, radial_one, radial_two, kept = call(
        functools.partial(pack_kernel, width_x, width_y),
        [f32(packet_rows, depth)] * 4 + [f32(chunks, LANES)],
        fields + [parcels2, cells2, slots2, leave_counts],
        10**8, "pack_faces", far_ins=range(7),
        scratch=[near(x) for x in fields + [parcels2, cells2, slots2]]
        + [pltpu.SMEM(leave_counts.shape, I32), pltpu.SemaphoreType.DMA((7,))],
    )
    from_odd = permute(axial_odd, axial_swap(sizes, True))
    from_even = permute(axial_even, axial_swap(sizes, False))
    beside_one = permute(radial_one, radial_shift(sizes, True))
    beside_two = permute(radial_two, radial_shift(sizes, False))
    counts, kept = lax.optimization_barrier((counts, kept))
    staying, source = call(
        functools.partial(parcel_kernel, width_x, width_y),
        [f32(ROWS, slots), f32(4 * rows, depth)],
        [velocity2, parcels2, cells.reshape(1, 1, slots), kept, counts],
        10**9, "push_parcels",
    )
    state = f32(6, 2 * (FLOW + 1) * width_y, depth)
    staying, arrivals, state, result = call(
        functools.partial(stencil_kernel, width_x, width_y),
        [f32(ROWS, slots), f32(4, ROWS, movers), state, f32(FLOW, rows, depth)],
        fields + [from_odd, from_even, beside_two, beside_one, source, staying],
        10**7, "stencils", far_outs=(0, 1),
        scratch=[near(f32(4, ROWS, movers)), pltpu.SemaphoreType.DMA((2,))],
    )
    corner_one, corner_two = call(
        functools.partial(corner_kernel, width_x, width_y),
        [f32(3 * width_y, depth)] * 2, [from_odd, from_even], 10**6, "take_corners",
    )
    corner_two = permute(corner_two, radial_shift(sizes, False))
    corner_one = permute(corner_one, radial_shift(sizes, True))
    species_out, velocity_out = call(
        functools.partial(end_kernel, width_x, width_y),
        [f32(SPECIES, rows, depth), f32(VECTORS, rows, depth)],
        [corner_two, corner_one, state, result],
        10**6, "ends", far_outs=(0, 1),
        scratch=[near(f32(2, FLOW * width_y, depth)), pltpu.SemaphoreType.DMA((2 + 2 * FLOW,))],
    )
    return (
        species_out.reshape(species.shape),
        velocity_out.reshape(velocity.shape),
        staying[None, None],
        arrivals[None, None],
    )


def solution(mesh):
    sizes = tuple(mesh.shape[axis] for axis in AXES)
    return jax.shard_map(
        functools.partial(body, sizes),
        mesh=mesh,
        in_specs=(
            P(None, "axial", "radial", None),
            P(None, "axial", "radial", None),
            P("axial", "radial", None),
            P("axial", "radial", None, None),
            P("axial", "radial"),
            P("axial", "radial", None),
            P("axial", "radial", None, None),
            P("axial", "radial", None),
        ),
        out_specs=(
            P(None, "axial", "radial", None),
            P(None, "axial", "radial", None),
            P("axial", "radial", None, None),
            P("axial", "radial", None, None, None),
        ),
        check_vma=False,
    )
```

time: 13.8 us -> 13 us (0.942)
  the two profiles are of different devices: /device:TPU:3 before, /device:TPU:0 now
where the time goes in v4:
time: 13 us; the launch traced here: 12.9 us
  starting transfers between devices  7.17 us (55%)
  Pallas kernels  4.24 us (33%)
  between operations  1.43 us (11%)
    ppermute x6, starting transfers between devices, body(): permute = lambda x, pairs: lax.ppermute(x, AXES, pairs)  7.17 us
    pallas_call x5, Pallas kernels, call(): pl.pallas_call(kernel, out_shape=[jax.ShapeDtypeStruct(s.shape, s.dtype)...  4.24 us
  transfers between devices with their start and end apart: 6, of which 0 were waited for; matrix products, arithmetic and copies ran while one was open for 0% of the time, Pallas kernels for 14%

profile of v4, /device:TPU:0, one launch (start us, length us, event | category | flops | bytes accessed | tf_op | source)
XLA Modules:
  0.0 12.9 jit_solution(9834001782104120658)
XLA Ops:
  0.6 0.0 copy-start.3
  0.6 1.6 %pack_faces.1 = (f32[160,128]{1,0:T(8,128)S(1)}, f32[160,128]{1,0:T(8,128)S(1)}, f32[160,128]{1,0:T(8,128)S(1)}, f32[160,128]{1,0:T(8,128)S(1)}, f32[16,128]{1,0:T(8,128)S(1)}) custom-call(f32[320,128]{1,0:T(8,128)} %bitcast.10, f32[192,128]{1,0:T(8,128)} %bitcast.12, f32[64,128]{1,0:T(8,128)} %bitcast.15, f32[16,2048]{1,0:T(8,128)} %bitcast.17, ...), custom_call_target="tpu_custom_call" | custom-call | flops 100000000 | bytes 771088 | tf_op jit(solution)/shard_map/pack_faces/pallas_call | solution.py:471
  2.3 0.0 copy-start.1
  2.3 3.1 %collective-permute-start = (f32[160,128]{1,0:T(8,128)S(1)}, f32[160,128]{1,0:T(8,128)S(1)}, u32[]{:S(2)}, u32[]{:S(2)}) collective-permute-start(f32[160,128]{1,0:T(8,128)S(1)} %get-tuple-element.21), channel_id=1, source_target_pairs={{0,1},{1,0},{2,3},{3,2},{4,8},{5,9},{6,10},{7,11},{8,4},{9,5},{10,... | collective-permute-start | bytes 245768 | tf_op jit(solution)/shard_map/ppermute | solution.py:492
  5.4 0.0 collective-permute-start.1
  5.4 0.5 %collective-permute-start.4 = (f32[160,128]{1,0:T(8,128)S(1)}, f32[160,128]{1,0:T(8,128)S(1)}, u32[]{:S(2)}, u32[]{:S(2)}) collective-permute-start(f32[160,128]{1,0:T(8,128)S(1)} %get-tuple-element.25), channel_id=1, source_target_pairs={{0,4},{1,0},{2,1},{3,2},{4,5},{5,6},{6,7},{7,3},{8,12},{9,8},{10,9... | collective-permute-start | bytes 245768 | tf_op jit(solution)/shard_map/ppermute | solution.py:492
  5.9 1.5 %collective-permute-start.5 = (f32[160,128]{1,0:T(8,128)S(1)}, f32[160,128]{1,0:T(8,128)S(1)}, u32[]{:S(2)}, u32[]{:S(2)}) collective-permute-start(f32[160,128]{1,0:T(8,128)S(1)} %get-tuple-element.26), channel_id=1, source_target_pairs={{0,1},{1,2},{2,3},{3,7},{4,0},{5,4},{6,5},{7,6},{8,9},{9,10},{10,1... | collective-permute-start | bytes 245768 | tf_op jit(solution)/shard_map/ppermute | solution.py:492
  8.1 0.0 copy-start.4
  8.1 0.0 collective-permute-done.from_odd
  8.1 0.0 collective-permute-done.1.from_even
  8.1 0.0 collective-permute-start.2
  8.2 0.0 copy-start
  8.2 0.0 copy-start.2
  8.2 2.0 %collective-permute-start.3 = (f32[24,128]{1,0:T(8,128)S(1)}, f32[24,128]{1,0:T(8,128)S(1)}, u32[]{:S(2)}, u32[]{:S(2)}) collective-permute-start(f32[24,128]{1,0:T(8,128)S(1)} %get-tuple-element.24), channel_id=1, source_target_pairs={{0,1},{1,2},{2,3},{3,7},{4,0},{5,4},{6,5},{7,6},{8,9},{9,10},{10,1... | collective-permute-start | bytes 36872 | tf_op jit(solution)/shard_map/ppermute | solution.py:492
  10.2 0.0 copy-done.3
  10.2 0.0 copy-done.1
  10.2 0.0 copy-done.4
  10.2 1.0 %push_parcels.1 = (f32[16,2048]{1,0:T(8,128)S(1)}, f32[256,128]{1,0:T(8,128)S(1)}) custom-call(f32[192,128]{1,0:T(8,128)S(1)} %bitcast.13, f32[16,2048]{1,0:T(8,128)S(1)} %bitcast.18, s32[1,1,2048]{2,1,0:T(1,128)S(1)} %copy-done.4, f32[16,128]{1,0:T(8,128)S(1)} %get-tuple-element.28.kept, s32[1,1]{1,0:T(1,128)S(6)} %copy.12.counts), custom_call_target="tpu_custom_call" | custom-call | flops 1000000000 | bytes 507908 | tf_op jit(solution)/shard_map/push_parcels/pallas_call | solution.py:471
  11.2 0.0 collective-permute-done.4.beside_two
  11.2 0.0 collective-permute-done.5.beside_one
  11.2 0.0 copy-done
  11.2 0.0 copy-done.2
  11.2 0.8 %stencils.1 = (f32[16,2048]{1,0:T(8,128)}, f32[4,16,64]{2,1,0:T(8,128)}, f32[6,144,128]{2,1,0:T(8,128)S(1)}, f32[8,64,128]{2,1,0:T(8,128)S(1)}) custom-call(f32[320,128]{1,0:T(8,128)S(1)} %bitcast.11, f32[192,128]{1,0:T(8,128)S(1)} %bitcast.14, f32[64,128]{1,0:T(8,128)S(1)} %bitcast.16, f32[160,128]{1,0:T(8,128)S(1)} %collective-permute-done.from_odd, ...), custom_call_target="tpu_custom_call" | custom-call | flops 10000000 | bytes 1736704 | tf_op jit(solution)/shard_map/stencils/pallas_call | solution.py:471
  12.0 0.0 collective-permute-done.2.corner_two
  12.0 0.0 collective-permute-done.3.corner_one
  12.0 0.9 %ends.1 = (f32[5,64,128]{2,1,0:T(8,128)}, f32[3,64,128]{2,1,0:T(8,128)}) custom-call(f32[24,128]{1,0:T(8,128)S(1)} %collective-permute-done.2.corner_two, f32[24,128]{1,0:T(8,128)S(1)} %collective-permute-done.3.corner_one, f32[6,144,128]{2,1,0:T(8,128)S(1)} %get-tuple-element.32.state, f32[8,64,128]{2,1,0:T(8,128)S(1)} %get-tuple-element.33.result), custom_call_target="tpu_custom_call" | custom-call | flops 1000000 | bytes 991232 | tf_op jit(solution)/shard_map/ends/pallas_call | solution.py:471
  (1 shorter events, 0.0 us)
Async XLA Ops:
  0.6 9.6 %copy-start.3 = (f32[1,1,16,2048]{3,2,1,0:T(8,128)S(1)}, f32[1,1,16,2048]{3,2,1,0:T(8,128)}, u32[]{:S(2)}) copy-start(f32[1,1,16,2048]{3,2,1,0:T(8,128)} %param.11) | copy-start | bytes 393220
  2.3 7.9 %copy-start.1 = (f32[3,8,8,128]{3,2,1,0:T(8,128)S(1)}, f32[3,8,8,128]{3,2,1,0:T(8,128)}, u32[]{:S(2)}) copy-start(f32[3,8,8,128]{3,2,1,0:T(8,128)} %param.9) | copy-start | bytes 294916
  2.3 5.8 %collective-permute-start = (f32[160,128]{1,0:T(8,128)S(1)}, f32[160,128]{1,0:T(8,128)S(1)}, u32[]{:S(2)}, u32[]{:S(2)}) collective-permute-start(f32[160,128]{1,0:T(8,128)S(1)} %get-tuple-element.21), channel_id=1, source_target_pairs={{0,1},{1,0},{2,3},{3,2},{4,8},{5,9},{6,10},{7,11},{8,4},{9,5},{10,... | collective-permute-start | bytes 245768 | tf_op jit(solution)/shard_map/ppermute | solution.py:492
  5.4 2.7 %collective-permute-start.1 = (f32[160,128]{1,0:T(8,128)S(1)}, f32[160,128]{1,0:T(8,128)S(1)}, u32[]{:S(2)}, u32[]{:S(2)}) collective-permute-start(f32[160,128]{1,0:T(8,128)S(1)} %get-tuple-element.22), channel_id=1, source_target_pairs={{0,4},{1,5},{2,6},{3,7},{4,0},{5,1},{6,2},{7,3},{8,12},{9,13},{10,... | collective-permute-start | bytes 245768 | tf_op jit(solution)/shard_map/ppermute | solution.py:492
  5.4 5.8 %collective-permute-start.4 = (f32[160,128]{1,0:T(8,128)S(1)}, f32[160,128]{1,0:T(8,128)S(1)}, u32[]{:S(2)}, u32[]{:S(2)}) collective-permute-start(f32[160,128]{1,0:T(8,128)S(1)} %get-tuple-element.25), channel_id=1, source_target_pairs={{0,4},{1,0},{2,1},{3,2},{4,5},{5,6},{6,7},{7,3},{8,12},{9,8},{10,9... | collective-permute-start | bytes 245768 | tf_op jit(solution)/shard_map/ppermute | solution.py:492
  5.9 5.3 %collective-permute-start.5 = (f32[160,128]{1,0:T(8,128)S(1)}, f32[160,128]{1,0:T(8,128)S(1)}, u32[]{:S(2)}, u32[]{:S(2)}) collective-permute-start(f32[160,128]{1,0:T(8,128)S(1)} %get-tuple-element.26), channel_id=1, source_target_pairs={{0,1},{1,2},{2,3},{3,7},{4,0},{5,4},{6,5},{7,6},{8,9},{9,10},{10,1... | collective-permute-start | bytes 245768 | tf_op jit(solution)/shard_map/ppermute | solution.py:492
  8.1 2.1 %copy-start.4 = (s32[1,1,2048]{2,1,0:T(1,128)S(1)}, s32[1,1,2048]{2,1,0:T(1,128)}, u32[]{:S(2)}) copy-start(s32[1,1,2048]{2,1,0:T(1,128)} %cells.1) | copy-start | bytes 24580
  8.1 3.8 %collective-permute-start.2 = (f32[24,128]{1,0:T(8,128)S(1)}, f32[24,128]{1,0:T(8,128)S(1)}, u32[]{:S(2)}, u32[]{:S(2)}) collective-permute-start(f32[24,128]{1,0:T(8,128)S(1)} %get-tuple-element.23), channel_id=1, source_target_pairs={{0,4},{1,0},{2,1},{3,2},{4,5},{5,6},{6,7},{7,3},{8,12},{9,8},{10,9... | collective-permute-start | bytes 36872 | tf_op jit(solution)/shard_map/ppermute | solution.py:492
  8.2 3.0 %copy-start = (f32[5,8,8,128]{3,2,1,0:T(8,128)S(1)}, f32[5,8,8,128]{3,2,1,0:T(8,128)}, u32[]{:S(2)}) copy-start(f32[5,8,8,128]{3,2,1,0:T(8,128)} %param.8) | copy-start | bytes 491524
  8.2 3.0 %copy-start.2 = (f32[8,8,128]{2,1,0:T(8,128)S(1)}, f32[8,8,128]{2,1,0:T(8,128)}, u32[]{:S(2)}) copy-start(f32[8,8,128]{2,1,0:T(8,128)} %param.10) | copy-start | bytes 98308
  8.2 3.8 %collective-permute-start.3 = (f32[24,128]{1,0:T(8,128)S(1)}, f32[24,128]{1,0:T(8,128)S(1)}, u32[]{:S(2)}, u32[]{:S(2)}) collective-permute-start(f32[24,128]{1,0:T(8,128)S(1)} %get-tuple-element.24), channel_id=1, source_target_pairs={{0,1},{1,2},{2,3},{3,7},{4,0},{5,4},{6,5},{7,6},{8,9},{9,10},{10,1... | collective-permute-start | bytes 36872 | tf_op jit(solution)/shard_map/ppermute | solution.py:492

commit v5 on v4

--- a/solution.py
+++ b/solution.py
@@ -70,23 +70,24 @@
 def pack_kernel(
     width_x, width_y, species_in, velocity_in, diffusivity_in, parcels_in, cells_in, slots_in, face_counts_in,
     axial_even, axial_odd, radial_one, radial_two, kept,
-    species, velocity, diffusivity, parcels, cells, slots, face_counts, arrived,
+    species, velocity, diffusivity, parcels, cells, slots, face_counts, moved, arrived,
 ):
     copies = [
         pltpu.make_async_copy(src, dst, arrived.at[i])
         for i, (src, dst) in enumerate(
             (
                 (slots_in, slots), (face_counts_in, face_counts), (cells_in, cells),
-                (parcels_in, parcels), (velocity_in, velocity), (species_in, species),
+                (velocity_in, velocity), (parcels_in, parcels), (species_in, species),
                 (diffusivity_in, diffusivity),
             )
         )
     ]
     for copy in copies:
         copy.start()
-    for copy in copies[:4]:
+    for copy in copies[:3]:
         copy.wait()
     cells_of, tile = width_x * width_y, width_y
+    even_x = lax.rem(lax.axis_index("axial"), 2) == 0
     movers = slots.shape[1]
     lane = lax.broadcasted_iota(I32, (1, 2 * movers), 1)
     pairs = [jnp.concatenate([slots[i : i + 1, :], slots[i + 1 : i + 2, :]], axis=1) for i in (0, 2)]
@@ -101,41 +102,16 @@
     hot_chunk = lax.broadcasted_iota(I32, (chunks, slot.shape[1]), 0) == chunk
     leaving = dot_t(jnp.where(hot_chunk, valid, 0.0).astype(BF16), hot_place)
     kept[...] = jnp.where(leaving > 0.5, 0.0, 1.0)
-    stacked = jnp.concatenate([parcels[:, h * LANES : (h + 1) * LANES] for h in range(chunks)], axis=0)
     cell = cells[...]
-    cell_high = lax.shift_right_logical(cell, 7).astype(F32)
-    cell_low = lax.bitwise_and(cell, LANES - 1).astype(F32)
-    first, second = split(stacked)
-    left = jnp.concatenate([first, cell_high.astype(BF16), cell_low.astype(BF16)], axis=0)
-    right = jnp.concatenate([second, jnp.zeros((2 * chunks, LANES), BF16)], axis=0)
-    table = dot(jnp.concatenate([left, right], axis=1), jnp.concatenate([hot_place, hot_place], axis=0))
-    rows = jnp.zeros((ROWS, slot.shape[1]), F32)
-    for h in range(chunks):
-        rows = rows + jnp.where(chunk == h, table[h * ROWS : (h + 1) * ROWS], 0.0)
-    row_of = jnp.sum(
-        jnp.where(hot_chunk, table[chunks * ROWS : chunks * ROWS + chunks], 0.0), axis=0, keepdims=True
-    ).astype(I32)
-    lane_of = jnp.sum(
-        jnp.where(hot_chunk, table[chunks * ROWS + chunks :], 0.0), axis=0, keepdims=True
-    ).astype(I32)
-    copies[4].wait()
-    gas = gas_at(velocity[...], row_of, one_hot(lane_of, LANES), cells_of)
-    response, evaporation = rows[4:5], rows[5:6]
-    pushed = [rows[i : i + 1] + time_step * (response * (gas[i] - rows[i : i + 1])) for i in range(3)]
-    pushed.append(rows[3:4] * (1.0 - time_step * evaporation))
-    pushed.extend([response, evaporation])
-    pushed.extend(rows[6 + i : 7 + i] + time_step * pushed[i] for i in range(3))
-    base = 2 * FIELDS * tile
-    for packets, lo in (((axial_even, axial_odd), 0), ((radial_one, radial_two), 2 * movers)):
-        for ref in packets:
-            part = slice(lo, lo + 2 * movers)
-            for i, row in enumerate(pushed):
-                ref[base + i : base + i + 1, :] = row[:, part] * valid[:, part]
-            ref[base + 9 : base + ROWS, :] = rows[9:ROWS, part] * valid[:, part]
-
-    for copy in copies[5:]:
+    halves = [lax.shift_right_logical(cell, 7), lax.bitwise_and(cell, LANES - 1)]
+    table = dot(jnp.concatenate([h.astype(F32) for h in halves], axis=0).astype(BF16), hot_place)
+    row_of, lane_of = (
+        jnp.sum(jnp.where(hot_chunk, table[i * chunks : (i + 1) * chunks], 0.0), axis=0, keepdims=True).astype(I32)
+        for i in range(2)
+    )
+    hot_lane = one_hot(lane_of, LANES)
+    for copy in copies[3:]:
         copy.wait()
-    even_x = lax.rem(lax.axis_index("axial"), 2) == 0
     for f in range(FIELDS):
         ref, base = (
             (species, f) if f < SPECIES else (velocity, f - SPECIES) if f < FLOW else (diffusivity, 0)
@@ -150,6 +126,30 @@
             high = ref[pl.ds(base * cells_of + width_y - 2 + layer, width_x, stride=width_y), :]
             radial_one[at, :] = jnp.where(even_x, high, low)
             radial_two[at, :] = jnp.where(even_x, low, high)
+    gas = gas_at(velocity[...], row_of, hot_lane, cells_of)
+    stacked = jnp.concatenate([parcels[:, h * LANES : (h + 1) * LANES] for h in range(chunks)], axis=0)
+    table = dot(
+        jnp.concatenate(split(stacked), axis=1), jnp.concatenate([hot_place, hot_place], axis=0)
+    )
+    rows = jnp.zeros((ROWS, slot.shape[1]), F32)
+    for h in range(chunks):
+        rows = rows + jnp.where(chunk == h, table[h * ROWS : (h + 1) * ROWS], 0.0)
+    response, evaporation = rows[4:5], rows[5:6]
+    pushed = [rows[i : i + 1] + time_step * (response * (gas[i] - rows[i : i + 1])) for i in range(3)]
+    pushed.append(rows[3:4] * (1.0 - time_step * evaporation))
+    pushed.extend([response, evaporation])
+    pushed.extend(rows[6 + i : 7 + i] + time_step * pushed[i] for i in range(3))
+    for i, line in enumerate(pushed):
+        moved[i : i + 1, :] = line * valid
+    moved[9:ROWS, :] = rows[9:ROWS] * valid
+    base = 2 * FIELDS * tile
+    left_half = lax.broadcasted_iota(I32, (ROWS // 2, 2 * movers), 1) < movers
+    for packets, lo in (((axial_even, axial_odd), 0), ((radial_one, radial_two), 2 * movers)):
+        top, bottom = (moved[i : i + ROWS // 2, lo : lo + 2 * movers] for i in (0, ROWS // 2))
+        up = jnp.where(left_half, top, pltpu.roll(bottom, movers, 1))
+        down = jnp.where(left_half, pltpu.roll(top, movers, 1), bottom)
+        packets[0][base : base + ROWS // 2, :] = jnp.where(even_x, up, down)
+        packets[1][base : base + ROWS // 2, :] = jnp.where(even_x, down, up)
 
 
 def gas_at(velocity, row_of, hot_lane, rows):
@@ -224,10 +224,10 @@
 
 def stencil_kernel(
     width_x, width_y, species, velocity, diffusivity, from_odd, from_even, beside_two, beside_one, source, staying,
-    staying_out, arrivals_out, state, result, arrivals, sent,
+    staying_out, state, result, arrivals, sent,
 ):
-    copies = [pltpu.make_async_copy(staying, staying_out, sent.at[0])]
-    copies[0].start()
+    copy = pltpu.make_async_copy(staying, staying_out, sent)
+    copy.start()
     tile = width_y
     rows = width_x * width_y
     depth = LANES
@@ -263,11 +263,10 @@
 
     movers = arrivals.shape[-1]
     base = 2 * FIELDS * tile
-    for side, (low, high) in ((0, axial_halo(base, ROWS)), (2, radial_halo(base, ROWS))):
-        arrivals[side] = low[:, :movers]
-        arrivals[side + 1] = high[:, movers : 2 * movers]
-    copies.append(pltpu.make_async_copy(arrivals, arrivals_out, sent.at[1]))
-    copies[-1].start()
+    for side, parts in ((0, axial_halo(base, ROWS // 2)), (2, radial_halo(base, ROWS // 2))):
+        for i, part in enumerate(parts):
+            arrivals[side + i, : ROWS // 2] = part[:, :movers]
+            arrivals[side + i, ROWS // 2 :] = part[:, movers : 2 * movers]
 
     def up_down(x, axis):
         size = x.shape[axis]
@@ -398,11 +397,12 @@
         if part is not None:
             value = value + time_step * source[part * rows : (part + 1) * rows, :]
         result[f] = value
-    for copy in copies:
-        copy.wait()
-
-
-def end_kernel(width_x, width_y, corner_two, corner_one, state, result, species_out, velocity_out, ends, sent):
+    copy.wait()
+
+
+def end_kernel(
+    width_x, width_y, corner_two, corner_one, state, result, arrivals, species_out, velocity_out, arrivals_out, ends, sent,
+):
     tile = width_y
     rows = width_x * width_y
     at_x, size_x = lax.axis_index("axial"), lax.axis_size("axial")
@@ -418,12 +418,13 @@
         pltpu.make_async_copy(
             result.at[pl.ds(SPECIES, VECTORS), middle, :], velocity_out.at[:, middle, :], sent.at[1]
         ),
+        pltpu.make_async_copy(arrivals, arrivals_out, sent.at[6]),
     ]
     for copy in copies:
         copy.start()
     for f in range(FLOW):
-        ends[0, f * tile : (f + 1) * tile, :] = result[f, :tile, :]
-        ends[1, f * tile : (f + 1) * tile, :] = result[f, last:, :]
+        ends[0, f] = result[f, :tile, :]
+        ends[1, f] = result[f, last:, :]
 
     def fields_at(part, side, place):
         return state[part, pl.ds(side * tile + place, FLOW, stride=2 * tile), :]
@@ -448,15 +449,13 @@
                 moved = jnp.where(has, fields_at(part + 2, side, place) + 0.5 * time_step * flux, 0.0)
                 term = (later + of(moved, one_at(part + 2, side, place))) * (moved - here)
                 total = term if total is None else total + term
-            at = pl.ds(y, FLOW, stride=tile)
-            ends[side_x, at, :] = ends[side_x, at, :] + 0.25 * time_step * total
-    for f in range(FLOW):
-        ref, at = (species_out, f) if f < SPECIES else (velocity_out, f - SPECIES)
-        for side, x in ((0, 0), (1, last)):
+            at = (side_x, slice(None), y)
+            ends[at] = ends[at] + 0.25 * time_step * total
+    for side, x in ((0, 0), (1, last)):
+        for i, (ref, lo, n) in enumerate(((species_out, 0, SPECIES), (velocity_out, SPECIES, VECTORS))):
             copies.append(
                 pltpu.make_async_copy(
-                    ends.at[side, pl.ds(f * tile, tile), :], ref.at[at, pl.ds(x, tile), :],
-                    sent.at[2 + 2 * f + side],
+                    ends.at[side, pl.ds(lo, n)], ref.at[:, pl.ds(x, tile), :], sent.at[2 + 2 * side + i]
                 )
             )
             copies[-1].start()
@@ -494,7 +493,7 @@
     velocity2 = velocity.reshape(VECTORS * rows, depth)
     diffusivity2 = diffusivity.reshape(rows, depth)
     parcels2 = parcels.reshape(ROWS, slots)
-    packet_rows = 2 * FIELDS * width_y + ROWS
+    packet_rows = 2 * FIELDS * width_y + ROWS // 2
     chunks = slots // LANES
 
     def near(x):
@@ -509,7 +508,7 @@
         fields + [parcels2, cells2, slots2, leave_counts],
         10**8, "pack_faces", far_ins=range(7),
         scratch=[near(x) for x in fields + [parcels2, cells2, slots2]]
-        + [pltpu.SMEM(leave_counts.shape, I32), pltpu.SemaphoreType.DMA((7,))],
+        + [pltpu.SMEM(leave_counts.shape, I32), near(f32(ROWS, 4 * movers)), pltpu.SemaphoreType.DMA((7,))],
     )
     from_odd = permute(axial_odd, axial_swap(sizes, True))
     from_even = permute(axial_even, axial_swap(sizes, False))
@@ -523,12 +522,11 @@
         10**9, "push_parcels",
     )
     state = f32(6, 2 * (FLOW + 1) * width_y, depth)
-    staying, arrivals, state, result = call(
+    staying, state, result, arrivals = call(
         functools.partial(stencil_kernel, width_x, width_y),
-        [f32(ROWS, slots), f32(4, ROWS, movers), state, f32(FLOW, rows, depth)],
+        [f32(ROWS, slots), state, f32(FLOW, rows, depth), f32(4, ROWS, movers)],
         fields + [from_odd, from_even, beside_two, beside_one, source, staying],
-        10**7, "stencils", far_outs=(0, 1),
-        scratch=[near(f32(4, ROWS, movers)), pltpu.SemaphoreType.DMA((2,))],
+        10**7, "stencils", far_outs=(0,), scratch=[pltpu.SemaphoreType.DMA],
     )
     corner_one, corner_two = call(
         functools.partial(corner_kernel, width_x, width_y),
@@ -536,12 +534,12 @@
     )
     corner_two = permute(corner_two, radial_shift(sizes, False))
     corner_one = permute(corner_one, radial_shift(sizes, True))
-    species_out, velocity_out = call(
+    species_out, velocity_out, arrivals = call(
         functools.partial(end_kernel, width_x, width_y),
-        [f32(SPECIES, rows, depth), f32(VECTORS, rows, depth)],
-        [corner_two, corner_one, state, result],
-        10**6, "ends", far_outs=(0, 1),
-        scratch=[near(f32(2, FLOW * width_y, depth)), pltpu.SemaphoreType.DMA((2 + 2 * FLOW,))],
+        [f32(SPECIES, rows, depth), f32(VECTORS, rows, depth), f32(4, ROWS, movers)],
+        [corner_two, corner_one, state, result, arrivals],
+        10**6, "ends", far_outs=(0, 1, 2),
+        scratch=[near(f32(2, FLOW, width_y, depth)), pltpu.SemaphoreType.DMA((7,))],
     )
     return (
         species_out.reshape(species.shape),

time: 13 us -> 12.8 us (0.985)
  Pallas kernels: 4.24 us -> 4.04 us
    pallas_call x5, Pallas kernels: 4.24 us -> 4.04 us  [call(): pl.pallas_call(kernel, out_shape=[jax.ShapeDtypeStruct(s.shape, s.dtype)...]
where the time goes in v5:
time: 12.8 us; the launch traced here: 12.7 us
  starting transfers between devices  7.16 us (56%)
  Pallas kernels  4.04 us (32%)
  between operations  1.43 us (11%)
    ppermute x6, starting transfers between devices, body(): permute = lambda x, pairs: lax.ppermute(x, AXES, pairs)  7.16 us
    pallas_call x5, Pallas kernels, call(): pl.pallas_call(kernel, out_shape=[jax.ShapeDtypeStruct(s.shape, s.dtype)...  4.04 us
  transfers between devices with their start and end apart: 6, of which 0 were waited for; matrix products, arithmetic and copies ran while one was open for 0% of the time, Pallas kernels for 14%

profile of v5, /device:TPU:0, one launch (start us, length us, event | category | flops | bytes accessed | tf_op | source)
XLA Modules:
  0.0 12.7 jit_solution(2464865023965895228)
XLA Ops:
  0.6 0.0 copy-start.2
  0.6 1.5 %pack_faces.1 = (f32[152,128]{1,0:T(8,128)S(1)}, f32[152,128]{1,0:T(8,128)S(1)}, f32[152,128]{1,0:T(8,128)S(1)}, f32[152,128]{1,0:T(8,128)S(1)}, f32[16,128]{1,0:T(8,128)S(1)}) custom-call(f32[320,128]{1,0:T(8,128)} %bitcast.10, f32[192,128]{1,0:T(8,128)} %bitcast.12, f32[64,128]{1,0:T(8,128)} %bitcast.17, f32[16,2048]{1,0:T(8,128)} %bitcast.15, ...), custom_call_target="tpu_custom_call" | custom-call | flops 100000000 | bytes 754704 | tf_op jit(solution)/shard_map/pack_faces/pallas_call | solution.py:470
  2.1 0.0 copy-start.1
  2.1 3.1 %collective-permute-start = (f32[152,128]{1,0:T(8,128)S(1)}, f32[152,128]{1,0:T(8,128)S(1)}, u32[]{:S(2)}, u32[]{:S(2)}) collective-permute-start(f32[152,128]{1,0:T(8,128)S(1)} %get-tuple-element.22), channel_id=1, source_target_pairs={{0,1},{1,0},{2,3},{3,2},{4,8},{5,9},{6,10},{7,11},{8,4},{9,5},{10,... | collective-permute-start | bytes 233480 | tf_op jit(solution)/shard_map/ppermute | solution.py:491
  5.2 0.0 collective-permute-start.1
  5.3 0.5 %collective-permute-start.4 = (f32[152,128]{1,0:T(8,128)S(1)}, f32[152,128]{1,0:T(8,128)S(1)}, u32[]{:S(2)}, u32[]{:S(2)}) collective-permute-start(f32[152,128]{1,0:T(8,128)S(1)} %get-tuple-element.26), channel_id=1, source_target_pairs={{0,4},{1,0},{2,1},{3,2},{4,5},{5,6},{6,7},{7,3},{8,12},{9,8},{10,9... | collective-permute-start | bytes 233480 | tf_op jit(solution)/shard_map/ppermute | solution.py:491
  5.8 1.5 %collective-permute-start.5 = (f32[152,128]{1,0:T(8,128)S(1)}, f32[152,128]{1,0:T(8,128)S(1)}, u32[]{:S(2)}, u32[]{:S(2)}) collective-permute-start(f32[152,128]{1,0:T(8,128)S(1)} %get-tuple-element.27), channel_id=1, source_target_pairs={{0,1},{1,2},{2,3},{3,7},{4,0},{5,4},{6,5},{7,6},{8,9},{9,10},{10,1... | collective-permute-start | bytes 233480 | tf_op jit(solution)/shard_map/ppermute | solution.py:491
  7.9 0.0 copy-start.4
  8.0 0.0 collective-permute-done.from_odd
  8.0 0.0 collective-permute-done.1.from_even
  8.0 0.0 collective-permute-start.2
  8.0 0.0 copy-start
  8.1 0.0 copy-start.3
  8.1 2.0 %collective-permute-start.3 = (f32[24,128]{1,0:T(8,128)S(1)}, f32[24,128]{1,0:T(8,128)S(1)}, u32[]{:S(2)}, u32[]{:S(2)}) collective-permute-start(f32[24,128]{1,0:T(8,128)S(1)} %get-tuple-element.25), channel_id=1, source_target_pairs={{0,1},{1,2},{2,3},{3,7},{4,0},{5,4},{6,5},{7,6},{8,9},{9,10},{10,1... | collective-permute-start | bytes 36872 | tf_op jit(solution)/shard_map/ppermute | solution.py:491
  10.1 0.0 copy-done.2
  10.1 0.0 copy-done.1
  10.1 0.0 copy-done.4
  10.1 1.0 %push_parcels.1 = (f32[16,2048]{1,0:T(8,128)S(1)}, f32[256,128]{1,0:T(8,128)S(1)}) custom-call(f32[192,128]{1,0:T(8,128)S(1)} %bitcast.13, f32[16,2048]{1,0:T(8,128)S(1)} %bitcast.16, s32[1,1,2048]{2,1,0:T(1,128)S(1)} %copy-done.4, f32[16,128]{1,0:T(8,128)S(1)} %get-tuple-element.29.kept, s32[1,1]{1,0:T(1,128)S(6)} %copy.12.counts), custom_call_target="tpu_custom_call" | custom-call | flops 1000000000 | bytes 507908 | tf_op jit(solution)/shard_map/push_parcels/pallas_call | solution.py:470
  11.0 0.0 collective-permute-done.4.beside_two
  11.1 0.0 collective-permute-done.5.beside_one
  11.1 0.0 copy-done
  11.1 0.0 copy-done.3
  11.1 0.8 %stencils.1 = (f32[16,2048]{1,0:T(8,128)}, f32[6,144,128]{2,1,0:T(8,128)S(1)}, f32[8,64,128]{2,1,0:T(8,128)S(1)}, f32[4,16,64]{2,1,0:T(8,128)S(1)}) custom-call(f32[320,128]{1,0:T(8,128)S(1)} %bitcast.11, f32[192,128]{1,0:T(8,128)S(1)} %bitcast.14, f32[64,128]{1,0:T(8,128)S(1)} %bitcast.18, f32[152,128]{1,0:T(8,128)S(1)} %collective-permute-done.from_odd, ...), custom_call_target="tpu_custom_call" | custom-call | flops 10000000 | bytes 1720320 | tf_op jit(solution)/shard_map/stencils/pallas_call | solution.py:470
  11.9 0.0 collective-permute-done.2.corner_two
  11.9 0.0 collective-permute-done.3.corner_one
  11.9 0.8 %ends.1 = (f32[5,64,128]{2,1,0:T(8,128)}, f32[3,64,128]{2,1,0:T(8,128)}, f32[4,16,64]{2,1,0:T(8,128)}) custom-call(f32[24,128]{1,0:T(8,128)S(1)} %collective-permute-done.2.corner_two, f32[24,128]{1,0:T(8,128)S(1)} %collective-permute-done.3.corner_one, f32[6,144,128]{2,1,0:T(8,128)S(1)} %get-tuple-element.33.state, ...), custom_call_target="tpu_custom_call" | custom-call | flops 1000000 | bytes 1024000 | tf_op jit(solution)/shard_map/ends/pallas_call | solution.py:470
  (1 shorter events, 0.0 us)
Async XLA Ops:
  0.6 9.4 %copy-start.2 = (f32[1,1,16,2048]{3,2,1,0:T(8,128)S(1)}, f32[1,1,16,2048]{3,2,1,0:T(8,128)}, u32[]{:S(2)}) copy-start(f32[1,1,16,2048]{3,2,1,0:T(8,128)} %param.11) | copy-start | bytes 393220
  2.1 7.9 %copy-start.1 = (f32[3,8,8,128]{3,2,1,0:T(8,128)S(1)}, f32[3,8,8,128]{3,2,1,0:T(8,128)}, u32[]{:S(2)}) copy-start(f32[3,8,8,128]{3,2,1,0:T(8,128)} %param.9) | copy-start | bytes 294916
  2.1 5.8 %collective-permute-start = (f32[152,128]{1,0:T(8,128)S(1)}, f32[152,128]{1,0:T(8,128)S(1)}, u32[]{:S(2)}, u32[]{:S(2)}) collective-permute-start(f32[152,128]{1,0:T(8,128)S(1)} %get-tuple-element.22), channel_id=1, source_target_pairs={{0,1},{1,0},{2,3},{3,2},{4,8},{5,9},{6,10},{7,11},{8,4},{9,5},{10,... | collective-permute-start | bytes 233480 | tf_op jit(solution)/shard_map/ppermute | solution.py:491
  5.2 2.7 %collective-permute-start.1 = (f32[152,128]{1,0:T(8,128)S(1)}, f32[152,128]{1,0:T(8,128)S(1)}, u32[]{:S(2)}, u32[]{:S(2)}) collective-permute-start(f32[152,128]{1,0:T(8,128)S(1)} %get-tuple-element.23), channel_id=1, source_target_pairs={{0,4},{1,5},{2,6},{3,7},{4,0},{5,1},{6,2},{7,3},{8,12},{9,13},{10,... | collective-permute-start | bytes 233480 | tf_op jit(solution)/shard_map/ppermute | solution.py:491
  5.3 5.8 %collective-permute-start.4 = (f32[152,128]{1,0:T(8,128)S(1)}, f32[152,128]{1,0:T(8,128)S(1)}, u32[]{:S(2)}, u32[]{:S(2)}) collective-permute-start(f32[152,128]{1,0:T(8,128)S(1)} %get-tuple-element.26), channel_id=1, source_target_pairs={{0,4},{1,0},{2,1},{3,2},{4,5},{5,6},{6,7},{7,3},{8,12},{9,8},{10,9... | collective-permute-start | bytes 233480 | tf_op jit(solution)/shard_map/ppermute | solution.py:491
  5.8 5.3 %collective-permute-start.5 = (f32[152,128]{1,0:T(8,128)S(1)}, f32[152,128]{1,0:T(8,128)S(1)}, u32[]{:S(2)}, u32[]{:S(2)}) collective-permute-start(f32[152,128]{1,0:T(8,128)S(1)} %get-tuple-element.27), channel_id=1, source_target_pairs={{0,1},{1,2},{2,3},{3,7},{4,0},{5,4},{6,5},{7,6},{8,9},{9,10},{10,1... | collective-permute-start | bytes 233480 | tf_op jit(solution)/shard_map/ppermute | solution.py:491
  7.9 2.1 %copy-start.4 = (s32[1,1,2048]{2,1,0:T(1,128)S(1)}, s32[1,1,2048]{2,1,0:T(1,128)}, u32[]{:S(2)}) copy-start(s32[1,1,2048]{2,1,0:T(1,128)} %cells.1) | copy-start | bytes 24580
  8.0 3.9 %collective-permute-start.2 = (f32[24,128]{1,0:T(8,128)S(1)}, f32[24,128]{1,0:T(8,128)S(1)}, u32[]{:S(2)}, u32[]{:S(2)}) collective-permute-start(f32[24,128]{1,0:T(8,128)S(1)} %get-tuple-element.24), channel_id=1, source_target_pairs={{0,4},{1,0},{2,1},{3,2},{4,5},{5,6},{6,7},{7,3},{8,12},{9,8},{10,9... | collective-permute-start | bytes 36872 | tf_op jit(solution)/shard_map/ppermute | solution.py:491
  8.0 3.0 %copy-start = (f32[5,8,8,128]{3,2,1,0:T(8,128)S(1)}, f32[5,8,8,128]{3,2,1,0:T(8,128)}, u32[]{:S(2)}) copy-start(f32[5,8,8,128]{3,2,1,0:T(8,128)} %param.8) | copy-start | bytes 491524
  8.1 3.0 %copy-start.3 = (f32[8,8,128]{2,1,0:T(8,128)S(1)}, f32[8,8,128]{2,1,0:T(8,128)}, u32[]{:S(2)}) copy-start(f32[8,8,128]{2,1,0:T(8,128)} %param.10) | copy-start | bytes 98308
  8.1 3.8 %collective-permute-start.3 = (f32[24,128]{1,0:T(8,128)S(1)}, f32[24,128]{1,0:T(8,128)S(1)}, u32[]{:S(2)}, u32[]{:S(2)}) collective-permute-start(f32[24,128]{1,0:T(8,128)S(1)} %get-tuple-element.25), channel_id=1, source_target_pairs={{0,1},{1,2},{2,3},{3,7},{4,0},{5,4},{6,5},{7,6},{8,9},{9,10},{10,1... | collective-permute-start | bytes 36872 | tf_op jit(solution)/shard_map/ppermute | solution.py:491

commit v6 on v5

--- a/solution.py
+++ b/solution.py
@@ -50,8 +50,13 @@
 
 
 def one_hot(index, depth):
-    rows = lax.broadcasted_iota(I32, (depth, index.shape[1]), 0)
-    return (rows == index).astype(F32).astype(BF16)
+    assert depth <= 256
+    rows = lax.broadcasted_iota(I32, (depth, LANES), 0).astype(F32).astype(BF16)
+    index = index.astype(F32).astype(BF16)
+    one, zero = jnp.ones((), BF16), jnp.zeros((), BF16)
+    return jnp.concatenate(
+        [jnp.where(rows == index[:, i : i + LANES], one, zero) for i in range(0, index.shape[1], LANES)], axis=1
+    )
 
 
 def pick(table, index):
@@ -110,7 +115,17 @@
         for i in range(2)
     )
     hot_lane = one_hot(lane_of, LANES)
-    for copy in copies[3:]:
+    copies[3].wait()
+    copies[4].wait()
+    gas = gas_at(velocity[...], row_of, hot_lane, cells_of)
+    stacked = jnp.concatenate([parcels[:, h * LANES : (h + 1) * LANES] for h in range(chunks)], axis=0)
+    table = dot(
+        jnp.concatenate(split(stacked), axis=1), jnp.concatenate([hot_place, hot_place], axis=0)
+    )
+    rows = jnp.zeros((ROWS, slot.shape[1]), F32)
+    for h in range(chunks):
+        rows = rows + jnp.where(chunk == h, table[h * ROWS : (h + 1) * ROWS], 0.0)
+    for copy in copies[5:]:
         copy.wait()
     for f in range(FIELDS):
         ref, base = (
@@ -126,14 +141,6 @@
             high = ref[pl.ds(base * cells_of + width_y - 2 + layer, width_x, stride=width_y), :]
             radial_one[at, :] = jnp.where(even_x, high, low)
             radial_two[at, :] = jnp.where(even_x, low, high)
-    gas = gas_at(velocity[...], row_of, hot_lane, cells_of)
-    stacked = jnp.concatenate([parcels[:, h * LANES : (h + 1) * LANES] for h in range(chunks)], axis=0)
-    table = dot(
-        jnp.concatenate(split(stacked), axis=1), jnp.concatenate([hot_place, hot_place], axis=0)
-    )
-    rows = jnp.zeros((ROWS, slot.shape[1]), F32)
-    for h in range(chunks):
-        rows = rows + jnp.where(chunk == h, table[h * ROWS : (h + 1) * ROWS], 0.0)
     response, evaporation = rows[4:5], rows[5:6]
     pushed = [rows[i : i + 1] + time_step * (response * (gas[i] - rows[i : i + 1])) for i in range(3)]
     pushed.append(rows[3:4] * (1.0 - time_step * evaporation))

time: 12.8 us -> 12.7 us (level)
  Pallas kernels: 4.04 us -> 3.83 us
    pallas_call x5, Pallas kernels: 4.04 us -> 3.83 us  [call(): pl.pallas_call(kernel, out_shape=[jax.ShapeDtypeStruct(s.shape, s.dtype)...]
  transfers between devices with their start and end apart: 6 -> 6, of which waited for: 0 -> 0; matrix products, arithmetic and copies ran while one was open for 0% -> 0% of each run, Pallas kernels for 14% -> 13%
where the time goes in v6:
time: 12.7 us; the launch traced here: 12.5 us
  starting transfers between devices  7.16 us (56%)
  Pallas kernels  3.83 us (30%)
  between operations  1.41 us (11%)
    ppermute x6, starting transfers between devices, body(): permute = lambda x, pairs: lax.ppermute(x, AXES, pairs)  7.16 us
    pallas_call x5, Pallas kernels, call(): pl.pallas_call(kernel, out_shape=[jax.ShapeDtypeStruct(s.shape, s.dtype)...  3.83 us
  transfers between devices with their start and end apart: 6, of which 0 were waited for; matrix products, arithmetic and copies ran while one was open for 0% of the time, Pallas kernels for 13%

profile of v6, /device:TPU:0, one launch (start us, length us, event | category | flops | bytes accessed | tf_op | source)
XLA Modules:
  0.0 12.5 jit_solution(6661604752140178456)
XLA Ops:
  0.6 0.0 copy-start.2
  0.6 1.4 %pack_faces.1 = (f32[152,128]{1,0:T(8,128)S(1)}, f32[152,128]{1,0:T(8,128)S(1)}, f32[152,128]{1,0:T(8,128)S(1)}, f32[152,128]{1,0:T(8,128)S(1)}, f32[16,128]{1,0:T(8,128)S(1)}) custom-call(f32[320,128]{1,0:T(8,128)} %bitcast.10, f32[192,128]{1,0:T(8,128)} %bitcast.12, f32[64,128]{1,0:T(8,128)} %bitcast.17, f32[16,2048]{1,0:T(8,128)} %bitcast.15, ...), custom_call_target="tpu_custom_call" | custom-call | flops 100000000 | bytes 754704 | tf_op jit(solution)/shard_map/pack_faces/pallas_call | solution.py:477
  2.1 0.0 copy-start.1
  2.1 3.1 %collective-permute-start = (f32[152,128]{1,0:T(8,128)S(1)}, f32[152,128]{1,0:T(8,128)S(1)}, u32[]{:S(2)}, u32[]{:S(2)}) collective-permute-start(f32[152,128]{1,0:T(8,128)S(1)} %get-tuple-element.22), channel_id=1, source_target_pairs={{0,1},{1,0},{2,3},{3,2},{4,8},{5,9},{6,10},{7,11},{8,4},{9,5},{10,... | collective-permute-start | bytes 233480 | tf_op jit(solution)/shard_map/ppermute | solution.py:498
  5.2 0.0 collective-permute-start.1
  5.2 0.5 %collective-permute-start.4 = (f32[152,128]{1,0:T(8,128)S(1)}, f32[152,128]{1,0:T(8,128)S(1)}, u32[]{:S(2)}, u32[]{:S(2)}) collective-permute-start(f32[152,128]{1,0:T(8,128)S(1)} %get-tuple-element.26), channel_id=1, source_target_pairs={{0,4},{1,0},{2,1},{3,2},{4,5},{5,6},{6,7},{7,3},{8,12},{9,8},{10,9... | collective-permute-start | bytes 233480 | tf_op jit(solution)/shard_map/ppermute | solution.py:498
  5.7 1.5 %collective-permute-start.5 = (f32[152,128]{1,0:T(8,128)S(1)}, f32[152,128]{1,0:T(8,128)S(1)}, u32[]{:S(2)}, u32[]{:S(2)}) collective-permute-start(f32[152,128]{1,0:T(8,128)S(1)} %get-tuple-element.27), channel_id=1, source_target_pairs={{0,1},{1,2},{2,3},{3,7},{4,0},{5,4},{6,5},{7,6},{8,9},{9,10},{10,1... | collective-permute-start | bytes 233480 | tf_op jit(solution)/shard_map/ppermute | solution.py:498
  7.9 0.0 copy-start.4
  7.9 0.0 collective-permute-done.from_odd
  7.9 0.0 collective-permute-done.1.from_even
  8.0 0.0 collective-permute-start.2
  8.0 0.0 copy-start
  8.0 0.0 copy-start.3
  8.0 2.0 %collective-permute-start.3 = (f32[24,128]{1,0:T(8,128)S(1)}, f32[24,128]{1,0:T(8,128)S(1)}, u32[]{:S(2)}, u32[]{:S(2)}) collective-permute-start(f32[24,128]{1,0:T(8,128)S(1)} %get-tuple-element.25), channel_id=1, source_target_pairs={{0,1},{1,2},{2,3},{3,7},{4,0},{5,4},{6,5},{7,6},{8,9},{9,10},{10,1... | collective-permute-start | bytes 36872 | tf_op jit(solution)/shard_map/ppermute | solution.py:498
  10.0 0.0 copy-done.2
  10.0 0.0 copy-done.1
  10.0 0.0 copy-done.4
  10.0 0.8 %push_parcels.1 = (f32[16,2048]{1,0:T(8,128)S(1)}, f32[256,128]{1,0:T(8,128)S(1)}) custom-call(f32[192,128]{1,0:T(8,128)S(1)} %bitcast.13, f32[16,2048]{1,0:T(8,128)S(1)} %bitcast.16, s32[1,1,2048]{2,1,0:T(1,128)S(1)} %copy-done.4, f32[16,128]{1,0:T(8,128)S(1)} %get-tuple-element.29.kept, s32[1,1]{1,0:T(1,128)S(6)} %copy.12.counts), custom_call_target="tpu_custom_call" | custom-call | flops 1000000000 | bytes 507908 | tf_op jit(solution)/shard_map/push_parcels/pallas_call | solution.py:477
  10.8 0.0 collective-permute-done.4.beside_two
  10.8 0.0 collective-permute-done.5.beside_one
  10.8 0.0 copy-done
  10.9 0.0 copy-done.3
  10.9 0.8 %stencils.1 = (f32[16,2048]{1,0:T(8,128)}, f32[6,144,128]{2,1,0:T(8,128)S(1)}, f32[8,64,128]{2,1,0:T(8,128)S(1)}, f32[4,16,64]{2,1,0:T(8,128)S(1)}) custom-call(f32[320,128]{1,0:T(8,128)S(1)} %bitcast.11, f32[192,128]{1,0:T(8,128)S(1)} %bitcast.14, f32[64,128]{1,0:T(8,128)S(1)} %bitcast.18, f32[152,128]{1,0:T(8,128)S(1)} %collective-permute-done.from_odd, ...), custom_call_target="tpu_custom_call" | custom-call | flops 10000000 | bytes 1720320 | tf_op jit(solution)/shard_map/stencils/pallas_call | solution.py:477
  11.7 0.0 collective-permute-done.2.corner_two
  11.7 0.0 collective-permute-done.3.corner_one
  11.7 0.8 %ends.1 = (f32[5,64,128]{2,1,0:T(8,128)}, f32[3,64,128]{2,1,0:T(8,128)}, f32[4,16,64]{2,1,0:T(8,128)}) custom-call(f32[24,128]{1,0:T(8,128)S(1)} %collective-permute-done.2.corner_two, f32[24,128]{1,0:T(8,128)S(1)} %collective-permute-done.3.corner_one, f32[6,144,128]{2,1,0:T(8,128)S(1)} %get-tuple-element.33.state, ...), custom_call_target="tpu_custom_call" | custom-call | flops 1000000 | bytes 1024000 | tf_op jit(solution)/shard_map/ends/pallas_call | solution.py:477
  (1 shorter events, 0.0 us)
Async XLA Ops:
  0.6 9.4 %copy-start.2 = (f32[1,1,16,2048]{3,2,1,0:T(8,128)S(1)}, f32[1,1,16,2048]{3,2,1,0:T(8,128)}, u32[]{:S(2)}) copy-start(f32[1,1,16,2048]{3,2,1,0:T(8,128)} %param.11) | copy-start | bytes 393220
  2.1 7.9 %copy-start.1 = (f32[3,8,8,128]{3,2,1,0:T(8,128)S(1)}, f32[3,8,8,128]{3,2,1,0:T(8,128)}, u32[]{:S(2)}) copy-start(f32[3,8,8,128]{3,2,1,0:T(8,128)} %param.9) | copy-start | bytes 294916
  2.1 5.8 %collective-permute-start = (f32[152,128]{1,0:T(8,128)S(1)}, f32[152,128]{1,0:T(8,128)S(1)}, u32[]{:S(2)}, u32[]{:S(2)}) collective-permute-start(f32[152,128]{1,0:T(8,128)S(1)} %get-tuple-element.22), channel_id=1, source_target_pairs={{0,1},{1,0},{2,3},{3,2},{4,8},{5,9},{6,10},{7,11},{8,4},{9,5},{10,... | collective-permute-start | bytes 233480 | tf_op jit(solution)/shard_map/ppermute | solution.py:498
  5.2 2.7 %collective-permute-start.1 = (f32[152,128]{1,0:T(8,128)S(1)}, f32[152,128]{1,0:T(8,128)S(1)}, u32[]{:S(2)}, u32[]{:S(2)}) collective-permute-start(f32[152,128]{1,0:T(8,128)S(1)} %get-tuple-element.23), channel_id=1, source_target_pairs={{0,4},{1,5},{2,6},{3,7},{4,0},{5,1},{6,2},{7,3},{8,12},{9,13},{10,... | collective-permute-start | bytes 233480 | tf_op jit(solution)/shard_map/ppermute | solution.py:498
  5.2 5.6 %collective-permute-start.4 = (f32[152,128]{1,0:T(8,128)S(1)}, f32[152,128]{1,0:T(8,128)S(1)}, u32[]{:S(2)}, u32[]{:S(2)}) collective-permute-start(f32[152,128]{1,0:T(8,128)S(1)} %get-tuple-element.26), channel_id=1, source_target_pairs={{0,4},{1,0},{2,1},{3,2},{4,5},{5,6},{6,7},{7,3},{8,12},{9,8},{10,9... | collective-permute-start | bytes 233480 | tf_op jit(solution)/shard_map/ppermute | solution.py:498
  5.7 5.1 %collective-permute-start.5 = (f32[152,128]{1,0:T(8,128)S(1)}, f32[152,128]{1,0:T(8,128)S(1)}, u32[]{:S(2)}, u32[]{:S(2)}) collective-permute-start(f32[152,128]{1,0:T(8,128)S(1)} %get-tuple-element.27), channel_id=1, source_target_pairs={{0,1},{1,2},{2,3},{3,7},{4,0},{5,4},{6,5},{7,6},{8,9},{9,10},{10,1... | collective-permute-start | bytes 233480 | tf_op jit(solution)/shard_map/ppermute | solution.py:498
  7.9 2.1 %copy-start.4 = (s32[1,1,2048]{2,1,0:T(1,128)S(1)}, s32[1,1,2048]{2,1,0:T(1,128)}, u32[]{:S(2)}) copy-start(s32[1,1,2048]{2,1,0:T(1,128)} %cells.1) | copy-start | bytes 24580
  8.0 3.8 %collective-permute-start.2 = (f32[24,128]{1,0:T(8,128)S(1)}, f32[24,128]{1,0:T(8,128)S(1)}, u32[]{:S(2)}, u32[]{:S(2)}) collective-permute-start(f32[24,128]{1,0:T(8,128)S(1)} %get-tuple-element.24), channel_id=1, source_target_pairs={{0,4},{1,0},{2,1},{3,2},{4,5},{5,6},{6,7},{7,3},{8,12},{9,8},{10,9... | collective-permute-start | bytes 36872 | tf_op jit(solution)/shard_map/ppermute | solution.py:498
  8.0 2.9 %copy-start = (f32[5,8,8,128]{3,2,1,0:T(8,128)S(1)}, f32[5,8,8,128]{3,2,1,0:T(8,128)}, u32[]{:S(2)}) copy-start(f32[5,8,8,128]{3,2,1,0:T(8,128)} %param.8) | copy-start | bytes 491524
  8.0 2.9 %copy-start.3 = (f32[8,8,128]{2,1,0:T(8,128)S(1)}, f32[8,8,128]{2,1,0:T(8,128)}, u32[]{:S(2)}) copy-start(f32[8,8,128]{2,1,0:T(8,128)} %param.10) | copy-start | bytes 98308
  8.0 3.7 %collective-permute-start.3 = (f32[24,128]{1,0:T(8,128)S(1)}, f32[24,128]{1,0:T(8,128)S(1)}, u32[]{:S(2)}, u32[]{:S(2)}) collective-permute-start(f32[24,128]{1,0:T(8,128)S(1)} %get-tuple-element.25), channel_id=1, source_target_pairs={{0,1},{1,2},{2,3},{3,7},{4,0},{5,4},{6,5},{7,6},{8,9},{9,10},{10,1... | collective-permute-start | bytes 36872 | tf_op jit(solution)/shard_map/ppermute | solution.py:498

commit v7 on v6

--- a/solution.py
+++ b/solution.py
@@ -74,8 +74,8 @@
 
 def pack_kernel(
     width_x, width_y, species_in, velocity_in, diffusivity_in, parcels_in, cells_in, slots_in, face_counts_in,
-    axial_even, axial_odd, radial_one, radial_two, kept,
-    species, velocity, diffusivity, parcels, cells, slots, face_counts, moved, arrived,
+    axial_even, odd_near, odd_far, radial_parcels, kept, species, velocity, diffusivity, parcels,
+    staying, source, last, cells, slots, face_counts, moved, arrived,
 ):
     copies = [
         pltpu.make_async_copy(src, dst, arrived.at[i])
@@ -131,16 +131,16 @@
         ref, base = (
             (species, f) if f < SPECIES else (velocity, f - SPECIES) if f < FLOW else (diffusivity, 0)
         )
+        odd = [None, None]
         for layer in range(2):
             at = pl.ds((2 * f + layer) * tile, tile)
             low = ref[pl.ds(base * cells_of + layer * width_y, width_y), :]
             high = ref[pl.ds(base * cells_of + (width_x - 2 + layer) * width_y, width_y), :]
             axial_even[at, :] = jnp.where(even_x, high, low)
-            axial_odd[at, :] = jnp.where(even_x, low, high)
-            low = ref[pl.ds(base * cells_of + layer, width_x, stride=width_y), :]
-            high = ref[pl.ds(base * cells_of + width_y - 2 + layer, width_x, stride=width_y), :]
-            radial_one[at, :] = jnp.where(even_x, high, low)
-            radial_two[at, :] = jnp.where(even_x, low, high)
+            odd[layer] = low, high
+        at = pl.ds(f * tile, tile)
+        odd_near[at, :] = jnp.where(even_x, odd[0][0], odd[1][1])
+        odd_far[at, :] = jnp.where(even_x, odd[1][0], odd[0][1])
     response, evaporation = rows[4:5], rows[5:6]
     pushed = [rows[i : i + 1] + time_step * (response * (gas[i] - rows[i : i + 1])) for i in range(3)]
     pushed.append(rows[3:4] * (1.0 - time_step * evaporation))
@@ -149,14 +149,43 @@
     for i, line in enumerate(pushed):
         moved[i : i + 1, :] = line * valid
     moved[9:ROWS, :] = rows[9:ROWS] * valid
-    base = 2 * FIELDS * tile
     left_half = lax.broadcasted_iota(I32, (ROWS // 2, 2 * movers), 1) < movers
-    for packets, lo in (((axial_even, axial_odd), 0), ((radial_one, radial_two), 2 * movers)):
+    half = ROWS // 2
+    first_rows = (axial_even.shape[0] - half, odd_near.shape[0] - half)
+    for packets, starts, lo in (
+        ((axial_even, odd_near), first_rows, 0), ((radial_parcels, radial_parcels), (0, half), 2 * movers)
+    ):
         top, bottom = (moved[i : i + ROWS // 2, lo : lo + 2 * movers] for i in (0, ROWS // 2))
         up = jnp.where(left_half, top, pltpu.roll(bottom, movers, 1))
         down = jnp.where(left_half, pltpu.roll(top, movers, 1), bottom)
-        packets[0][base : base + ROWS // 2, :] = jnp.where(even_x, up, down)
-        packets[1][base : base + ROWS // 2, :] = jnp.where(even_x, down, up)
+        for ref, at, part in zip(packets, starts, (jnp.where(even_x, up, down), jnp.where(even_x, down, up))):
+            ref[at : at + half, :] = part
+
+    @pl.when(launches_first())
+    def _():
+        row = jnp.concatenate([cells[h : h + 1, :] for h in range(chunks)], axis=1)
+        push(width_x, width_y, velocity, parcels, row, kept, staying, source, last)
+
+
+def radial_kernel(
+    width_x, width_y, species, velocity, diffusivity, radial_parcels, from_even, radial_one, radial_two
+):
+    del from_even
+    cells_of, tile = width_x * width_y, width_y
+    even_x = lax.rem(lax.axis_index("axial"), 2) == 0
+    for f in range(FIELDS):
+        ref, base = (
+            (species, f) if f < SPECIES else (velocity, f - SPECIES) if f < FLOW else (diffusivity, 0)
+        )
+        for layer in range(2):
+            at = pl.ds((2 * f + layer) * tile, tile)
+            low = ref[pl.ds(base * cells_of + layer, width_x, stride=width_y), :]
+            high = ref[pl.ds(base * cells_of + width_y - 2 + layer, width_x, stride=width_y), :]
+            radial_one[at, :] = jnp.where(even_x, high, low)
+            radial_two[at, :] = jnp.where(even_x, low, high)
+    half = ROWS // 2
+    for i, ref in enumerate((radial_one, radial_two)):
+        ref[2 * FIELDS * tile :, :] = radial_parcels[i * half : (i + 1) * half, :]
 
 
 def gas_at(velocity, row_of, hot_lane, rows):
@@ -167,11 +196,10 @@
     return [pick(table[i * rows : (i + 1) * rows], row_of) for i in range(VECTORS)]
 
 
-def parcel_kernel(width_x, width_y, velocity, parcels, cells, kept, counts, staying, source):
+def push(width_x, width_y, velocity, parcels, cell, kept, staying, source, last):
     rows = width_x * width_y
     half, wide = rows // 2, 2 * LANES
     slots = parcels.shape[1]
-    cell = cells[0]
     row_of, lane_of = lax.shift_right_logical(cell, 8), lax.bitwise_and(cell, wide - 1)
     hot_lane = one_hot(lane_of, wide)
     pairs = jnp.concatenate([velocity[pl.ds(i, VECTORS * half, stride=2), :] for i in range(2)], axis=1)
@@ -179,8 +207,7 @@
     table = table[: VECTORS * half] + table[VECTORS * half :]
     gas = [pick(table[i * half : (i + 1) * half], row_of) for i in range(VECTORS)]
     chunks = slots // LANES
-    live = (lax.broadcasted_iota(I32, (1, slots), 1) < counts[...]).astype(F32)
-    keep = jnp.concatenate([kept[h : h + 1, :] for h in range(chunks)], axis=1) * live
+    keep = jnp.concatenate([kept[h : h + 1, :] for h in range(chunks)], axis=1)
     mass, response, evaporation = parcels[3:4], parcels[4:5], parcels[5:6]
     drag = [response * (gas[i] - parcels[i : i + 1]) for i in range(3)]
     for i in range(3):
@@ -192,12 +219,29 @@
     staying[9:ROWS, :] = parcels[9:ROWS] * keep
     deposits = [mass * evaporation] + [-mass * d for d in drag]
     hot_row = one_hot(row_of, half)
-    halves = [split(d * live) for d in deposits]
+    at_last = cell == rows * LANES - 1
+    for i, d in enumerate(deposits):
+        last[i : i + 1, :] = jnp.where(at_last, d, 0.0)
+    halves = [split(jnp.where(at_last, 0.0, d)) for d in deposits]
     left = jnp.concatenate([hot_row * part[i] for i in range(2) for part in halves], axis=0)
     total = dot_t(left, hot_lane)
     total = total[: 4 * half] + total[4 * half :]
     for i in range(2):
         source[pl.ds(i, 4 * half, stride=2), :] = total[:, i * LANES : (i + 1) * LANES]
+
+
+def launches_first():
+    return (lax.axis_index("axial") == 0) & (lax.axis_index("radial") == 0)
+
+
+def parcel_kernel(
+    width_x, width_y, velocity, parcels, cells, kept, staying_in, source_in, last_in, staying, source, last,
+):
+    del staying_in, source_in, last_in
+
+    @pl.when(jnp.logical_not(launches_first()))
+    def _():
+        push(width_x, width_y, velocity, parcels, cells[0], kept, staying, source, last)
 
 
 def corner_kernel(width_x, width_y, from_odd, from_even, radial_one, radial_two):
@@ -213,12 +257,10 @@
         choose = lambda v: jnp.where(has[side], jnp.where(lower_is_odd, v[1], v[0]), 0.0)
         flow, base_rate = [], []
         for y in (0, width_y - 1):
-            flow.append(
-                choose([r[pl.ds(layer * tile + y, FLOW, stride=2 * tile), :] for r in (from_even, from_odd)])
-            )
-            base_rate.append(
-                choose([r[pl.ds((2 * FLOW + layer) * tile + y, 1), :] for r in (from_even, from_odd)])
-            )
+            even = from_even[pl.ds(layer * tile + y, FLOW, stride=2 * tile), :]
+            flow.append(choose([even, from_odd[pl.ds(y, FLOW, stride=tile), :]]))
+            even = from_even[pl.ds((2 * FLOW + layer) * tile + y, 1), :]
+            base_rate.append(choose([even, from_odd[pl.ds(FLOW * tile + y, 1), :]]))
         for ref, high in ((radial_one, even_x), (radial_two, jnp.logical_not(even_x))):
             ref[side * tile : side * tile + FLOW, :] = jnp.where(high, flow[1], flow[0])
             ref[2 * tile + side : 2 * tile + side + 1, :] = jnp.where(high, base_rate[1], base_rate[0])
@@ -230,11 +272,14 @@
 
 
 def stencil_kernel(
-    width_x, width_y, species, velocity, diffusivity, from_odd, from_even, beside_two, beside_one, source, staying,
-    staying_out, state, result, arrivals, sent,
+    width_x, width_y, species, velocity, diffusivity, from_odd, odd_far, from_even, beside_two, beside_one, source, staying, last, counts,
+    staying_out, state, result, arrivals, live_staying, sent,
 ):
-    copy = pltpu.make_async_copy(staying, staying_out, sent)
+    live = lax.broadcasted_iota(I32, (1, staying.shape[1]), 1) < counts[...]
+    live_staying[...] = jnp.where(live, staying[...], 0.0)
+    copy = pltpu.make_async_copy(live_staying, staying_out, sent)
     copy.start()
+    last_sum = jnp.sum(jnp.where(live, last[...], 0.0), axis=1, keepdims=True)
     tile = width_y
     rows = width_x * width_y
     depth = LANES
@@ -254,12 +299,16 @@
         base = index * tile
         return [state[part, base + i : base + i + 1, :].reshape(1, 1, depth) for i in range(tile)]
 
-    def axial_halo(lo, n):
-        a, b = from_even[lo : lo + n, :], from_odd[lo : lo + n, :]
+    def axial_halo(even, odd_low, odd_high):
         return (
-            jnp.where(has_x[0], jnp.where(even_x, b, a), 0.0),
-            jnp.where(has_x[1], jnp.where(even_x, a, b), 0.0),
+            jnp.where(has_x[0], jnp.where(even_x, odd_low, even), 0.0),
+            jnp.where(has_x[1], jnp.where(even_x, even, odd_high), 0.0),
         )
+
+    def axial_layers(f):
+        even = from_even[2 * f * tile : 2 * (f + 1) * tile, :]
+        near, far = (ref[f * tile : (f + 1) * tile, :] for ref in (from_odd, odd_far))
+        return axial_halo(even, jnp.concatenate([far, near], axis=0), jnp.concatenate([near, far], axis=0))
 
     def radial_halo(lo, n):
         a, b = beside_one[lo : lo + n, :], beside_two[lo : lo + n, :]
@@ -270,7 +319,9 @@
 
     movers = arrivals.shape[-1]
     base = 2 * FIELDS * tile
-    for side, parts in ((0, axial_halo(base, ROWS // 2)), (2, radial_halo(base, ROWS // 2))):
+    odd_parcels = from_odd[FIELDS * tile :, :]
+    axial_parcels = axial_halo(from_even[base:, :], odd_parcels, odd_parcels)
+    for side, parts in ((0, axial_parcels), (2, radial_halo(base, ROWS // 2))):
         for i, part in enumerate(parts):
             arrivals[side + i, : ROWS // 2] = part[:, :movers]
             arrivals[side + i, ROWS // 2 :] = part[:, movers : 2 * movers]
@@ -304,7 +355,7 @@
     long, sides = [], []
     for f in range(FIELDS):
         ref, at = (species, f) if f < SPECIES else (velocity, f - SPECIES) if f < FLOW else (diffusivity, 0)
-        low, high = (h.reshape(2, tile, depth) for h in axial_halo(2 * f * tile, 2 * tile))
+        low, high = (h.reshape(2, tile, depth) for h in axial_layers(f))
         main = ref[at * rows : (at + 1) * rows, :].reshape(width_x, tile, depth)
         long.append(jnp.concatenate([low, main, high], axis=0))
         low, high = (h.reshape(2, tile, depth) for h in radial_halo(2 * f * tile, 2 * tile))
@@ -377,6 +428,7 @@
     for s in range(2):
         keep(5, s, later_side[s])
 
+    at_last = (row[0] == tile - 1) & (lane[0] == depth - 1)
     scale = 0.5
     half = 0.5 * half
     inner = later[1:-1]
@@ -404,6 +456,9 @@
         if part is not None:
             value = value + time_step * source[part * rows : (part + 1) * rows, :]
         result[f] = value
+        if part is not None:
+            end = value[-tile:] + jnp.where(at_last, time_step * last_sum[part : part + 1], 0.0)
+            result[f, rows - tile :, :] = end
     copy.wait()
 
 
@@ -470,7 +525,7 @@
         copy.wait()
 
 
-def call(kernel, outs, ins, flops, name, scratch=(), far_ins=(), far_outs=()):
+def call(kernel, outs, ins, flops, name, scratch=(), far_ins=(), far_outs=(), aliases=None):
     vmem, far = (pl.BlockSpec(memory_space=m) for m in (pltpu.VMEM, pltpu.HBM))
     moved = sum(int(np.prod(x.shape)) * 4 for x in list(ins) + list(outs))
     ins = [pltpu.with_memory_space_constraint(x, pltpu.HBM) if i in far_ins else x for i, x in enumerate(ins)]
@@ -482,6 +537,7 @@
         scratch_shapes=list(scratch),
         compiler_params=pltpu.CompilerParams(vmem_limit_bytes=VMEM_LIMIT),
         cost_estimate=pl.CostEstimate(flops=flops, bytes_accessed=moved, transcendentals=0),
+        input_output_aliases=aliases or {},
         name=name,
     )(*ins)
 
@@ -500,7 +556,9 @@
     velocity2 = velocity.reshape(VECTORS * rows, depth)
     diffusivity2 = diffusivity.reshape(rows, depth)
     parcels2 = parcels.reshape(ROWS, slots)
-    packet_rows = 2 * FIELDS * width_y + ROWS // 2
+    odd_rows = FIELDS * width_y
+    pushed = [f32(ROWS, slots), f32(4 * rows, depth), f32(4, slots)]
+    packet_rows = 2 * odd_rows + ROWS // 2
     chunks = slots // LANES
 
     def near(x):
@@ -509,31 +567,39 @@
     fields = [species2, velocity2, diffusivity2]
     cells2 = cells.reshape(chunks, LANES)
     slots2 = leave_slots.reshape(4, movers)
-    axial_even, axial_odd, radial_one, radial_two, kept = call(
+    axial_even, odd_near, odd_far, radial_parcels, kept, *fields, parcels2, staying, source, last = call(
         functools.partial(pack_kernel, width_x, width_y),
-        [f32(packet_rows, depth)] * 4 + [f32(chunks, LANES)],
+        [f32(n, depth) for n in (packet_rows, odd_rows + ROWS // 2, odd_rows, ROWS)]
+        + [f32(chunks, LANES)] + [f32(*x.shape) for x in fields + [parcels2]] + pushed,
         fields + [parcels2, cells2, slots2, leave_counts],
         10**8, "pack_faces", far_ins=range(7),
-        scratch=[near(x) for x in fields + [parcels2, cells2, slots2]]
-        + [pltpu.SMEM(leave_counts.shape, I32), near(f32(ROWS, 4 * movers)), pltpu.SemaphoreType.DMA((7,))],
-    )
-    from_odd = permute(axial_odd, axial_swap(sizes, True))
+        scratch=[
+            near(cells2), near(slots2), pltpu.SMEM(leave_counts.shape, I32), near(f32(ROWS, 4 * movers)),
+            pltpu.SemaphoreType.DMA((7,)),
+        ],
+    )
+    velocity2 = fields[1]
+    from_odd = permute(odd_near, axial_swap(sizes, True))
+    odd_far = permute(odd_far, axial_swap(sizes, True))
     from_even = permute(axial_even, axial_swap(sizes, False))
+    radial_one, radial_two = call(
+        functools.partial(radial_kernel, width_x, width_y),
+        [f32(packet_rows, depth)] * 2, fields + [radial_parcels, from_even], 10**6, "pack_radial",
+    )
     beside_one = permute(radial_one, radial_shift(sizes, True))
     beside_two = permute(radial_two, radial_shift(sizes, False))
-    counts, kept = lax.optimization_barrier((counts, kept))
-    staying, source = call(
-        functools.partial(parcel_kernel, width_x, width_y),
-        [f32(ROWS, slots), f32(4 * rows, depth)],
-        [velocity2, parcels2, cells.reshape(1, 1, slots), kept, counts],
-        10**9, "push_parcels",
-    )
+    staying, source, last = call(
+        functools.partial(parcel_kernel, width_x, width_y), pushed,
+        [velocity2, parcels2, cells.reshape(1, 1, slots), kept, staying, source, last],
+        10**9, "push_parcels", aliases={4: 0, 5: 1, 6: 2},
+    )
+    counts, last = lax.optimization_barrier((counts, last))
     state = f32(6, 2 * (FLOW + 1) * width_y, depth)
     staying, state, result, arrivals = call(
         functools.partial(stencil_kernel, width_x, width_y),
         [f32(ROWS, slots), state, f32(FLOW, rows, depth), f32(4, ROWS, movers)],
-        fields + [from_odd, from_even, beside_two, beside_one, source, staying],
-        10**7, "stencils", far_outs=(0,), scratch=[pltpu.SemaphoreType.DMA],
+        fields + [from_odd, odd_far, from_even, beside_two, beside_one, source, staying, last, counts],
+        10**7, "stencils", far_outs=(0,), scratch=[near(f32(ROWS, slots)), pltpu.SemaphoreType.DMA],
     )
     corner_one, corner_two = call(
         functools.partial(corner_kernel, width_x, width_y),

time: 12.7 us -> 12.4 us (0.976)
  the two profiles are of different devices: /device:TPU:0 before, /device:TPU:3 now
where the time goes in v7:
time: 12.4 us; the launch traced here: 12.2 us
  starting transfers between devices  6.02 us (49%)
  Pallas kernels  3.86 us (31%)
  between operations  1.36 us (11%)
  waiting for transfers between devices  0.97 us (8%)
    ppermute x7, starting transfers between devices, body(): permute = lambda x, pairs: lax.ppermute(x, AXES, pairs)  6.02 us
    pallas_call x6, Pallas kernels, call(): pl.pallas_call(kernel, out_shape=[jax.ShapeDtypeStruct(s.shape, s.dtype)...  3.86 us
    ppermute x7, waiting for transfers between devices, body(): permute = lambda x, pairs: lax.ppermute(x, AXES, pairs)  0.97 us
  transfers between devices with their start and end apart: 7, of which 2 were waited for; matrix products, arithmetic and copies ran while one was open for 0% of the time, Pallas kernels for 13%

profile of v7, /device:TPU:3, one launch (start us, length us, event | category | flops | bytes accessed | tf_op | source)
XLA Modules:
  0.0 12.2 jit_solution(14035771717021418010)
XLA Ops:
  0.6 1.4 %pack_faces.1 = (f32[152,128]{1,0:T(8,128)S(1)}, f32[80,128]{1,0:T(8,128)S(1)}, f32[72,128]{1,0:T(8,128)S(1)}, f32[16,128]{1,0:T(8,128)S(1)}, f32[16,128]{1,0:T(...) custom-call(f32[320,128]{1,0:T(8,128)} %bitcast.11, ...), custom_call_target="tpu_custom_call" | custom-call | flops 100000000 | bytes 1328144 | tf_op jit(solution)/shard_map/pack_faces/pallas_call | solution.py:532
  2.1 0.7 %collective-permute-start.1 = (f32[152,128]{1,0:T(8,128)S(1)}, f32[152,128]{1,0:T(8,128)S(1)}, u32[]{:S(2)}, u32[]{:S(2)}) collective-permute-start(f32[152,128]{1,0:T(8,128)S(1)} %get-tuple-element.33), channel_id=1, source_target_pairs={{0,4},{1,5},{2,6},{3,7},{4,0},{5,1},{6,2},{7,3},{8,12},{9,13},{10,... | collective-permute-start | bytes 233480 | tf_op jit(solution)/shard_map/ppermute | solution.py:554
  2.8 1.2 %collective-permute-start = (f32[80,128]{1,0:T(8,128)S(1)}, f32[80,128]{1,0:T(8,128)S(1)}, u32[]{:S(2)}, u32[]{:S(2)}) collective-permute-start(f32[80,128]{1,0:T(8,128)S(1)} %get-tuple-element.32), channel_id=1, source_target_pairs={{0,1},{1,0},{2,3},{3,2},{4,8},{5,9},{6,10},{7,11},{8,4},{9,5},{10,... | collective-permute-start | bytes 122888 | tf_op jit(solution)/shard_map/ppermute | solution.py:554
  4.0 1.5 %collective-permute-start.4 = (f32[72,128]{1,0:T(8,128)S(1)}, f32[72,128]{1,0:T(8,128)S(1)}, u32[]{:S(2)}, u32[]{:S(2)}) collective-permute-start(f32[72,128]{1,0:T(8,128)S(1)} %get-tuple-element.39), channel_id=1, source_target_pairs={{0,1},{1,0},{2,3},{3,2},{4,8},{5,9},{6,10},{7,11},{8,4},{9,5},{10,... | collective-permute-start | bytes 110600 | tf_op jit(solution)/shard_map/ppermute | solution.py:554
  5.5 0.0 collective-permute-done.1.from_even
  5.5 1.3 %collective-permute-start.5 = (f32[152,128]{1,0:T(8,128)S(1)}, f32[152,128]{1,0:T(8,128)S(1)}, u32[]{:S(2)}, u32[]{:S(2)}) collective-permute-start(f32[152,128]{1,0:T(8,128)S(1)} %get-tuple-element.41), channel_id=1, source_target_pairs={{0,4},{1,0},{2,1},{3,2},{4,5},{5,6},{6,7},{7,3},{8,12},{9,8},{10,9... | collective-permute-start | bytes 233480 | tf_op jit(solution)/shard_map/ppermute | solution.py:554
  6.8 0.0 collective-permute-start.6
  6.8 0.7 %collective-permute-done.from_odd = f32[80,128]{1,0:T(8,128)S(1)} collective-permute-done((f32[80,128]{1,0:T(8,128)S(1)}, f32[80,128]{1,0:T(8,128)S(1)}, u32[]{:S(2)}, u32[]{:S(2)}) %collective-permute-start) | collective-permute-done | bytes 40992 | tf_op jit(solution)/shard_map/ppermute | solution.py:554
  7.6 0.0 copy-start
  7.6 1.3 %collective-permute-start.2 = (f32[24,128]{1,0:T(8,128)S(1)}, f32[24,128]{1,0:T(8,128)S(1)}, u32[]{:S(2)}, u32[]{:S(2)}) collective-permute-start(f32[24,128]{1,0:T(8,128)S(1)} %get-tuple-element.34), channel_id=1, source_target_pairs={{0,4},{1,0},{2,1},{3,2},{4,5},{5,6},{6,7},{7,3},{8,12},{9,8},{10,9... | collective-permute-start | bytes 36872 | tf_op jit(solution)/shard_map/ppermute | solution.py:554
  8.9 0.0 collective-permute-start.3
  8.9 0.0 copy-done
  8.9 0.8 %push_parcels.1 = (f32[16,2048]{1,0:T(8,128)S(1)}, f32[256,128]{1,0:T(8,128)S(1)}, f32[4,2048]{1,0:T(4,128)S(1)}) custom-call(f32[192,128]{1,0:T(8,128)S(1)} %get-tuple-element.37.velocity, f32[16,2048]{1,0:T(8,128)S(1)} %get-tuple-element.43.parcels, s32[1,1,2048]{2,1,0:T(1,128)S(1)} %copy-done, ...), custom_call_target="tpu_custom_call", output_to_operand_aliasing={{0}: (4, {}), {1}: (5, {}), {2}: (6, {})} | custom-call | flops 1000000000 | bytes 835584 | tf_op jit(solution)/shard_map/push_parcels/pallas_call | solution.py:532
  10.4 0.0 collective-permute-done.4.odd_far
  10.4 0.0 collective-permute-done.5.beside_two
  10.4 0.0 collective-permute-done.6.beside_one
  10.4 0.8 %stencils.1 = (f32[16,2048]{1,0:T(8,128)}, f32[6,144,128]{2,1,0:T(8,128)S(1)}, f32[8,64,128]{2,1,0:T(8,128)S(1)}, f32[4,16,64]{2,1,0:T(8,128)S(1)}) custom-call(f32[320,128]{1,0:T(8,128)S(1)} %get-tuple-element.36.species, f32[192,128]{1,0:T(8,128)S(1)} %get-tuple-element.37.velocity, f32[64,128]{1,0:T(8,128)S(1)} %get-tuple-element.38.diffusivity, ...), custom_call_target="tpu_custom_call" | custom-call | flops 10000000 | bytes 1753092 | tf_op jit(solution)/shard_map/stencils/pallas_call | solution.py:532
  11.2 0.0 collective-permute-done.2.corner_two
  11.2 0.2 %collective-permute-done.3.corner_one = f32[24,128]{1,0:T(8,128)S(1)} collective-permute-done((f32[24,128]{1,0:T(8,128)S(1)}, f32[24,128]{1,0:T(8,128)S(1)}, u32[]{:S(2)}, u32[]{:S(2)}) %collective-permute-start.3) | collective-permute-done | bytes 12320 | tf_op jit(solution)/shard_map/ppermute | solution.py:554
  11.4 0.8 %ends.1 = (f32[5,64,128]{2,1,0:T(8,128)}, f32[3,64,128]{2,1,0:T(8,128)}, f32[4,16,64]{2,1,0:T(8,128)}) custom-call(f32[24,128]{1,0:T(8,128)S(1)} %collective-permute-done.2.corner_two, f32[24,128]{1,0:T(8,128)S(1)} %collective-permute-done.3.corner_one, f32[6,144,128]{2,1,0:T(8,128)S(1)} %get-tuple-element.53.state, ...), custom_call_target="tpu_custom_call" | custom-call | flops 1000000 | bytes 1024000 | tf_op jit(solution)/shard_map/ends/pallas_call | solution.py:532
  (2 shorter events, 0.0 us)
Async XLA Ops:
  2.1 3.4 %collective-permute-start.1 = (f32[152,128]{1,0:T(8,128)S(1)}, f32[152,128]{1,0:T(8,128)S(1)}, u32[]{:S(2)}, u32[]{:S(2)}) collective-permute-start(f32[152,128]{1,0:T(8,128)S(1)} %get-tuple-element.33), channel_id=1, source_target_pairs={{0,4},{1,5},{2,6},{3,7},{4,0},{5,1},{6,2},{7,3},{8,12},{9,13},{10,... | collective-permute-start | bytes 233480 | tf_op jit(solution)/shard_map/ppermute | solution.py:554
  2.8 4.7 %collective-permute-start = (f32[80,128]{1,0:T(8,128)S(1)}, f32[80,128]{1,0:T(8,128)S(1)}, u32[]{:S(2)}, u32[]{:S(2)}) collective-permute-start(f32[80,128]{1,0:T(8,128)S(1)} %get-tuple-element.32), channel_id=1, source_target_pairs={{0,1},{1,0},{2,3},{3,2},{4,8},{5,9},{6,10},{7,11},{8,4},{9,5},{10,... | collective-permute-start | bytes 122888 | tf_op jit(solution)/shard_map/ppermute | solution.py:554
  4.0 6.4 %collective-permute-start.4 = (f32[72,128]{1,0:T(8,128)S(1)}, f32[72,128]{1,0:T(8,128)S(1)}, u32[]{:S(2)}, u32[]{:S(2)}) collective-permute-start(f32[72,128]{1,0:T(8,128)S(1)} %get-tuple-element.39), channel_id=1, source_target_pairs={{0,1},{1,0},{2,3},{3,2},{4,8},{5,9},{6,10},{7,11},{8,4},{9,5},{10,... | collective-permute-start | bytes 110600 | tf_op jit(solution)/shard_map/ppermute | solution.py:554
  5.5 4.9 %collective-permute-start.5 = (f32[152,128]{1,0:T(8,128)S(1)}, f32[152,128]{1,0:T(8,128)S(1)}, u32[]{:S(2)}, u32[]{:S(2)}) collective-permute-start(f32[152,128]{1,0:T(8,128)S(1)} %get-tuple-element.41), channel_id=1, source_target_pairs={{0,4},{1,0},{2,1},{3,2},{4,5},{5,6},{6,7},{7,3},{8,12},{9,8},{10,9... | collective-permute-start | bytes 233480 | tf_op jit(solution)/shard_map/ppermute | solution.py:554
  6.8 3.6 %collective-permute-start.6 = (f32[152,128]{1,0:T(8,128)S(1)}, f32[152,128]{1,0:T(8,128)S(1)}, u32[]{:S(2)}, u32[]{:S(2)}) collective-permute-start(f32[152,128]{1,0:T(8,128)S(1)} %get-tuple-element.42), channel_id=1, source_target_pairs={{0,1},{1,2},{2,3},{3,7},{4,0},{5,4},{6,5},{7,6},{8,9},{9,10},{10,1... | collective-permute-start | bytes 233480 | tf_op jit(solution)/shard_map/ppermute | solution.py:554
  7.6 1.3 %copy-start = (s32[1,1,2048]{2,1,0:T(1,128)S(1)}, s32[1,1,2048]{2,1,0:T(1,128)}, u32[]{:S(2)}) copy-start(s32[1,1,2048]{2,1,0:T(1,128)} %cells.1) | copy-start | bytes 24580
  7.6 3.6 %collective-permute-start.2 = (f32[24,128]{1,0:T(8,128)S(1)}, f32[24,128]{1,0:T(8,128)S(1)}, u32[]{:S(2)}, u32[]{:S(2)}) collective-permute-start(f32[24,128]{1,0:T(8,128)S(1)} %get-tuple-element.34), channel_id=1, source_target_pairs={{0,4},{1,0},{2,1},{3,2},{4,5},{5,6},{6,7},{7,3},{8,12},{9,8},{10,9... | collective-permute-start | bytes 36872 | tf_op jit(solution)/shard_map/ppermute | solution.py:554
  8.9 2.5 %collective-permute-start.3 = (f32[24,128]{1,0:T(8,128)S(1)}, f32[24,128]{1,0:T(8,128)S(1)}, u32[]{:S(2)}, u32[]{:S(2)}) collective-permute-start(f32[24,128]{1,0:T(8,128)S(1)} %get-tuple-element.35), channel_id=1, source_target_pairs={{0,1},{1,2},{2,3},{3,7},{4,0},{5,4},{6,5},{7,6},{8,9},{9,10},{10,1... | collective-permute-start | bytes 36872 | tf_op jit(solution)/shard_map/ppermute | solution.py:554

commit v8 on v7

--- a/solution.py
+++ b/solution.py
@@ -237,9 +237,15 @@
 def parcel_kernel(
     width_x, width_y, velocity, parcels, cells, kept, staying_in, source_in, last_in, staying, source, last,
 ):
-    del staying_in, source_in, last_in
-
-    @pl.when(jnp.logical_not(launches_first()))
+    done = launches_first()
+
+    @pl.when(done)
+    def _():
+        staying[...] = staying_in[...]
+        source[...] = source_in[...]
+        last[...] = last_in[...]
+
+    @pl.when(jnp.logical_not(done))
     def _():
         push(width_x, width_y, velocity, parcels, cells[0], kept, staying, source, last)
 
@@ -525,7 +531,7 @@
         copy.wait()
 
 
-def call(kernel, outs, ins, flops, name, scratch=(), far_ins=(), far_outs=(), aliases=None):
+def call(kernel, outs, ins, flops, name, scratch=(), far_ins=(), far_outs=()):
     vmem, far = (pl.BlockSpec(memory_space=m) for m in (pltpu.VMEM, pltpu.HBM))
     moved = sum(int(np.prod(x.shape)) * 4 for x in list(ins) + list(outs))
     ins = [pltpu.with_memory_space_constraint(x, pltpu.HBM) if i in far_ins else x for i, x in enumerate(ins)]
@@ -537,7 +543,6 @@
         scratch_shapes=list(scratch),
         compiler_params=pltpu.CompilerParams(vmem_limit_bytes=VMEM_LIMIT),
         cost_estimate=pl.CostEstimate(flops=flops, bytes_accessed=moved, transcendentals=0),
-        input_output_aliases=aliases or {},
         name=name,
     )(*ins)
 
@@ -591,7 +596,7 @@
     staying, source, last = call(
         functools.partial(parcel_kernel, width_x, width_y), pushed,
         [velocity2, parcels2, cells.reshape(1, 1, slots), kept, staying, source, last],
-        10**9, "push_parcels", aliases={4: 0, 5: 1, 6: 2},
+        10**9, "push_parcels",
     )
     counts, last = lax.optimization_barrier((counts, last))
     state = f32(6, 2 * (FLOW + 1) * width_y, depth)

time: 12.4 us -> 12.4 us (level)
  transfers between devices with their start and end apart: 7 -> 7, of which waited for: 2 -> 2; matrix products, arithmetic and copies ran while one was open for 0% -> 0% of each run, Pallas kernels for 13% -> 14%
where the time goes in v8:
time: 12.4 us; the launch traced here: 12.2 us
  starting transfers between devices  6.02 us (49%)
  Pallas kernels  3.86 us (31%)
  between operations  1.36 us (11%)
  waiting for transfers between devices  0.97 us (8%)
    ppermute x7, starting transfers between devices, body(): permute = lambda x, pairs: lax.ppermute(x, AXES, pairs)  6.02 us
    pallas_call x6, Pallas kernels, call(): pl.pallas_call(kernel, out_shape=[jax.ShapeDtypeStruct(s.shape, s.dtype)...  3.86 us
    ppermute x7, waiting for transfers between devices, body(): permute = lambda x, pairs: lax.ppermute(x, AXES, pairs)  0.97 us
  transfers between devices with their start and end apart: 7, of which 2 were waited for; matrix products, arithmetic and copies ran while one was open for 0% of the time, Pallas kernels for 14%

profile of v8, /device:TPU:3, one launch (start us, length us, event | category | flops | bytes accessed | tf_op | source)
XLA Modules:
  0.0 12.2 jit_solution(15808252107212747616)
XLA Ops:
  0.6 1.4 %pack_faces.1 = (f32[152,128]{1,0:T(8,128)S(1)}, f32[80,128]{1,0:T(8,128)S(1)}, f32[72,128]{1,0:T(8,128)S(1)}, f32[16,128]{1,0:T(8,128)S(1)}, f32[16,128]{1,0:T(...) custom-call(f32[320,128]{1,0:T(8,128)} %bitcast.11, ...), custom_call_target="tpu_custom_call" | custom-call | flops 100000000 | bytes 1328144 | tf_op jit(solution)/shard_map/pack_faces/pallas_call | solution.py:538
  2.1 0.7 %collective-permute-start.1 = (f32[152,128]{1,0:T(8,128)S(1)}, f32[152,128]{1,0:T(8,128)S(1)}, u32[]{:S(2)}, u32[]{:S(2)}) collective-permute-start(f32[152,128]{1,0:T(8,128)S(1)} %get-tuple-element.33), channel_id=1, source_target_pairs={{0,4},{1,5},{2,6},{3,7},{4,0},{5,1},{6,2},{7,3},{8,12},{9,13},{10,... | collective-permute-start | bytes 233480 | tf_op jit(solution)/shard_map/ppermute | solution.py:559
  2.8 1.2 %collective-permute-start = (f32[80,128]{1,0:T(8,128)S(1)}, f32[80,128]{1,0:T(8,128)S(1)}, u32[]{:S(2)}, u32[]{:S(2)}) collective-permute-start(f32[80,128]{1,0:T(8,128)S(1)} %get-tuple-element.32), channel_id=1, source_target_pairs={{0,1},{1,0},{2,3},{3,2},{4,8},{5,9},{6,10},{7,11},{8,4},{9,5},{10,... | collective-permute-start | bytes 122888 | tf_op jit(solution)/shard_map/ppermute | solution.py:559
  4.0 1.5 %collective-permute-start.4 = (f32[72,128]{1,0:T(8,128)S(1)}, f32[72,128]{1,0:T(8,128)S(1)}, u32[]{:S(2)}, u32[]{:S(2)}) collective-permute-start(f32[72,128]{1,0:T(8,128)S(1)} %get-tuple-element.39), channel_id=1, source_target_pairs={{0,1},{1,0},{2,3},{3,2},{4,8},{5,9},{6,10},{7,11},{8,4},{9,5},{10,... | collective-permute-start | bytes 110600 | tf_op jit(solution)/shard_map/ppermute | solution.py:559
  5.5 0.0 collective-permute-done.1.from_even
  5.5 1.3 %collective-permute-start.5 = (f32[152,128]{1,0:T(8,128)S(1)}, f32[152,128]{1,0:T(8,128)S(1)}, u32[]{:S(2)}, u32[]{:S(2)}) collective-permute-start(f32[152,128]{1,0:T(8,128)S(1)} %get-tuple-element.41), channel_id=1, source_target_pairs={{0,4},{1,0},{2,1},{3,2},{4,5},{5,6},{6,7},{7,3},{8,12},{9,8},{10,9... | collective-permute-start | bytes 233480 | tf_op jit(solution)/shard_map/ppermute | solution.py:559
  6.8 0.0 collective-permute-start.6
  6.8 0.7 %collective-permute-done.from_odd = f32[80,128]{1,0:T(8,128)S(1)} collective-permute-done((f32[80,128]{1,0:T(8,128)S(1)}, f32[80,128]{1,0:T(8,128)S(1)}, u32[]{:S(2)}, u32[]{:S(2)}) %collective-permute-start) | collective-permute-done | bytes 40992 | tf_op jit(solution)/shard_map/ppermute | solution.py:559
  7.6 0.0 copy-start
  7.6 1.3 %collective-permute-start.2 = (f32[24,128]{1,0:T(8,128)S(1)}, f32[24,128]{1,0:T(8,128)S(1)}, u32[]{:S(2)}, u32[]{:S(2)}) collective-permute-start(f32[24,128]{1,0:T(8,128)S(1)} %get-tuple-element.34), channel_id=1, source_target_pairs={{0,4},{1,0},{2,1},{3,2},{4,5},{5,6},{6,7},{7,3},{8,12},{9,8},{10,9... | collective-permute-start | bytes 36872 | tf_op jit(solution)/shard_map/ppermute | solution.py:559
  8.9 0.0 collective-permute-start.3
  8.9 0.0 copy-done
  8.9 0.8 %push_parcels.1 = (f32[16,2048]{1,0:T(8,128)S(1)}, f32[256,128]{1,0:T(8,128)S(1)}, f32[4,2048]{1,0:T(4,128)S(1)}) custom-call(f32[192,128]{1,0:T(8,128)S(1)} %get-tuple-element.37.velocity, f32[16,2048]{1,0:T(8,128)S(1)} %get-tuple-element.43.parcels, s32[1,1,2048]{2,1,0:T(1,128)S(1)} %copy-done, f32[16,128]{1,0:T(8,128)S(1)} %get-tuple-element.44.kept, ...), custom_call_target="tpu_custom_call" | custom-call | flops 1000000000 | bytes 835584 | tf_op jit(solution)/shard_map/push_parcels/pallas_call | solution.py:538
  10.4 0.0 collective-permute-done.4.odd_far
  10.4 0.0 collective-permute-done.5.beside_two
  10.4 0.0 collective-permute-done.6.beside_one
  10.4 0.8 %stencils.1 = (f32[16,2048]{1,0:T(8,128)}, f32[6,144,128]{2,1,0:T(8,128)S(1)}, f32[8,64,128]{2,1,0:T(8,128)S(1)}, f32[4,16,64]{2,1,0:T(8,128)S(1)}) custom-call(f32[320,128]{1,0:T(8,128)S(1)} %get-tuple-element.36.species, f32[192,128]{1,0:T(8,128)S(1)} %get-tuple-element.37.velocity, f32[64,128]{1,0:T(8,128)S(1)} %get-tuple-element.38.diffusivity, ...), custom_call_target="tpu_custom_call" | custom-call | flops 10000000 | bytes 1753092 | tf_op jit(solution)/shard_map/stencils/pallas_call | solution.py:538
  11.2 0.0 collective-permute-done.2.corner_two
  11.2 0.2 %collective-permute-done.3.corner_one = f32[24,128]{1,0:T(8,128)S(1)} collective-permute-done((f32[24,128]{1,0:T(8,128)S(1)}, f32[24,128]{1,0:T(8,128)S(1)}, u32[]{:S(2)}, u32[]{:S(2)}) %collective-permute-start.3) | collective-permute-done | bytes 12320 | tf_op jit(solution)/shard_map/ppermute | solution.py:559
  11.4 0.8 %ends.1 = (f32[5,64,128]{2,1,0:T(8,128)}, f32[3,64,128]{2,1,0:T(8,128)}, f32[4,16,64]{2,1,0:T(8,128)}) custom-call(f32[24,128]{1,0:T(8,128)S(1)} %collective-permute-done.2.corner_two, f32[24,128]{1,0:T(8,128)S(1)} %collective-permute-done.3.corner_one, f32[6,144,128]{2,1,0:T(8,128)S(1)} %get-tuple-element.53.state, ...), custom_call_target="tpu_custom_call" | custom-call | flops 1000000 | bytes 1024000 | tf_op jit(solution)/shard_map/ends/pallas_call | solution.py:538
  (2 shorter events, 0.0 us)
Async XLA Ops:
  2.1 3.4 %collective-permute-start.1 = (f32[152,128]{1,0:T(8,128)S(1)}, f32[152,128]{1,0:T(8,128)S(1)}, u32[]{:S(2)}, u32[]{:S(2)}) collective-permute-start(f32[152,128]{1,0:T(8,128)S(1)} %get-tuple-element.33), channel_id=1, source_target_pairs={{0,4},{1,5},{2,6},{3,7},{4,0},{5,1},{6,2},{7,3},{8,12},{9,13},{10,... | collective-permute-start | bytes 233480 | tf_op jit(solution)/shard_map/ppermute | solution.py:559
  2.8 4.7 %collective-permute-start = (f32[80,128]{1,0:T(8,128)S(1)}, f32[80,128]{1,0:T(8,128)S(1)}, u32[]{:S(2)}, u32[]{:S(2)}) collective-permute-start(f32[80,128]{1,0:T(8,128)S(1)} %get-tuple-element.32), channel_id=1, source_target_pairs={{0,1},{1,0},{2,3},{3,2},{4,8},{5,9},{6,10},{7,11},{8,4},{9,5},{10,... | collective-permute-start | bytes 122888 | tf_op jit(solution)/shard_map/ppermute | solution.py:559
  4.0 6.4 %collective-permute-start.4 = (f32[72,128]{1,0:T(8,128)S(1)}, f32[72,128]{1,0:T(8,128)S(1)}, u32[]{:S(2)}, u32[]{:S(2)}) collective-permute-start(f32[72,128]{1,0:T(8,128)S(1)} %get-tuple-element.39), channel_id=1, source_target_pairs={{0,1},{1,0},{2,3},{3,2},{4,8},{5,9},{6,10},{7,11},{8,4},{9,5},{10,... | collective-permute-start | bytes 110600 | tf_op jit(solution)/shard_map/ppermute | solution.py:559
  5.5 4.9 %collective-permute-start.5 = (f32[152,128]{1,0:T(8,128)S(1)}, f32[152,128]{1,0:T(8,128)S(1)}, u32[]{:S(2)}, u32[]{:S(2)}) collective-permute-start(f32[152,128]{1,0:T(8,128)S(1)} %get-tuple-element.41), channel_id=1, source_target_pairs={{0,4},{1,0},{2,1},{3,2},{4,5},{5,6},{6,7},{7,3},{8,12},{9,8},{10,9... | collective-permute-start | bytes 233480 | tf_op jit(solution)/shard_map/ppermute | solution.py:559
  6.8 3.6 %collective-permute-start.6 = (f32[152,128]{1,0:T(8,128)S(1)}, f32[152,128]{1,0:T(8,128)S(1)}, u32[]{:S(2)}, u32[]{:S(2)}) collective-permute-start(f32[152,128]{1,0:T(8,128)S(1)} %get-tuple-element.42), channel_id=1, source_target_pairs={{0,1},{1,2},{2,3},{3,7},{4,0},{5,4},{6,5},{7,6},{8,9},{9,10},{10,1... | collective-permute-start | bytes 233480 | tf_op jit(solution)/shard_map/ppermute | solution.py:559
  7.6 1.3 %copy-start = (s32[1,1,2048]{2,1,0:T(1,128)S(1)}, s32[1,1,2048]{2,1,0:T(1,128)}, u32[]{:S(2)}) copy-start(s32[1,1,2048]{2,1,0:T(1,128)} %cells.1) | copy-start | bytes 24580
  7.6 3.6 %collective-permute-start.2 = (f32[24,128]{1,0:T(8,128)S(1)}, f32[24,128]{1,0:T(8,128)S(1)}, u32[]{:S(2)}, u32[]{:S(2)}) collective-permute-start(f32[24,128]{1,0:T(8,128)S(1)} %get-tuple-element.34), channel_id=1, source_target_pairs={{0,4},{1,0},{2,1},{3,2},{4,5},{5,6},{6,7},{7,3},{8,12},{9,8},{10,9... | collective-permute-start | bytes 36872 | tf_op jit(solution)/shard_map/ppermute | solution.py:559
  8.9 2.5 %collective-permute-start.3 = (f32[24,128]{1,0:T(8,128)S(1)}, f32[24,128]{1,0:T(8,128)S(1)}, u32[]{:S(2)}, u32[]{:S(2)}) collective-permute-start(f32[24,128]{1,0:T(8,128)S(1)} %get-tuple-element.35), channel_id=1, source_target_pairs={{0,1},{1,2},{2,3},{3,7},{4,0},{5,4},{6,5},{7,6},{8,9},{9,10},{10,1... | collective-permute-start | bytes 36872 | tf_op jit(solution)/shard_map/ppermute | solution.py:559

commit v9 on v8

--- a/solution.py
+++ b/solution.py
@@ -151,9 +151,9 @@
     moved[9:ROWS, :] = rows[9:ROWS] * valid
     left_half = lax.broadcasted_iota(I32, (ROWS // 2, 2 * movers), 1) < movers
     half = ROWS // 2
-    first_rows = (axial_even.shape[0] - half, odd_near.shape[0] - half)
+    first_rows = (axial_even.shape[0] - half, odd_far.shape[0] - half)
     for packets, starts, lo in (
-        ((axial_even, odd_near), first_rows, 0), ((radial_parcels, radial_parcels), (0, half), 2 * movers)
+        ((axial_even, odd_far), first_rows, 0), ((radial_parcels, radial_parcels), (0, half), 2 * movers)
     ):
         top, bottom = (moved[i : i + ROWS // 2, lo : lo + 2 * movers] for i in (0, ROWS // 2))
         up = jnp.where(left_half, top, pltpu.roll(bottom, movers, 1))
@@ -325,7 +325,7 @@
 
     movers = arrivals.shape[-1]
     base = 2 * FIELDS * tile
-    odd_parcels = from_odd[FIELDS * tile :, :]
+    odd_parcels = odd_far[FIELDS * tile :, :]
     axial_parcels = axial_halo(from_even[base:, :], odd_parcels, odd_parcels)
     for side, parts in ((0, axial_parcels), (2, radial_halo(base, ROWS // 2))):
         for i, part in enumerate(parts):
@@ -574,7 +574,7 @@
     slots2 = leave_slots.reshape(4, movers)
     axial_even, odd_near, odd_far, radial_parcels, kept, *fields, parcels2, staying, source, last = call(
         functools.partial(pack_kernel, width_x, width_y),
-        [f32(n, depth) for n in (packet_rows, odd_rows + ROWS // 2, odd_rows, ROWS)]
+        [f32(n, depth) for n in (packet_rows, odd_rows, odd_rows + ROWS // 2, ROWS)]
         + [f32(chunks, LANES)] + [f32(*x.shape) for x in fields + [parcels2]] + pushed,
         fields + [parcels2, cells2, slots2, leave_counts],
         10**8, "pack_faces", far_ins=range(7),

time: 12.4 us -> 12.3 us (level)
  transfers between devices with their start and end apart: 7 -> 7, of which waited for: 2 -> 2; matrix products, arithmetic and copies ran while one was open for 0% -> 0% of each run, Pallas kernels for 14% -> 13%
where the time goes in v9:
time: 12.3 us; the launch traced here: 12.1 us
  starting transfers between devices  6.02 us (49%)
  Pallas kernels  3.84 us (31%)
  between operations  1.36 us (11%)
  waiting for transfers between devices  0.92 us (7%)
    ppermute x7, starting transfers between devices, body(): permute = lambda x, pairs: lax.ppermute(x, AXES, pairs)  6.02 us
    pallas_call x6, Pallas kernels, call(): pl.pallas_call(kernel, out_shape=[jax.ShapeDtypeStruct(s.shape, s.dtype)...  3.84 us
    ppermute x7, waiting for transfers between devices, body(): permute = lambda x, pairs: lax.ppermute(x, AXES, pairs)  0.92 us
  transfers between devices with their start and end apart: 7, of which 2 were waited for; matrix products, arithmetic and copies ran while one was open for 0% of the time, Pallas kernels for 13%

profile of v9, /device:TPU:3, one launch (start us, length us, event | category | flops | bytes accessed | tf_op | source)
XLA Modules:
  0.0 12.1 jit_solution(15638523208141450599)
XLA Ops:
  0.6 1.4 %pack_faces.1 = (f32[152,128]{1,0:T(8,128)S(1)}, f32[72,128]{1,0:T(8,128)S(1)}, f32[80,128]{1,0:T(8,128)S(1)}, f32[16,128]{1,0:T(8,128)S(1)}, f32[16,128]{1,0:T(...) custom-call(f32[320,128]{1,0:T(8,128)} %bitcast.11, ...), custom_call_target="tpu_custom_call" | custom-call | flops 100000000 | bytes 1328144 | tf_op jit(solution)/shard_map/pack_faces/pallas_call | solution.py:538
  2.1 0.7 %collective-permute-start.1 = (f32[152,128]{1,0:T(8,128)S(1)}, f32[152,128]{1,0:T(8,128)S(1)}, u32[]{:S(2)}, u32[]{:S(2)}) collective-permute-start(f32[152,128]{1,0:T(8,128)S(1)} %get-tuple-element.33), channel_id=1, source_target_pairs={{0,4},{1,5},{2,6},{3,7},{4,0},{5,1},{6,2},{7,3},{8,12},{9,13},{10,... | collective-permute-start | bytes 233480 | tf_op jit(solution)/shard_map/ppermute | solution.py:559
  2.8 1.2 %collective-permute-start = (f32[72,128]{1,0:T(8,128)S(1)}, f32[72,128]{1,0:T(8,128)S(1)}, u32[]{:S(2)}, u32[]{:S(2)}) collective-permute-start(f32[72,128]{1,0:T(8,128)S(1)} %get-tuple-element.32), channel_id=1, source_target_pairs={{0,1},{1,0},{2,3},{3,2},{4,8},{5,9},{6,10},{7,11},{8,4},{9,5},{10,... | collective-permute-start | bytes 110600 | tf_op jit(solution)/shard_map/ppermute | solution.py:559
  4.0 1.5 %collective-permute-start.4 = (f32[80,128]{1,0:T(8,128)S(1)}, f32[80,128]{1,0:T(8,128)S(1)}, u32[]{:S(2)}, u32[]{:S(2)}) collective-permute-start(f32[80,128]{1,0:T(8,128)S(1)} %get-tuple-element.39), channel_id=1, source_target_pairs={{0,1},{1,0},{2,3},{3,2},{4,8},{5,9},{6,10},{7,11},{8,4},{9,5},{10,... | collective-permute-start | bytes 122888 | tf_op jit(solution)/shard_map/ppermute | solution.py:559
  5.5 0.0 collective-permute-done.1.from_even
  5.5 1.3 %collective-permute-start.5 = (f32[152,128]{1,0:T(8,128)S(1)}, f32[152,128]{1,0:T(8,128)S(1)}, u32[]{:S(2)}, u32[]{:S(2)}) collective-permute-start(f32[152,128]{1,0:T(8,128)S(1)} %get-tuple-element.41), channel_id=1, source_target_pairs={{0,4},{1,0},{2,1},{3,2},{4,5},{5,6},{6,7},{7,3},{8,12},{9,8},{10,9... | collective-permute-start | bytes 233480 | tf_op jit(solution)/shard_map/ppermute | solution.py:559
  6.8 0.0 collective-permute-start.6
  6.8 0.7 %collective-permute-done.from_odd = f32[72,128]{1,0:T(8,128)S(1)} collective-permute-done((f32[72,128]{1,0:T(8,128)S(1)}, f32[72,128]{1,0:T(8,128)S(1)}, u32[]{:S(2)}, u32[]{:S(2)}) %collective-permute-start) | collective-permute-done | bytes 36896 | tf_op jit(solution)/shard_map/ppermute | solution.py:559
  7.5 0.0 copy-start
  7.5 1.3 %collective-permute-start.2 = (f32[24,128]{1,0:T(8,128)S(1)}, f32[24,128]{1,0:T(8,128)S(1)}, u32[]{:S(2)}, u32[]{:S(2)}) collective-permute-start(f32[24,128]{1,0:T(8,128)S(1)} %get-tuple-element.34), channel_id=1, source_target_pairs={{0,4},{1,0},{2,1},{3,2},{4,5},{5,6},{6,7},{7,3},{8,12},{9,8},{10,9... | collective-permute-start | bytes 36872 | tf_op jit(solution)/shard_map/ppermute | solution.py:559
  8.8 0.0 collective-permute-start.3
  8.8 0.0 copy-done
  8.8 0.8 %push_parcels.1 = (f32[16,2048]{1,0:T(8,128)S(1)}, f32[256,128]{1,0:T(8,128)S(1)}, f32[4,2048]{1,0:T(4,128)S(1)}) custom-call(f32[192,128]{1,0:T(8,128)S(1)} %get-tuple-element.37.velocity, f32[16,2048]{1,0:T(8,128)S(1)} %get-tuple-element.43.parcels, s32[1,1,2048]{2,1,0:T(1,128)S(1)} %copy-done, f32[16,128]{1,0:T(8,128)S(1)} %get-tuple-element.44.kept, ...), custom_call_target="tpu_custom_call" | custom-call | flops 1000000000 | bytes 835584 | tf_op jit(solution)/shard_map/push_parcels/pallas_call | solution.py:538
  10.3 0.0 collective-permute-done.4.odd_far
  10.3 0.0 collective-permute-done.5.beside_two
  10.3 0.0 collective-permute-done.6.beside_one
  10.3 0.8 %stencils.1 = (f32[16,2048]{1,0:T(8,128)}, f32[6,144,128]{2,1,0:T(8,128)S(1)}, f32[8,64,128]{2,1,0:T(8,128)S(1)}, f32[4,16,64]{2,1,0:T(8,128)S(1)}) custom-call(f32[320,128]{1,0:T(8,128)S(1)} %get-tuple-element.36.species, f32[192,128]{1,0:T(8,128)S(1)} %get-tuple-element.37.velocity, f32[64,128]{1,0:T(8,128)S(1)} %get-tuple-element.38.diffusivity, ...), custom_call_target="tpu_custom_call" | custom-call | flops 10000000 | bytes 1753092 | tf_op jit(solution)/shard_map/stencils/pallas_call | solution.py:538
  11.1 0.0 collective-permute-done.2.corner_two
  11.1 0.2 %collective-permute-done.3.corner_one = f32[24,128]{1,0:T(8,128)S(1)} collective-permute-done((f32[24,128]{1,0:T(8,128)S(1)}, f32[24,128]{1,0:T(8,128)S(1)}, u32[]{:S(2)}, u32[]{:S(2)}) %collective-permute-start.3) | collective-permute-done | bytes 12320 | tf_op jit(solution)/shard_map/ppermute | solution.py:559
  11.4 0.8 %ends.1 = (f32[5,64,128]{2,1,0:T(8,128)}, f32[3,64,128]{2,1,0:T(8,128)}, f32[4,16,64]{2,1,0:T(8,128)}) custom-call(f32[24,128]{1,0:T(8,128)S(1)} %collective-permute-done.2.corner_two, f32[24,128]{1,0:T(8,128)S(1)} %collective-permute-done.3.corner_one, f32[6,144,128]{2,1,0:T(8,128)S(1)} %get-tuple-element.53.state, ...), custom_call_target="tpu_custom_call" | custom-call | flops 1000000 | bytes 1024000 | tf_op jit(solution)/shard_map/ends/pallas_call | solution.py:538
  (2 shorter events, 0.0 us)
Async XLA Ops:
  2.1 3.4 %collective-permute-start.1 = (f32[152,128]{1,0:T(8,128)S(1)}, f32[152,128]{1,0:T(8,128)S(1)}, u32[]{:S(2)}, u32[]{:S(2)}) collective-permute-start(f32[152,128]{1,0:T(8,128)S(1)} %get-tuple-element.33), channel_id=1, source_target_pairs={{0,4},{1,5},{2,6},{3,7},{4,0},{5,1},{6,2},{7,3},{8,12},{9,13},{10,... | collective-permute-start | bytes 233480 | tf_op jit(solution)/shard_map/ppermute | solution.py:559
  2.8 4.7 %collective-permute-start = (f32[72,128]{1,0:T(8,128)S(1)}, f32[72,128]{1,0:T(8,128)S(1)}, u32[]{:S(2)}, u32[]{:S(2)}) collective-permute-start(f32[72,128]{1,0:T(8,128)S(1)} %get-tuple-element.32), channel_id=1, source_target_pairs={{0,1},{1,0},{2,3},{3,2},{4,8},{5,9},{6,10},{7,11},{8,4},{9,5},{10,... | collective-permute-start | bytes 110600 | tf_op jit(solution)/shard_map/ppermute | solution.py:559
  4.0 6.3 %collective-permute-start.4 = (f32[80,128]{1,0:T(8,128)S(1)}, f32[80,128]{1,0:T(8,128)S(1)}, u32[]{:S(2)}, u32[]{:S(2)}) collective-permute-start(f32[80,128]{1,0:T(8,128)S(1)} %get-tuple-element.39), channel_id=1, source_target_pairs={{0,1},{1,0},{2,3},{3,2},{4,8},{5,9},{6,10},{7,11},{8,4},{9,5},{10,... | collective-permute-start | bytes 122888 | tf_op jit(solution)/shard_map/ppermute | solution.py:559
  5.5 4.8 %collective-permute-start.5 = (f32[152,128]{1,0:T(8,128)S(1)}, f32[152,128]{1,0:T(8,128)S(1)}, u32[]{:S(2)}, u32[]{:S(2)}) collective-permute-start(f32[152,128]{1,0:T(8,128)S(1)} %get-tuple-element.41), channel_id=1, source_target_pairs={{0,4},{1,0},{2,1},{3,2},{4,5},{5,6},{6,7},{7,3},{8,12},{9,8},{10,9... | collective-permute-start | bytes 233480 | tf_op jit(solution)/shard_map/ppermute | solution.py:559
  6.8 3.5 %collective-permute-start.6 = (f32[152,128]{1,0:T(8,128)S(1)}, f32[152,128]{1,0:T(8,128)S(1)}, u32[]{:S(2)}, u32[]{:S(2)}) collective-permute-start(f32[152,128]{1,0:T(8,128)S(1)} %get-tuple-element.42), channel_id=1, source_target_pairs={{0,1},{1,2},{2,3},{3,7},{4,0},{5,4},{6,5},{7,6},{8,9},{9,10},{10,1... | collective-permute-start | bytes 233480 | tf_op jit(solution)/shard_map/ppermute | solution.py:559
  7.5 1.3 %copy-start = (s32[1,1,2048]{2,1,0:T(1,128)S(1)}, s32[1,1,2048]{2,1,0:T(1,128)}, u32[]{:S(2)}) copy-start(s32[1,1,2048]{2,1,0:T(1,128)} %cells.1) | copy-start | bytes 24580
  7.5 3.6 %collective-permute-start.2 = (f32[24,128]{1,0:T(8,128)S(1)}, f32[24,128]{1,0:T(8,128)S(1)}, u32[]{:S(2)}, u32[]{:S(2)}) collective-permute-start(f32[24,128]{1,0:T(8,128)S(1)} %get-tuple-element.34), channel_id=1, source_target_pairs={{0,4},{1,0},{2,1},{3,2},{4,5},{5,6},{6,7},{7,3},{8,12},{9,8},{10,9... | collective-permute-start | bytes 36872 | tf_op jit(solution)/shard_map/ppermute | solution.py:559
  8.8 2.5 %collective-permute-start.3 = (f32[24,128]{1,0:T(8,128)S(1)}, f32[24,128]{1,0:T(8,128)S(1)}, u32[]{:S(2)}, u32[]{:S(2)}) collective-permute-start(f32[24,128]{1,0:T(8,128)S(1)} %get-tuple-element.35), channel_id=1, source_target_pairs={{0,1},{1,2},{2,3},{3,7},{4,0},{5,4},{6,5},{7,6},{8,9},{9,10},{10,1... | collective-permute-start | bytes 36872 | tf_op jit(solution)/shard_map/ppermute | solution.py:559

commit v10 on v9

--- a/solution.py
+++ b/solution.py
@@ -142,13 +142,14 @@
         odd_near[at, :] = jnp.where(even_x, odd[0][0], odd[1][1])
         odd_far[at, :] = jnp.where(even_x, odd[1][0], odd[0][1])
     response, evaporation = rows[4:5], rows[5:6]
-    pushed = [rows[i : i + 1] + time_step * (response * (gas[i] - rows[i : i + 1])) for i in range(3)]
-    pushed.append(rows[3:4] * (1.0 - time_step * evaporation))
-    pushed.extend([response, evaporation])
-    pushed.extend(rows[6 + i : 7 + i] + time_step * pushed[i] for i in range(3))
-    for i, line in enumerate(pushed):
-        moved[i : i + 1, :] = line * valid
-    moved[9:ROWS, :] = rows[9:ROWS] * valid
+    drag = jnp.concatenate(gas + [rows[3:ROWS]], axis=0) - rows
+    number = lax.broadcasted_iota(I32, rows.shape, 0)
+    fresh = rows + time_step * (response * drag)
+    later = jnp.concatenate([rows[:6], fresh[:3], rows[9:]], axis=0)
+    values = jnp.where(number < 3, fresh, rows)
+    values = jnp.where(number == 3, rows * (1.0 - time_step * evaporation), values)
+    values = jnp.where((number >= 6) & (number < 9), rows + time_step * later, values)
+    moved[...] = values * valid
     left_half = lax.broadcasted_iota(I32, (ROWS // 2, 2 * movers), 1) < movers
     half = ROWS // 2
     first_rows = (axial_even.shape[0] - half, odd_far.shape[0] - half)

time: 12.3 us -> 12.3 us (level)
  no operation moved by 1% of the time
where the time goes in v10:
time: 12.3 us; the launch traced here: 12.1 us
  starting transfers between devices  6.02 us (49%)
  Pallas kernels  3.82 us (31%)
  between operations  1.36 us (11%)
  waiting for transfers between devices  0.92 us (7%)
    ppermute x7, starting transfers between devices, body(): permute = lambda x, pairs: lax.ppermute(x, AXES, pairs)  6.02 us
    pallas_call x6, Pallas kernels, call(): pl.pallas_call(kernel, out_shape=[jax.ShapeDtypeStruct(s.shape, s.dtype)...  3.82 us
    ppermute x7, waiting for transfers between devices, body(): permute = lambda x, pairs: lax.ppermute(x, AXES, pairs)  0.92 us
  transfers between devices with their start and end apart: 7, of which 2 were waited for; matrix products, arithmetic and copies ran while one was open for 0% of the time, Pallas kernels for 13%

profile of v10, /device:TPU:3, one launch (start us, length us, event | category | flops | bytes accessed | tf_op | source)
XLA Modules:
  0.0 12.1 jit_solution(6254809907687108527)
XLA Ops:
  0.6 1.4 %pack_faces.1 = (f32[152,128]{1,0:T(8,128)S(1)}, f32[72,128]{1,0:T(8,128)S(1)}, f32[80,128]{1,0:T(8,128)S(1)}, f32[16,128]{1,0:T(8,128)S(1)}, f32[16,128]{1,0:T(...) custom-call(f32[320,128]{1,0:T(8,128)} %bitcast.11, ...), custom_call_target="tpu_custom_call" | custom-call | flops 100000000 | bytes 1328144 | tf_op jit(solution)/shard_map/pack_faces/pallas_call | solution.py:539
  2.1 0.7 %collective-permute-start.1 = (f32[152,128]{1,0:T(8,128)S(1)}, f32[152,128]{1,0:T(8,128)S(1)}, u32[]{:S(2)}, u32[]{:S(2)}) collective-permute-start(f32[152,128]{1,0:T(8,128)S(1)} %get-tuple-element.33), channel_id=1, source_target_pairs={{0,4},{1,5},{2,6},{3,7},{4,0},{5,1},{6,2},{7,3},{8,12},{9,13},{10,... | collective-permute-start | bytes 233480 | tf_op jit(solution)/shard_map/ppermute | solution.py:560
  2.8 1.2 %collective-permute-start = (f32[72,128]{1,0:T(8,128)S(1)}, f32[72,128]{1,0:T(8,128)S(1)}, u32[]{:S(2)}, u32[]{:S(2)}) collective-permute-start(f32[72,128]{1,0:T(8,128)S(1)} %get-tuple-element.32), channel_id=1, source_target_pairs={{0,1},{1,0},{2,3},{3,2},{4,8},{5,9},{6,10},{7,11},{8,4},{9,5},{10,... | collective-permute-start | bytes 110600 | tf_op jit(solution)/shard_map/ppermute | solution.py:560
  4.0 1.5 %collective-permute-start.4 = (f32[80,128]{1,0:T(8,128)S(1)}, f32[80,128]{1,0:T(8,128)S(1)}, u32[]{:S(2)}, u32[]{:S(2)}) collective-permute-start(f32[80,128]{1,0:T(8,128)S(1)} %get-tuple-element.39), channel_id=1, source_target_pairs={{0,1},{1,0},{2,3},{3,2},{4,8},{5,9},{6,10},{7,11},{8,4},{9,5},{10,... | collective-permute-start | bytes 122888 | tf_op jit(solution)/shard_map/ppermute | solution.py:560
  5.4 0.0 collective-permute-done.1.from_even
  5.5 1.3 %collective-permute-start.5 = (f32[152,128]{1,0:T(8,128)S(1)}, f32[152,128]{1,0:T(8,128)S(1)}, u32[]{:S(2)}, u32[]{:S(2)}) collective-permute-start(f32[152,128]{1,0:T(8,128)S(1)} %get-tuple-element.41), channel_id=1, source_target_pairs={{0,4},{1,0},{2,1},{3,2},{4,5},{5,6},{6,7},{7,3},{8,12},{9,8},{10,9... | collective-permute-start | bytes 233480 | tf_op jit(solution)/shard_map/ppermute | solution.py:560
  6.8 0.0 collective-permute-start.6
  6.8 0.7 %collective-permute-done.from_odd = f32[72,128]{1,0:T(8,128)S(1)} collective-permute-done((f32[72,128]{1,0:T(8,128)S(1)}, f32[72,128]{1,0:T(8,128)S(1)}, u32[]{:S(2)}, u32[]{:S(2)}) %collective-permute-start) | collective-permute-done | bytes 36896 | tf_op jit(solution)/shard_map/ppermute | solution.py:560
  7.5 0.0 copy-start
  7.5 1.3 %collective-permute-start.2 = (f32[24,128]{1,0:T(8,128)S(1)}, f32[24,128]{1,0:T(8,128)S(1)}, u32[]{:S(2)}, u32[]{:S(2)}) collective-permute-start(f32[24,128]{1,0:T(8,128)S(1)} %get-tuple-element.34), channel_id=1, source_target_pairs={{0,4},{1,0},{2,1},{3,2},{4,5},{5,6},{6,7},{7,3},{8,12},{9,8},{10,9... | collective-permute-start | bytes 36872 | tf_op jit(solution)/shard_map/ppermute | solution.py:560
  8.8 0.0 collective-permute-start.3
  8.8 0.0 copy-done
  8.8 0.8 %push_parcels.1 = (f32[16,2048]{1,0:T(8,128)S(1)}, f32[256,128]{1,0:T(8,128)S(1)}, f32[4,2048]{1,0:T(4,128)S(1)}) custom-call(f32[192,128]{1,0:T(8,128)S(1)} %get-tuple-element.37.velocity, f32[16,2048]{1,0:T(8,128)S(1)} %get-tuple-element.43.parcels, s32[1,1,2048]{2,1,0:T(1,128)S(1)} %copy-done, f32[16,128]{1,0:T(8,128)S(1)} %get-tuple-element.44.kept, ...), custom_call_target="tpu_custom_call" | custom-call | flops 1000000000 | bytes 835584 | tf_op jit(solution)/shard_map/push_parcels/pallas_call | solution.py:539
  10.3 0.0 collective-permute-done.4.odd_far
  10.3 0.0 collective-permute-done.5.beside_two
  10.3 0.0 collective-permute-done.6.beside_one
  10.3 0.8 %stencils.1 = (f32[16,2048]{1,0:T(8,128)}, f32[6,144,128]{2,1,0:T(8,128)S(1)}, f32[8,64,128]{2,1,0:T(8,128)S(1)}, f32[4,16,64]{2,1,0:T(8,128)S(1)}) custom-call(f32[320,128]{1,0:T(8,128)S(1)} %get-tuple-element.36.species, f32[192,128]{1,0:T(8,128)S(1)} %get-tuple-element.37.velocity, f32[64,128]{1,0:T(8,128)S(1)} %get-tuple-element.38.diffusivity, ...), custom_call_target="tpu_custom_call" | custom-call | flops 10000000 | bytes 1753092 | tf_op jit(solution)/shard_map/stencils/pallas_call | solution.py:539
  11.1 0.0 collective-permute-done.2.corner_two
  11.1 0.2 %collective-permute-done.3.corner_one = f32[24,128]{1,0:T(8,128)S(1)} collective-permute-done((f32[24,128]{1,0:T(8,128)S(1)}, f32[24,128]{1,0:T(8,128)S(1)}, u32[]{:S(2)}, u32[]{:S(2)}) %collective-permute-start.3) | collective-permute-done | bytes 12320 | tf_op jit(solution)/shard_map/ppermute | solution.py:560
  11.4 0.8 %ends.1 = (f32[5,64,128]{2,1,0:T(8,128)}, f32[3,64,128]{2,1,0:T(8,128)}, f32[4,16,64]{2,1,0:T(8,128)}) custom-call(f32[24,128]{1,0:T(8,128)S(1)} %collective-permute-done.2.corner_two, f32[24,128]{1,0:T(8,128)S(1)} %collective-permute-done.3.corner_one, f32[6,144,128]{2,1,0:T(8,128)S(1)} %get-tuple-element.53.state, ...), custom_call_target="tpu_custom_call" | custom-call | flops 1000000 | bytes 1024000 | tf_op jit(solution)/shard_map/ends/pallas_call | solution.py:539
  (2 shorter events, 0.0 us)
Async XLA Ops:
  2.1 3.4 %collective-permute-start.1 = (f32[152,128]{1,0:T(8,128)S(1)}, f32[152,128]{1,0:T(8,128)S(1)}, u32[]{:S(2)}, u32[]{:S(2)}) collective-permute-start(f32[152,128]{1,0:T(8,128)S(1)} %get-tuple-element.33), channel_id=1, source_target_pairs={{0,4},{1,5},{2,6},{3,7},{4,0},{5,1},{6,2},{7,3},{8,12},{9,13},{10,... | collective-permute-start | bytes 233480 | tf_op jit(solution)/shard_map/ppermute | solution.py:560
  2.8 4.7 %collective-permute-start = (f32[72,128]{1,0:T(8,128)S(1)}, f32[72,128]{1,0:T(8,128)S(1)}, u32[]{:S(2)}, u32[]{:S(2)}) collective-permute-start(f32[72,128]{1,0:T(8,128)S(1)} %get-tuple-element.32), channel_id=1, source_target_pairs={{0,1},{1,0},{2,3},{3,2},{4,8},{5,9},{6,10},{7,11},{8,4},{9,5},{10,... | collective-permute-start | bytes 110600 | tf_op jit(solution)/shard_map/ppermute | solution.py:560
  4.0 6.3 %collective-permute-start.4 = (f32[80,128]{1,0:T(8,128)S(1)}, f32[80,128]{1,0:T(8,128)S(1)}, u32[]{:S(2)}, u32[]{:S(2)}) collective-permute-start(f32[80,128]{1,0:T(8,128)S(1)} %get-tuple-element.39), channel_id=1, source_target_pairs={{0,1},{1,0},{2,3},{3,2},{4,8},{5,9},{6,10},{7,11},{8,4},{9,5},{10,... | collective-permute-start | bytes 122888 | tf_op jit(solution)/shard_map/ppermute | solution.py:560
  5.5 4.8 %collective-permute-start.5 = (f32[152,128]{1,0:T(8,128)S(1)}, f32[152,128]{1,0:T(8,128)S(1)}, u32[]{:S(2)}, u32[]{:S(2)}) collective-permute-start(f32[152,128]{1,0:T(8,128)S(1)} %get-tuple-element.41), channel_id=1, source_target_pairs={{0,4},{1,0},{2,1},{3,2},{4,5},{5,6},{6,7},{7,3},{8,12},{9,8},{10,9... | collective-permute-start | bytes 233480 | tf_op jit(solution)/shard_map/ppermute | solution.py:560
  6.8 3.5 %collective-permute-start.6 = (f32[152,128]{1,0:T(8,128)S(1)}, f32[152,128]{1,0:T(8,128)S(1)}, u32[]{:S(2)}, u32[]{:S(2)}) collective-permute-start(f32[152,128]{1,0:T(8,128)S(1)} %get-tuple-element.42), channel_id=1, source_target_pairs={{0,1},{1,2},{2,3},{3,7},{4,0},{5,4},{6,5},{7,6},{8,9},{9,10},{10,1... | collective-permute-start | bytes 233480 | tf_op jit(solution)/shard_map/ppermute | solution.py:560
  7.5 1.3 %copy-start = (s32[1,1,2048]{2,1,0:T(1,128)S(1)}, s32[1,1,2048]{2,1,0:T(1,128)}, u32[]{:S(2)}) copy-start(s32[1,1,2048]{2,1,0:T(1,128)} %cells.1) | copy-start | bytes 24580
  7.5 3.6 %collective-permute-start.2 = (f32[24,128]{1,0:T(8,128)S(1)}, f32[24,128]{1,0:T(8,128)S(1)}, u32[]{:S(2)}, u32[]{:S(2)}) collective-permute-start(f32[24,128]{1,0:T(8,128)S(1)} %get-tuple-element.34), channel_id=1, source_target_pairs={{0,4},{1,0},{2,1},{3,2},{4,5},{5,6},{6,7},{7,3},{8,12},{9,8},{10,9... | collective-permute-start | bytes 36872 | tf_op jit(solution)/shard_map/ppermute | solution.py:560
  8.8 2.5 %collective-permute-start.3 = (f32[24,128]{1,0:T(8,128)S(1)}, f32[24,128]{1,0:T(8,128)S(1)}, u32[]{:S(2)}, u32[]{:S(2)}) collective-permute-start(f32[24,128]{1,0:T(8,128)S(1)} %get-tuple-element.35), channel_id=1, source_target_pairs={{0,1},{1,2},{2,3},{3,7},{4,0},{5,4},{6,5},{7,6},{8,9},{9,10},{10,1... | collective-permute-start | bytes 36872 | tf_op jit(solution)/shard_map/ppermute | solution.py:560

commit v11 on v9

--- a/solution.py
+++ b/solution.py
@@ -279,12 +279,10 @@
 
 def stencil_kernel(
     width_x, width_y, species, velocity, diffusivity, from_odd, odd_far, from_even, beside_two, beside_one, source, staying, last, counts,
-    staying_out, state, result, arrivals, live_staying, sent,
+    live_staying, state, result, arrivals,
 ):
     live = lax.broadcasted_iota(I32, (1, staying.shape[1]), 1) < counts[...]
     live_staying[...] = jnp.where(live, staying[...], 0.0)
-    copy = pltpu.make_async_copy(live_staying, staying_out, sent)
-    copy.start()
     last_sum = jnp.sum(jnp.where(live, last[...], 0.0), axis=1, keepdims=True)
     tile = width_y
     rows = width_x * width_y
@@ -465,11 +463,11 @@
         if part is not None:
             end = value[-tile:] + jnp.where(at_last, time_step * last_sum[part : part + 1], 0.0)
             result[f, rows - tile :, :] = end
-    copy.wait()
 
 
 def end_kernel(
-    width_x, width_y, corner_two, corner_one, state, result, arrivals, species_out, velocity_out, arrivals_out, ends, sent,
+    width_x, width_y, corner_two, corner_one, state, result, arrivals, staying,
+    species_out, velocity_out, arrivals_out, staying_out, ends, sent,
 ):
     tile = width_y
     rows = width_x * width_y
@@ -487,6 +485,7 @@
             result.at[pl.ds(SPECIES, VECTORS), middle, :], velocity_out.at[:, middle, :], sent.at[1]
         ),
         pltpu.make_async_copy(arrivals, arrivals_out, sent.at[6]),
+        pltpu.make_async_copy(staying, staying_out, sent.at[7]),
     ]
     for copy in copies:
         copy.start()
@@ -604,7 +603,7 @@
         functools.partial(stencil_kernel, width_x, width_y),
         [f32(ROWS, slots), state, f32(FLOW, rows, depth), f32(4, ROWS, movers)],
         fields + [from_odd, odd_far, from_even, beside_two, beside_one, source, staying, last, counts],
-        10**7, "stencils", far_outs=(0,), scratch=[near(f32(ROWS, slots)), pltpu.SemaphoreType.DMA],
+        10**7, "stencils",
     )
     corner_one, corner_two = call(
         functools.partial(corner_kernel, width_x, width_y),
@@ -612,12 +611,12 @@
     )
     corner_two = permute(corner_two, radial_shift(sizes, False))
     corner_one = permute(corner_one, radial_shift(sizes, True))
-    species_out, velocity_out, arrivals = call(
+    species_out, velocity_out, arrivals, staying = call(
         functools.partial(end_kernel, width_x, width_y),
-        [f32(SPECIES, rows, depth), f32(VECTORS, rows, depth), f32(4, ROWS, movers)],
-        [corner_two, corner_one, state, result, arrivals],
-        10**6, "ends", far_outs=(0, 1, 2),
-        scratch=[near(f32(2, FLOW, width_y, depth)), pltpu.SemaphoreType.DMA((7,))],
+        [f32(SPECIES, rows, depth), f32(VECTORS, rows, depth), f32(4, ROWS, movers), f32(ROWS, slots)],
+        [corner_two, corner_one, state, result, arrivals, staying],
+        10**6, "ends", far_outs=(0, 1, 2, 3),
+        scratch=[near(f32(2, FLOW, width_y, depth)), pltpu.SemaphoreType.DMA((8,))],
     )
     return (
         species_out.reshape(species.shape),

time: 12.3 us -> 12.4 us (level)
  no operation moved by 1% of the time
where the time goes in v11:
time: 12.4 us; the launch traced here: 12.2 us
  starting transfers between devices  6.02 us (49%)
  Pallas kernels  3.84 us (31%)
  between operations  1.36 us (11%)
  waiting for transfers between devices  0.96 us (8%)
    ppermute x7, starting transfers between devices, body(): permute = lambda x, pairs: lax.ppermute(x, AXES, pairs)  6.02 us
    pallas_call x6, Pallas kernels, call(): pl.pallas_call(kernel, out_shape=[jax.ShapeDtypeStruct(s.shape, s.dtype)...  3.84 us
    ppermute x7, waiting for transfers between devices, body(): permute = lambda x, pairs: lax.ppermute(x, AXES, pairs)  0.96 us
  transfers between devices with their start and end apart: 7, of which 2 were waited for; matrix products, arithmetic and copies ran while one was open for 0% of the time, Pallas kernels for 13%

profile of v11, /device:TPU:3, one launch (start us, length us, event | category | flops | bytes accessed | tf_op | source)
XLA Modules:
  0.0 12.2 jit_solution(1285854451012365335)
XLA Ops:
  0.6 1.4 %pack_faces.1 = (f32[152,128]{1,0:T(8,128)S(1)}, f32[72,128]{1,0:T(8,128)S(1)}, f32[80,128]{1,0:T(8,128)S(1)}, f32[16,128]{1,0:T(8,128)S(1)}, f32[16,128]{1,0:T(...) custom-call(f32[320,128]{1,0:T(8,128)} %bitcast.11, ...), custom_call_target="tpu_custom_call" | custom-call | flops 100000000 | bytes 1328144 | tf_op jit(solution)/shard_map/pack_faces/pallas_call | solution.py:537
  2.1 0.7 %collective-permute-start.1 = (f32[152,128]{1,0:T(8,128)S(1)}, f32[152,128]{1,0:T(8,128)S(1)}, u32[]{:S(2)}, u32[]{:S(2)}) collective-permute-start(f32[152,128]{1,0:T(8,128)S(1)} %get-tuple-element.34), channel_id=1, source_target_pairs={{0,4},{1,5},{2,6},{3,7},{4,0},{5,1},{6,2},{7,3},{8,12},{9,13},{10,... | collective-permute-start | bytes 233480 | tf_op jit(solution)/shard_map/ppermute | solution.py:558
  2.8 1.2 %collective-permute-start = (f32[72,128]{1,0:T(8,128)S(1)}, f32[72,128]{1,0:T(8,128)S(1)}, u32[]{:S(2)}, u32[]{:S(2)}) collective-permute-start(f32[72,128]{1,0:T(8,128)S(1)} %get-tuple-element.33), channel_id=1, source_target_pairs={{0,1},{1,0},{2,3},{3,2},{4,8},{5,9},{6,10},{7,11},{8,4},{9,5},{10,... | collective-permute-start | bytes 110600 | tf_op jit(solution)/shard_map/ppermute | solution.py:558
  4.0 1.5 %collective-permute-start.4 = (f32[80,128]{1,0:T(8,128)S(1)}, f32[80,128]{1,0:T(8,128)S(1)}, u32[]{:S(2)}, u32[]{:S(2)}) collective-permute-start(f32[80,128]{1,0:T(8,128)S(1)} %get-tuple-element.40), channel_id=1, source_target_pairs={{0,1},{1,0},{2,3},{3,2},{4,8},{5,9},{6,10},{7,11},{8,4},{9,5},{10,... | collective-permute-start | bytes 122888 | tf_op jit(solution)/shard_map/ppermute | solution.py:558
  5.5 0.0 collective-permute-done.1.from_even
  5.5 1.3 %collective-permute-start.5 = (f32[152,128]{1,0:T(8,128)S(1)}, f32[152,128]{1,0:T(8,128)S(1)}, u32[]{:S(2)}, u32[]{:S(2)}) collective-permute-start(f32[152,128]{1,0:T(8,128)S(1)} %get-tuple-element.42), channel_id=1, source_target_pairs={{0,4},{1,0},{2,1},{3,2},{4,5},{5,6},{6,7},{7,3},{8,12},{9,8},{10,9... | collective-permute-start | bytes 233480 | tf_op jit(solution)/shard_map/ppermute | solution.py:558
  6.8 0.0 collective-permute-start.6
  6.8 0.7 %collective-permute-done.from_odd = f32[72,128]{1,0:T(8,128)S(1)} collective-permute-done((f32[72,128]{1,0:T(8,128)S(1)}, f32[72,128]{1,0:T(8,128)S(1)}, u32[]{:S(2)}, u32[]{:S(2)}) %collective-permute-start) | collective-permute-done | bytes 36896 | tf_op jit(solution)/shard_map/ppermute | solution.py:558
  7.5 0.0 copy-start
  7.5 1.3 %collective-permute-start.2 = (f32[24,128]{1,0:T(8,128)S(1)}, f32[24,128]{1,0:T(8,128)S(1)}, u32[]{:S(2)}, u32[]{:S(2)}) collective-permute-start(f32[24,128]{1,0:T(8,128)S(1)} %get-tuple-element.35), channel_id=1, source_target_pairs={{0,4},{1,0},{2,1},{3,2},{4,5},{5,6},{6,7},{7,3},{8,12},{9,8},{10,9... | collective-permute-start | bytes 36872 | tf_op jit(solution)/shard_map/ppermute | solution.py:558
  8.8 0.0 collective-permute-start.3
  8.8 0.0 copy-done
  8.8 0.8 %push_parcels.1 = (f32[16,2048]{1,0:T(8,128)S(1)}, f32[256,128]{1,0:T(8,128)S(1)}, f32[4,2048]{1,0:T(4,128)S(1)}) custom-call(f32[192,128]{1,0:T(8,128)S(1)} %get-tuple-element.38.velocity, f32[16,2048]{1,0:T(8,128)S(1)} %get-tuple-element.44.parcels, s32[1,1,2048]{2,1,0:T(1,128)S(1)} %copy-done, f32[16,128]{1,0:T(8,128)S(1)} %get-tuple-element.45.kept, ...), custom_call_target="tpu_custom_call" | custom-call | flops 1000000000 | bytes 835584 | tf_op jit(solution)/shard_map/push_parcels/pallas_call | solution.py:537
  10.3 0.0 collective-permute-done.4.odd_far
  10.3 0.0 collective-permute-done.5.beside_two
  10.3 0.0 collective-permute-done.6.beside_one
  10.3 0.7 %stencils.1 = (f32[16,2048]{1,0:T(8,128)S(1)}, f32[6,144,128]{2,1,0:T(8,128)S(1)}, f32[8,64,128]{2,1,0:T(8,128)S(1)}, f32[4,16,64]{2,1,0:T(8,128)S(1)}) custom-call(f32[320,128]{1,0:T(8,128)S(1)} %get-tuple-element.37.species, f32[192,128]{1,0:T(8,128)S(1)} %get-tuple-element.38.velocity, f32[64,128]{1,0:T(8,128)S(1)} %get-tuple-element.39.diffusivity, ...), custom_call_target="tpu_custom_call" | custom-call | flops 10000000 | bytes 1753092 | tf_op jit(solution)/shard_map/stencils/pallas_call | solution.py:537
  11.1 0.0 collective-permute-done.2.corner_two
  11.1 0.3 %collective-permute-done.3.corner_one = f32[24,128]{1,0:T(8,128)S(1)} collective-permute-done((f32[24,128]{1,0:T(8,128)S(1)}, f32[24,128]{1,0:T(8,128)S(1)}, u32[]{:S(2)}, u32[]{:S(2)}) %collective-permute-start.3) | collective-permute-done | bytes 12320 | tf_op jit(solution)/shard_map/ppermute | solution.py:558
  11.4 0.8 %ends.1 = (f32[5,64,128]{2,1,0:T(8,128)}, f32[3,64,128]{2,1,0:T(8,128)}, f32[4,16,64]{2,1,0:T(8,128)}, f32[16,2048]{1,0:T(8,128)}) custom-call(f32[24,128]{1,0:T(8,128)S(1)} %collective-permute-done.2.corner_two, f32[24,128]{1,0:T(8,128)S(1)} %collective-permute-done.3.corner_one, f32[6,144,128]{2,1,0:T(8,128)S(1)} %get-tuple-element.54.state, ...), custom_call_target="tpu_custom_call" | custom-call | flops 1000000 | bytes 1286144 | tf_op jit(solution)/shard_map/ends/pallas_call | solution.py:537
  (2 shorter events, 0.0 us)
Async XLA Ops:
  2.1 3.4 %collective-permute-start.1 = (f32[152,128]{1,0:T(8,128)S(1)}, f32[152,128]{1,0:T(8,128)S(1)}, u32[]{:S(2)}, u32[]{:S(2)}) collective-permute-start(f32[152,128]{1,0:T(8,128)S(1)} %get-tuple-element.34), channel_id=1, source_target_pairs={{0,4},{1,5},{2,6},{3,7},{4,0},{5,1},{6,2},{7,3},{8,12},{9,13},{10,... | collective-permute-start | bytes 233480 | tf_op jit(solution)/shard_map/ppermute | solution.py:558
  2.8 4.7 %collective-permute-start = (f32[72,128]{1,0:T(8,128)S(1)}, f32[72,128]{1,0:T(8,128)S(1)}, u32[]{:S(2)}, u32[]{:S(2)}) collective-permute-start(f32[72,128]{1,0:T(8,128)S(1)} %get-tuple-element.33), channel_id=1, source_target_pairs={{0,1},{1,0},{2,3},{3,2},{4,8},{5,9},{6,10},{7,11},{8,4},{9,5},{10,... | collective-permute-start | bytes 110600 | tf_op jit(solution)/shard_map/ppermute | solution.py:558
  4.0 6.3 %collective-permute-start.4 = (f32[80,128]{1,0:T(8,128)S(1)}, f32[80,128]{1,0:T(8,128)S(1)}, u32[]{:S(2)}, u32[]{:S(2)}) collective-permute-start(f32[80,128]{1,0:T(8,128)S(1)} %get-tuple-element.40), channel_id=1, source_target_pairs={{0,1},{1,0},{2,3},{3,2},{4,8},{5,9},{6,10},{7,11},{8,4},{9,5},{10,... | collective-permute-start | bytes 122888 | tf_op jit(solution)/shard_map/ppermute | solution.py:558
  5.5 4.8 %collective-permute-start.5 = (f32[152,128]{1,0:T(8,128)S(1)}, f32[152,128]{1,0:T(8,128)S(1)}, u32[]{:S(2)}, u32[]{:S(2)}) collective-permute-start(f32[152,128]{1,0:T(8,128)S(1)} %get-tuple-element.42), channel_id=1, source_target_pairs={{0,4},{1,0},{2,1},{3,2},{4,5},{5,6},{6,7},{7,3},{8,12},{9,8},{10,9... | collective-permute-start | bytes 233480 | tf_op jit(solution)/shard_map/ppermute | solution.py:558
  6.8 3.5 %collective-permute-start.6 = (f32[152,128]{1,0:T(8,128)S(1)}, f32[152,128]{1,0:T(8,128)S(1)}, u32[]{:S(2)}, u32[]{:S(2)}) collective-permute-start(f32[152,128]{1,0:T(8,128)S(1)} %get-tuple-element.43), channel_id=1, source_target_pairs={{0,1},{1,2},{2,3},{3,7},{4,0},{5,4},{6,5},{7,6},{8,9},{9,10},{10,1... | collective-permute-start | bytes 233480 | tf_op jit(solution)/shard_map/ppermute | solution.py:558
  7.5 1.3 %copy-start = (s32[1,1,2048]{2,1,0:T(1,128)S(1)}, s32[1,1,2048]{2,1,0:T(1,128)}, u32[]{:S(2)}) copy-start(s32[1,1,2048]{2,1,0:T(1,128)} %cells.1) | copy-start | bytes 24580
  7.5 3.6 %collective-permute-start.2 = (f32[24,128]{1,0:T(8,128)S(1)}, f32[24,128]{1,0:T(8,128)S(1)}, u32[]{:S(2)}, u32[]{:S(2)}) collective-permute-start(f32[24,128]{1,0:T(8,128)S(1)} %get-tuple-element.35), channel_id=1, source_target_pairs={{0,4},{1,0},{2,1},{3,2},{4,5},{5,6},{6,7},{7,3},{8,12},{9,8},{10,9... | collective-permute-start | bytes 36872 | tf_op jit(solution)/shard_map/ppermute | solution.py:558
  8.8 2.5 %collective-permute-start.3 = (f32[24,128]{1,0:T(8,128)S(1)}, f32[24,128]{1,0:T(8,128)S(1)}, u32[]{:S(2)}, u32[]{:S(2)}) collective-permute-start(f32[24,128]{1,0:T(8,128)S(1)} %get-tuple-element.36), channel_id=1, source_target_pairs={{0,1},{1,2},{2,3},{3,7},{4,0},{5,4},{6,5},{7,6},{8,9},{9,10},{10,1... | collective-permute-start | bytes 36872 | tf_op jit(solution)/shard_map/ppermute | solution.py:558
